TPU v7x, 128 devices: a whole 4x4x4 slice. The times are simulated.
128 devices in a mesh: dom: 8 (over z, x_lo), shard: 16 (over x_hi, y, core).
Axes of the slice: x: 4 (x_hi: 2, x_lo: 2; x = x_hi * 2 + x_lo), y: 4, z: 4, core: 2. Of those that a mesh axis runs over, the one named last changes fastest.
Arguments:
- inputs: bfloat16 [32768, 4096], P(('dom', 'shard')), may hold values from -18 to 18
- grads_out: bfloat16 [32768, 4096], P(('dom', 'shard')), may hold values from -1 to 1
- domain_weight: bfloat16 [8, 4096, 4096], P('dom', 'shard'), may hold values from 0.099609375 to 1.8984375
- domain_ids: int32 [8], replicated, may hold values from 0 to 7, each once
- mix_weights: float32 [8], replicated, may hold values from 0.25 to 2
Outputs:
- combined: bfloat16 [4096, 4096], P('shard')
- gram: float32 [8, 8], replicated
Inputs may be any that keep to these rules, and one draw needn't show every extreme that they name: `domain_ids`: each domain id appears once.
All inputs are finite; a program needn't handle non-finite values.
Results may differ from a plain program's by a relative error of at most 0.017.
Values may be sent and summed in bfloat16 or wider, within the bound.
No kernel may reach another device: no remote copies, remote signals or barrier semaphores. Data moves between devices by JAX's collectives and lax.ppermute only.
A program may use at most 128 MiB of HBM per device.

v0:
```python
import jax
import jax.numpy as jnp
from jax import lax
from jax.sharding import PartitionSpec as P

D_IN = 4096
WIN = 4096


def partial_gram(stacked):
    flat = stacked.reshape(stacked.shape[0], -1)
    return lax.dot_general(flat, flat, (((1,), (1,)), ((), ())), preferred_element_type=jnp.float32)


def mix_rows(scale, stacked):
    return jnp.einsum("a,arc->rc", scale, stacked.astype(jnp.float32))


def per_device(inputs, grads_out, domain_weight, domain_ids, mix_weights):
    n_dom = lax.axis_size("dom")
    rows_own = domain_weight.shape[1]
    count = D_IN * WIN
    weff_grad = lax.psum_scatter(
        lax.dot_general(
            inputs, grads_out, (((0,), (0,)), ((), ())), preferred_element_type=jnp.float32
        ).astype(jnp.bfloat16),
        "shard",
        scatter_dimension=0,
        tiled=True,
    ).astype(jnp.float32)
    mine = (weff_grad * domain_weight[0].astype(jnp.float32)).astype(jnp.bfloat16)
    hi = lax.Precision.HIGHEST
    labels = jnp.arange(n_dom, dtype=jnp.int32)
    onehot = (domain_ids[:, None] == labels[None, :]).astype(jnp.float32)
    weights = jnp.dot(onehot, mix_weights, precision=hi)
    pieces = mine.reshape(n_dom, rows_own // n_dom, mine.shape[1])
    received = lax.all_to_all(pieces, "dom", split_axis=0, concat_axis=0, tiled=True)
    group_gram = lax.psum(partial_gram(received), ("dom", "shard")) / count
    diag = jnp.diagonal(group_gram)
    scale = weights / jnp.sqrt(diag + 1e-06)
    owned = mix_rows(scale, received).astype(jnp.bfloat16)
    combined = lax.all_gather(owned, "dom", axis=0, tiled=True)
    gram = jnp.dot(jnp.dot(onehot.T, group_gram, precision=hi), onehot, precision=hi)
    return (combined, gram)


def solution(mesh):
    in_specs = (
        P(("dom", "shard"), None),
        P(("dom", "shard"), None),
        P("dom", "shard", None),
        P(),
        P(),
    )
    out_specs = (P("shard", None), P())
    return jax.shard_map(
        per_device, mesh=mesh, in_specs=in_specs, out_specs=out_specs, check_vma=False
    )
```

profile of v0, /device:TPU:0, one launch (start us, length us, event | category | flops | bytes accessed | tf_op | source)
XLA Modules:
  0.0 442.5 jit_solution(16382628003142392506)
XLA Ops:
  7.2 0.0 copy-start
  7.2 0.0 reduce-scatter.2.cloned.1.call-start
  7.2 1.5 copy-done
  8.8 15.3 %convolution_convert_fusion = bf16[4096,4096]{1,0:T(8,128)(2,1)} fusion(bf16[256,4096]{1,0:T(8,128)(2,1)S(1)} %copy-done, bf16[256,4096]{1,0:T(8,128)(2,1)} %param.6), kind=kOutput, calls=%fused_computation.1 | convolution fusion | flops 8606711808 | bytes 37748736 | tf_op jit(solution)/shard_map/dot_general | solution.py:24
  24.1 0.0 reduce-scatter.2.cloned.1.call-update
  24.1 249.6 %reduce-scatter.2.cloned.1.call-done = bf16[256,4096]{1,0:T(8,128)(2,1)} async-done(((bf16[4096,4096]{1,0:T(8,128)(2,1)}), bf16[256,4096]{1,0:T(8,128)(2,1)}) %reduce-scatter.2.cloned.1.call-update) | async-done | bytes 2097168 | tf_op jit(solution)/shard_map/reduce_scatter | solution.py:23
  273.7 4.3 fusion
  278.0 5.4 %all-to-all-start = ((bf16[8,32,4096]{2,1,0:T(8,128)(2,1)}), bf16[8,32,4096]{2,1,0:T(8,128)(2,1)}, u32[]{:S(2)}, u32[]{:S(2)}) async-start(bf16[8,32,4096]{2,1,0:T(8,128)(2,1)} %bitcast.26), calls=%async_computation.1 | async-start | bytes 4194304 | tf_op jit(solution)/shard_map/all_to_all | solution.py:37
  283.4 0.0 copy-start.2
  283.4 0.0 all-gather.2.cloned.1.call-start
  283.5 23.8 %all-to-all-done = bf16[8,32,4096]{2,1,0:T(8,128)(2,1)} async-done(((bf16[8,32,4096]{2,1,0:T(8,128)(2,1)}), bf16[8,32,4096]{2,1,0:T(8,128)(2,1)}, u32[]{:S(2)}, u32[]{:S(2)}) %all-to-all-start) | async-done | bytes 2097184 | tf_op jit(solution)/shard_map/all_to_all | solution.py:37
  307.2 6.7 %fusion.5 = f32[8,8]{1,0:T(8,128)S(1)} fusion(bf16[8,32,4096]{2,1,0:T(8,128)(2,1)} %all-to-all-done), kind=kOutput, calls=%fused_computation.8 | convolution fusion | flops 16777216 | bytes 2097408 | tf_op jit(solution)/shard_map/dot_general | solution.py:12
  313.9 64.1 %psum.7 = f32[8,8]{1,0:T(8,128)S(1)} all-reduce(f32[8,8]{1,0:T(8,128)S(1)} %fusion.5), channel_id=1, replica_groups=mesh['dom'=8,'shard'=16] {'dom','shard'}, use_global_device_ids=true, to_apply=%region_1.0 | all-reduce | flops 64 | bytes 512 | tf_op jit(solution)/shard_map/psum | solution.py:38
  377.9 0.6 gather_fusion
  378.6 0.0 copy-done.1
  378.6 0.0 copy-done.2
  378.6 0.2 fusion.9
  378.8 4.1 fusion.1
  382.9 1.0 copy.19
  383.9 0.0 all-gather.2.cloned.1.call-update
  383.9 0.3 fusion.11
  384.1 0.8 fusion.10
  384.9 47.6 %all-gather.2.cloned.1.call-done = bf16[256,4096]{1,0:T(8,128)(2,1)} async-done(((bf16[32,4096]{1,0:T(8,128)(2,1)}), bf16[256,4096]{1,0:T(8,128)(2,1)}) %all-gather.2.cloned.1.call-update) | async-done | bytes 2097168 | tf_op jit(solution)/shard_map/all_gather | solution.py:42
  432.5 3.1 copy.21
  (3 shorter events, 0.0 us)
Async XLA Ops:
  7.2 1.6 copy-start
  7.2 266.5 %reduce-scatter.2.cloned.1.call-start = ((), (), s32[]{:S(2)}) async-start(), calls=%async_computation.2 | async-start | bytes 35651584 | tf_op jit(solution)/shard_map/reduce_scatter | solution.py:23
  278.0 29.2 %all-to-all-start = ((bf16[8,32,4096]{2,1,0:T(8,128)(2,1)}), bf16[8,32,4096]{2,1,0:T(8,128)(2,1)}, u32[]{:S(2)}, u32[]{:S(2)}) async-start(bf16[8,32,4096]{2,1,0:T(8,128)(2,1)} %bitcast.26), calls=%async_computation.1 | async-start | bytes 4194304 | tf_op jit(solution)/shard_map/all_to_all | solution.py:37
  283.4 95.2 %copy-start.1 = (f32[8]{0:T(128)S(1)}, f32[8]{0:T(128)}, u32[]{:S(2)}) copy-start(f32[8]{0:T(128)} %param.9) | copy-start | bytes 100
  283.4 95.2 %copy-start.2 = (s32[8]{0:T(128)S(1)}, s32[8]{0:T(128)}, u32[]{:S(2)}) copy-start(s32[8]{0:T(128)} %param.8) | copy-start | bytes 100
  283.4 149.1 %all-gather.2.cloned.1.call-start = ((), (), s32[]{:S(2)}) async-start(), calls=%async_computation.3 | async-start | bytes 2359296 | tf_op jit(solution)/shard_map/all_gather | solution.py:42
Sparse Core Ops, SparseCore 0:
  24.2 249.4 reduce-scatter.1
  384.0 48.4 all-gather.1
where the time goes:
time: 443 us; the launch traced here: 442 us
  waiting for transfers between devices  321 us (72%)
  blocking collectives  64.1 us (14%)
  matrix products  27.3 us (6%)
  between operations  14.1 us (3%)
  local copies, waits for them, and re-layouts  6.31 us (1%)
  starting transfers between devices  5.46 us (1%)
    reduce_scatter x1, waiting for transfers between devices, per_device(): lax.psum_scatter(lax.dot_general(inputs, grads_out, (((0,), (0,)), ((), (...  250 us
    psum x1, blocking collectives, per_device(): group_gram = lax.psum(partial_gram(received), ('dom', 'shard')) / count  64.1 us
    all_gather x1, waiting for transfers between devices, per_device(): combined = lax.all_gather(owned, 'dom', axis=0, tiled=True)  47.6 us
    all_to_all x1, waiting for transfers between devices, per_device(): lax.all_to_all(pieces, 'dom', split_axis=0, concat_axis=0, tiled=True)  23.8 us
    dot_general x1, matrix products, per_device(): lax.dot_general(inputs, grads_out, (((0,), (0,)), ((), ())), preferred_el...  15.3 us
  transfers between devices with their start and end apart: 3, of which 3 were waited for; matrix products, arithmetic and copies ran while one was open for 0% of the time, Pallas kernels for 0%

commit v1 on v0

v1 whole, which is shorter than its diff:
```python
import functools

import jax
import jax.numpy as jnp
from jax import lax
from jax.experimental import pallas as pl
from jax.experimental.pallas import tpu as pltpu
from jax.sharding import PartitionSpec as P

D_IN = 4096
WIN = 4096
AXES = ("dom", "shard")
EARLY = 1024
PIECES = ((1024,), (1024,), (512, 512))
HALF = 128
ORDER = ((0, 0), (0, 1), (1, 0), (3, 1), (2, 0), (1, 1), (2, 1), (3, 0))
PEERS = ((False, False), (False, True), (True, False), (True, True))
F32 = jnp.float32
BF16 = jnp.bfloat16


def device_index(x, y, z, core):
    return (z * 2 + x % 2) * 16 + (x // 2) * 8 + y * 2 + core


def shift(value, dx=0, dy=0, dz=0, pair=0, core=0):
    moves = [
        (
            device_index(x, y, z, c),
            device_index(((x ^ pair) + dx) % 4, (y + dy) % 4, (z + dz) % 4, c ^ core),
        )
        for x in range(4)
        for y in range(4)
        for z in range(4)
        for c in range(2)
    ]
    return lax.ppermute(value, AXES, moves)


def turn_kernel(at_ref, source, *outs):
    x_hi, y, core = at_ref[0], at_ref[1], at_ref[2]
    for out, (flip_x, flip_core) in zip(outs, PEERS):
        a = 1 - x_hi if flip_x else x_hi
        c = 1 - core if flip_core else core
        for i, (step, half) in enumerate(ORDER):
            block = ((a * 4 + lax.rem(y + step, 4)) * 2 + c) * 2 + half
            columns = pl.ds(pl.multiple_of(block * HALF, HALF), HALF)
            out[pl.ds(i * HALF, HALF), :] = source[:, columns].T


def turned_columns(inputs, at):
    rows = inputs.shape[0]
    return pl.pallas_call(
        turn_kernel,
        in_specs=[
            pl.BlockSpec(memory_space=pltpu.SMEM),
            pl.BlockSpec(memory_space=pltpu.VMEM),
        ],
        out_specs=[pl.BlockSpec(memory_space=pltpu.VMEM)] * 4,
        out_shape=[jax.ShapeDtypeStruct((8 * HALF, rows), BF16)] * 4,
        compiler_params=pltpu.CompilerParams(vmem_limit_bytes=16 * 1024 * 1024),
        cost_estimate=pl.CostEstimate(
            flops=0, bytes_accessed=4 * inputs.size, transcendentals=0
        ),
    )(at, inputs)


def matmul_kernel(sets, terms, *refs):
    lefts, rights, outs = refs[: sets * terms], refs[sets * terms : -4], refs[-4:]
    rows = outs[0].shape[1]
    for r in range(sets):
        for i, out in enumerate(outs):
            total = None
            for left, right in zip(lefts[r * terms : (r + 1) * terms], rights):
                term = jnp.dot(left[pl.ds(i * rows, rows), :], right[...], preferred_element_type=F32)
                total = term if total is None else total + term
            out[r] = total.astype(BF16)


def block_products(sets, rights, offsets, width):
    rows, depth = sets[0][0].shape
    terms = len(rights)
    tile = 512
    part = rows // 4

    def columns(offset):
        return pl.BlockSpec((depth, tile), lambda i: (0, i + offset // tile))

    n = len(sets)
    return pl.pallas_call(
        functools.partial(matmul_kernel, n, terms),
        grid=(width // tile,),
        in_specs=[pl.BlockSpec((rows, depth), lambda i: (0, 0))] * (n * terms)
        + [columns(offset) for offset in offsets],
        out_specs=[pl.BlockSpec((n, part, tile), lambda i: (0, 0, i))] * 4,
        out_shape=[jax.ShapeDtypeStruct((n, part, width), BF16)] * 4,
        compiler_params=pltpu.CompilerParams(vmem_limit_bytes=32 * 1024 * 1024),
        cost_estimate=pl.CostEstimate(
            flops=2 * n * rows * depth * terms * width,
            bytes_accessed=2 * (n * terms * rows * depth + terms * depth * width + n * rows * width),
            transcendentals=0,
        ),
    )(*sum(sets, []), *rights)


def after(values, *done):
    out = lax.optimization_barrier((tuple(values), done))
    return out[0]


def add(a, b):
    return (a.astype(F32) + b.astype(F32)).astype(BF16)


def per_device(inputs, grads_out, domain_weight, domain_ids, mix_weights):
    dom = lax.axis_index("dom")
    shard = lax.axis_index("shard")
    z, x_lo = dom // 2, dom % 2
    x_hi, y, core = shard // 8, (shard // 2) % 4, shard % 2
    count = D_IN * WIN
    hi = lax.Precision.HIGHEST
    weight = domain_weight[0]

    widths = [sum(piece) for piece in PIECES]
    edges = [EARLY + sum(widths[:p]) for p in range(len(widths) + 1)]
    own_left, core_left, x_left, both_left = turned_columns(inputs, jnp.stack([x_hi, y, core]))
    grads_core = shift(grads_out, core=1)
    lefts = [own_left, shift(core_left, core=1), shift(x_left, dx=2), shift(both_left, dx=2, core=1)]
    other_rows = [x_left, shift(both_left, core=1)]
    in_flight = [lefts[2], lefts[3]]
    across = []
    for lo, up in zip(edges, edges[1:]):
        (piece,) = after([lax.slice_in_dim(grads_out, lo, up, axis=1)], in_flight[-2])
        across.append(shift(piece, dx=2))
        in_flight.append(across[-1])
    swapped = [shift(a, core=1) for a in across]

    def reduce_first(products):
        own, keep, up, down = products
        return own, keep, shift(up, dy=1), shift(down, dy=-1)

    def reduce_second(first):
        own, keep, from_back, from_next = first
        sums = add(keep[:, :HALF], from_back[:, :HALF]), add(keep[:, HALF:], from_next[:, :HALF])
        return sums, (
            own, from_back[:, HALF:], from_next[:, HALF:], shift(sums[0], dy=1), shift(sums[1], dy=-1),
        )

    def reduce_last(second, *done):
        own, back_own, next_own, back2, next2 = after(second, *done)
        top = own[:, :HALF].astype(F32) + back2.astype(F32) + next_own.astype(F32)
        bottom = own[:, HALF:].astype(F32) + back_own.astype(F32) + next2.astype(F32)
        return jnp.concatenate([top, bottom], axis=1)

    def centered(weff_grad, start):
        block = weight[:, start : start + weff_grad.shape[1]].astype(F32)
        return (weff_grad * block).astype(BF16)

    def spread_x(*centers):
        pairs = jnp.concatenate(centers, axis=1).reshape(4, 2, 32, -1)
        kept = lax.dynamic_index_in_dim(pairs, x_lo, 1, keepdims=False)
        return kept, shift(lax.dynamic_index_in_dim(pairs, 1 - x_lo, 1, keepdims=False), pair=1)

    def spread_z(kept, passed):
        both = jnp.stack([kept, passed])
        parts = [lax.dynamic_index_in_dim(both, (z + n) % 4, 1, keepdims=False) for n in range(4)]
        return jnp.concatenate([parts[0]] + [shift(parts[n], dz=n) for n in (1, 2, 3)])

    def products(p, inner, width, *done):
        rights = after([across[p], swapped[p]], *done)
        start = edges[p] + inner
        return block_products([lefts], [grads_out, grads_core, *rights], [start, start, inner, inner], width)

    early = reduce_first(
        block_products([lefts[:2], other_rows], [grads_out, grads_core], [0, 0], EARLY)
    )
    early_sums, early = reduce_second(early)

    out1 = products(0, 0, 1024, *early_sums)
    first1 = reduce_first(out1)
    early = reduce_last(early, out1[2])
    early_other = shift(early[1].astype(BF16), dx=2)
    sums1, second1 = reduce_second(first1)

    out2 = products(1, 0, 1024, *sums1)
    first2 = reduce_first(out2)
    center1 = centered(reduce_last(second1, out2[2])[0], edges[0])
    center0 = centered(early[0] + early_other.astype(F32), 0)
    half_a = spread_x(center0, center1)
    sums2, second2 = reduce_second(first2)

    out3 = products(2, 0, 512, *sums2, center0, center1)
    first3 = reduce_first(out3)
    slots_a = spread_z(*after(half_a, out3[2]))
    sums3, second3 = reduce_second(first3)

    out4 = products(2, 512, 512, *sums3)
    first4 = reduce_first(out4)
    center2 = centered(reduce_last(second2, out4[2])[0], edges[1])
    sums4, second4 = reduce_second(first4)
    center3 = centered(reduce_last(second3, *sums4)[0], edges[2])
    slots_b = spread_z(*spread_x(center2, center3))
    center4 = centered(reduce_last(second4)[0], edges[2] + 512)
    slots_c = lax.all_to_all(center4.reshape(8, 32, -1), "dom", 0, 0, tiled=True)

    labels = jnp.arange(8, dtype=jnp.int32)
    group_of = ((z - labels // 2) % 4) * 2 + (x_lo ^ (labels % 2))
    place = (group_of[:, None] == labels[None, :]).astype(F32)
    onehot = (domain_ids[:, None] == labels[None, :]).astype(F32)
    weights = jnp.dot(onehot, mix_weights, precision=hi)

    def partial_gram(slots):
        flat = slots.reshape(8, -1)
        return lax.dot_general(flat, flat, (((1,), (1,)), ((), ())), preferred_element_type=F32)

    placed = partial_gram(slots_a) + partial_gram(slots_b)
    placed = jnp.sum(
        place[:, :, None, None] * place[None, None] * placed[:, None, :, None], axis=(0, 2)
    )
    local = placed + partial_gram(slots_c)
    sent = jnp.broadcast_to(jnp.pad(local, ((0, 0), (0, 120)))[None], (128, 8, 128))
    parts = lax.all_to_all(sent, AXES, 0, 0, tiled=True)
    group_gram = jnp.sum(parts, axis=0)[:, :8] / count
    scale = weights / jnp.sqrt(jnp.diagonal(group_gram) + 1e-06)
    slot_scale = jnp.dot(place, scale, precision=hi)

    def mixed(factors, slots):
        return jnp.sum(factors[:, None, None] * slots.astype(F32), axis=0).astype(BF16)

    owned = jnp.concatenate(
        [mixed(slot_scale, slots_a), mixed(slot_scale, slots_b), mixed(scale, slots_c)], axis=1
    )
    combined = lax.all_to_all(jnp.broadcast_to(owned[None], (8, *owned.shape)), "dom", 0, 0, tiled=True)
    gram = jnp.dot(jnp.dot(onehot.T, group_gram, precision=hi), onehot, precision=hi)
    return (combined.reshape(-1, WIN), gram)


def solution(mesh):
    in_specs = (
        P(AXES, None),
        P(AXES, None),
        P("dom", "shard", None),
        P(),
        P(),
    )
    out_specs = (P("shard", None), P())
    return jax.shard_map(
        per_device, mesh=mesh, in_specs=in_specs, out_specs=out_specs, check_vma=False
    )
```

time: 443 us -> 240 us (0.54)
  waiting for transfers between devices: 321 us -> 109 us
  starting transfers between devices: 5.46 us -> 81.9 us
  blocking collectives: 64.1 us -> 0 us
  matrix products: 27.3 us -> 3.94 us
  Pallas kernels: 0 us -> 17.8 us
  between operations: 14.1 us -> 1.26 us
  other arithmetic: 4.34 us -> 12.3 us
  local copies, waits for them, and re-layouts: 6.31 us -> 13 us
    reduce_scatter x1 -> x0, waiting for transfers between devices: 250 us -> none  [per_device(): lax.psum_scatter(lax.dot_general(inputs, grads_out, (((0,), (0,)), ((), (...]
    ppermute x0 -> x40, waiting for transfers between devices: none -> 67.8 us  [shift(): return lax.ppermute(value, AXES, moves)]
    psum x1 -> x0, blocking collectives: 64.1 us -> none  [per_device(): group_gram = lax.psum(partial_gram(received), ('dom', 'shard')) / count]
    ppermute x0 -> x40, starting transfers between devices: none -> 63.3 us  [shift(): return lax.ppermute(value, AXES, moves)]
    all_gather x1 -> x0, waiting for transfers between devices: 47.6 us -> none  [per_device(): combined = lax.all_gather(owned, 'dom', axis=0, tiled=True)]
    dot_general x2 -> x1, matrix products: 19.4 us -> 0.19 us  [per_device(): slot_scale = jnp.dot(place, scale, precision=hi)]
    pallas_call x0 -> x6, Pallas kernels: none -> 17.8 us  [the longest x5 16.7 us: block_products(): pl.pallas_call(functools.partial(matmul_kernel, n, terms), grid=(width //...]
    all_to_all x1 -> x3, waiting for transfers between devices: 23.8 us -> 41 us  [the longest x1 26.5 us: per_device(): lax.all_to_all(jnp.broadcast_to(owned[None], (8, *owned.shape)), 'dom', 0...]
  transfers between devices with their start and end apart: 3 -> 43, of which waited for: 3 -> 17; matrix products, arithmetic and copies ran while one was open for 0% -> 7% of each run, Pallas kernels for 0% -> 7%
where the time goes in v1:
time: 240 us; the launch traced here: 239 us
  waiting for transfers between devices  109 us (45%)
  starting transfers between devices  81.9 us (34%)
  Pallas kernels  17.8 us (7%)
  local copies, waits for them, and re-layouts  13 us (5%)
  other arithmetic  12.3 us (5%)
  matrix products  3.94 us (2%)
    ppermute x40, waiting for transfers between devices, shift(): return lax.ppermute(value, AXES, moves)  67.8 us
    ppermute x40, starting transfers between devices, shift(): return lax.ppermute(value, AXES, moves)  63.3 us
    all_to_all x1, waiting for transfers between devices, per_device(): lax.all_to_all(jnp.broadcast_to(owned[None], (8, *owned.shape)), 'dom', 0...  26.5 us
    pallas_call x5, Pallas kernels, block_products(): pl.pallas_call(functools.partial(matmul_kernel, n, terms), grid=(width //...  16.7 us
    all_to_all x1, waiting for transfers between devices, per_device(): parts = lax.all_to_all(sent, AXES, 0, 0, tiled=True)  13.1 us
    all_to_all x1, starting transfers between devices, per_device(): parts = lax.all_to_all(sent, AXES, 0, 0, tiled=True)  10.2 us
  transfers between devices with their start and end apart: 43, of which 17 were waited for; matrix products, arithmetic and copies ran while one was open for 7% of the time, Pallas kernels for 7%

profile of v1, /device:TPU:0, one launch (start us, length us, event | category | flops | bytes accessed | tf_op | source)
XLA Modules:
  0.0 239.0 jit_solution(5909651056092334597)
XLA Ops:
  7.5 3.8 %shard_map.69 = (bf16[2,256,1024]{2,1,0:T(8,128)(2,1)S(1)}, bf16[2,256,1024]{2,1,0:T(8,128)(2,1)S(1)}, bf16[2,256,1024]{2,1,0:T(8,128)(2,1)S(1)}, bf16[2,256,1024]{2,1,0:T(8,128)(2,1)S(1)}) custom-call(bf16[1024,256]{1,0:T(8,128)(2,1)S(1)} %get-tuple-element.64.refs_0_, bf16[1024,256]{1,0:T(8,128)(2,1)S(1)} %collective-permute-done.refs_1_, ...), custom_call_target="tpu_custom_call" | custom-call | flops 2147483648 | bytes 7340032 | tf_op jit(solution)/shard_map/pallas_call | solution.py:90
  14.8 5.2 %collective-permute-done.7.refs_2_ = bf16[1024,256]{1,0:T(8,128)(2,1)S(1)} collective-permute-done((bf16[1024,256]{1,0:T(8,128)(2,1)S(1)}, bf16[1024,256]{1,0:T(8,128)(2,1)S(1)}, u32[]{:S(2)}, u32[]{:S(2)}) %collective-permute-start.7) | collective-permute-done | bytes 524320 | tf_op jit(solution)/shard_map/ppermute | solution.py:37
  23.1 13.2 %collective-permute-done.9.refs_6_ = bf16[256,1024]{1,0:T(8,128)(2,1)S(1)} collective-permute-done((bf16[256,1024]{1,0:T(8,128)(2,1)S(1)}, bf16[256,1024]{1,0:T(8,128)(2,1)S(1)}, u32[]{:S(2)}, u32[]{:S(2)}) %collective-permute-start.9) | collective-permute-done | bytes 524320 | tf_op jit(solution)/shard_map/ppermute | solution.py:37
  36.4 8.9 %collective-permute-done.8.refs_3_ = bf16[1024,256]{1,0:T(8,128)(2,1)S(1)} collective-permute-done((bf16[1024,256]{1,0:T(8,128)(2,1)S(1)}, bf16[1024,256]{1,0:T(8,128)(2,1)S(1)}, u32[]{:S(2)}, u32[]{:S(2)}) %collective-permute-start.8) | collective-permute-done | bytes 524320 | tf_op jit(solution)/shard_map/ppermute | solution.py:37
  53.7 4.4 %shard_map.70 = (bf16[1,256,1024]{2,1,0:T(8,128)(2,1)S(1)}, bf16[1,256,1024]{2,1,0:T(8,128)(2,1)S(1)}, bf16[1,256,1024]{2,1,0:T(8,128)(2,1)}, bf16[1,256,1024]{2,1,0:T(8,128)(2,1)}) custom-call(bf16[1024,256]{1,0:T(8,128)(2,1)S(1)} %get-tuple-element.64.refs_0_, bf16[1024,256]{1,0:T(8,128)(2,1)S(1)} %collective-permute-done.refs_1_, ...), custom_call_target="tpu_custom_call" | custom-call | flops 2147483648 | bytes 6291456 | tf_op jit(solution)/shard_map/pallas_call | solution.py:90
  64.6 8.0 %collective-permute-done.19.refs_6_ = bf16[256,1024]{1,0:T(8,128)(2,1)} collective-permute-done((bf16[256,1024]{1,0:T(8,128)(2,1)S(1)}, bf16[256,1024]{1,0:T(8,128)(2,1)}, u32[]{:S(2)}, u32[]{:S(2)}) %collective-permute-start.19) | collective-permute-done | bytes 524320 | tf_op jit(solution)/shard_map/ppermute | solution.py:37
  73.2 4.1 %collective-permute-done.12 = bf16[1,256,1024]{2,1,0:T(8,128)(2,1)} collective-permute-done((bf16[1,256,1024]{2,1,0:T(8,128)(2,1)}, bf16[1,256,1024]{2,1,0:T(8,128)(2,1)}, u32[]{:S(2)}, u32[]{:S(2)}) %collective-permute-start.12) | collective-permute-done | bytes 524320 | tf_op jit(solution)/shard_map/ppermute | solution.py:37
  81.9 3.8 %shard_map.71 = (bf16[1,256,1024]{2,1,0:T(8,128)(2,1)S(1)}, bf16[1,256,1024]{2,1,0:T(8,128)(2,1)S(1)}, bf16[1,256,1024]{2,1,0:T(8,128)(2,1)S(1)}, bf16[1,256,1024]{2,1,0:T(8,128)(2,1)S(1)}) custom-call(bf16[1024,256]{1,0:T(8,128)(2,1)S(1)} %get-tuple-element.64.refs_0_, bf16[1024,256]{1,0:T(8,128)(2,1)S(1)} %collective-permute-done.refs_1_, ...), custom_call_target="tpu_custom_call" | custom-call | flops 2147483648 | bytes 6291456 | tf_op jit(solution)/shard_map/pallas_call | solution.py:90
  93.0 3.3 %collective-permute-start.11 = (bf16[256,1024]{1,0:T(8,128)(2,1)S(1)}, bf16[256,1024]{1,0:T(8,128)(2,1)S(1)}, u32[]{:S(2)}, u32[]{:S(2)}) collective-permute-start(bf16[256,1024]{1,0:T(8,128)(2,1)S(1)} %fusion.13), channel_id=1, source_target_pairs={{0,8},{1,9},{32,40},{33,41},{64,72},{65,73},{96,104},{97,105},{2,1... | collective-permute-start | bytes 1572872 | tf_op jit(solution)/shard_map/ppermute | solution.py:37
  96.5 3.2 %collective-permute-done.21 = bf16[1,256,1024]{2,1,0:T(8,128)(2,1)S(1)} collective-permute-done((bf16[1,256,1024]{2,1,0:T(8,128)(2,1)S(1)}, bf16[1,256,1024]{2,1,0:T(8,128)(2,1)S(1)}, u32[]{:S(2)}, u32[]{:S(2)}) %collective-permute-start.21) | collective-permute-done | bytes 524320 | tf_op jit(solution)/shard_map/ppermute | solution.py:37
  100.0 7.2 %collective-permute-done.11 = bf16[256,1024]{1,0:T(8,128)(2,1)S(1)} collective-permute-done((bf16[256,1024]{1,0:T(8,128)(2,1)S(1)}, bf16[256,1024]{1,0:T(8,128)(2,1)S(1)}, u32[]{:S(2)}, u32[]{:S(2)}) %collective-permute-start.11) | collective-permute-done | bytes 524320 | tf_op jit(solution)/shard_map/ppermute | solution.py:37
  110.0 3.2 %collective-permute-start.29 = (bf16[1,256,512]{2,1,0:T(8,128)(2,1)S(1)}, bf16[1,256,512]{2,1,0:T(8,128)(2,1)S(1)}, u32[]{:S(2)}, u32[]{:S(2)}) collective-permute-start(bf16[1,256,512]{2,1,0:T(8,128)(2,1)S(1)} %get-tuple-element.103), channel_id=1, source_target_pairs={{0,6},{1,7},{32,38},{33,39},{64,70},{65,71},{96,102},{97,103},{2,0... | collective-permute-start | bytes 786440 | tf_op jit(solution)/shard_map/ppermute | solution.py:37
  113.4 3.2 %collective-permute-start.27 = (bf16[1,128,1024]{2,1,0:T(8,128)(2,1)S(1)}, bf16[1,128,1024]{2,1,0:T(8,128)(2,1)S(1)}, u32[]{:S(2)}, u32[]{:S(2)}) collective-permute-start(bf16[1,128,1024]{2,1,0:T(8,128)(2,1)S(1)} %get-tuple-element.153), channel_id=1, source_target_pairs={{0,6},{1,7},{32,38},{33,39},{64,70},{65,71},{96,102},{97,103},{2,0... | collective-permute-start | bytes 786440 | tf_op jit(solution)/shard_map/ppermute | solution.py:37
  120.1 3.2 %collective-permute-start.31 = (bf16[1,128,512]{2,1,0:T(8,128)(2,1)S(1)}, bf16[1,128,512]{2,1,0:T(8,128)(2,1)S(1)}, u32[]{:S(2)}, u32[]{:S(2)}) collective-permute-start(bf16[1,128,512]{2,1,0:T(8,128)(2,1)S(1)} %get-tuple-element.163), channel_id=1, source_target_pairs={{0,6},{1,7},{32,38},{33,39},{64,70},{65,71},{96,102},{97,103},{2,0... | collective-permute-start | bytes 393224 | tf_op jit(solution)/shard_map/ppermute | solution.py:37
  125.7 3.2 %collective-permute-start.33 = (bf16[1,256,512]{2,1,0:T(8,128)(2,1)S(1)}, bf16[1,256,512]{2,1,0:T(8,128)(2,1)S(1)}, u32[]{:S(2)}, u32[]{:S(2)}) collective-permute-start(bf16[1,256,512]{2,1,0:T(8,128)(2,1)S(1)} %get-tuple-element.114), channel_id=1, source_target_pairs={{0,6},{1,7},{32,38},{33,39},{64,70},{65,71},{96,102},{97,103},{2,0... | collective-permute-start | bytes 786440 | tf_op jit(solution)/shard_map/ppermute | solution.py:37
  129.2 4.3 %collective-permute-done.32 = bf16[1,256,512]{2,1,0:T(8,128)(2,1)S(1)} collective-permute-done((bf16[1,256,512]{2,1,0:T(8,128)(2,1)S(1)}, bf16[1,256,512]{2,1,0:T(8,128)(2,1)S(1)}, u32[]{:S(2)}, u32[]{:S(2)}) %collective-permute-start.32) | collective-permute-done | bytes 262176 | tf_op jit(solution)/shard_map/ppermute | solution.py:37
  133.7 3.5 %collective-permute-start.39 = (bf16[1,128,512]{2,1,0:T(8,128)(2,1)S(1)}, bf16[1,128,512]{2,1,0:T(8,128)(2,1)S(1)}, u32[]{:S(2)}, u32[]{:S(2)}) collective-permute-start(bf16[1,128,512]{2,1,0:T(8,128)(2,1)S(1)} %get-tuple-element.161), channel_id=1, source_target_pairs={{0,6},{1,7},{32,38},{33,39},{64,70},{65,71},{96,102},{97,103},{2,0... | collective-permute-start | bytes 393224 | tf_op jit(solution)/shard_map/ppermute | solution.py:37
  141.3 3.2 %collective-permute-start.34 = (bf16[4,32,1536]{2,1,0:T(8,128)(2,1)S(1)}, bf16[4,32,1536]{2,1,0:T(8,128)(2,1)S(1)}, u32[]{:S(2)}, u32[]{:S(2)}) collective-permute-start(bf16[4,32,1536]{2,1,0:T(8,128)(2,1)S(1)} %get-tuple-element.147), channel_id=1, source_target_pairs={{0,16},{1,17},{32,48},{33,49},{64,80},{65,81},{96,112},{97,113},{2... | collective-permute-start | bytes 1179656 | tf_op jit(solution)/shard_map/ppermute | solution.py:37
  144.5 5.7 %collective-permute-done.34 = bf16[4,32,1536]{2,1,0:T(8,128)(2,1)S(1)} collective-permute-done((bf16[4,32,1536]{2,1,0:T(8,128)(2,1)S(1)}, bf16[4,32,1536]{2,1,0:T(8,128)(2,1)S(1)}, u32[]{:S(2)}, u32[]{:S(2)}) %collective-permute-start.34) | collective-permute-done | bytes 393248 | tf_op jit(solution)/shard_map/ppermute | solution.py:37
  164.2 4.7 %all-to-all-start = ((bf16[8,32,512]{2,1,0:T(8,128)(2,1)}), bf16[8,32,512]{2,1,0:T(8,128)(2,1)S(1)}, u32[]{:S(2)}, u32[]{:S(2)}) async-start(bf16[8,32,512]{2,1,0:T(8,128)(2,1)} %bitcast.31), calls=%async_computation | async-start | bytes 524288 | tf_op jit(solution)/shard_map/all_to_all | solution.py:204
  177.3 10.2 %all-to-all-start.1 = ((f32[128,8,128]{2,1,0:T(8,128)}), f32[128,8,128]{2,1,0:T(8,128)S(1)}, u32[]{:S(2)}, u32[]{:S(2)}) async-start(f32[128,8,128]{2,1,0:T(8,128)} %broadcast_in_dim.6), calls=%async_computation.1 | async-start | bytes 1048576 | tf_op jit(solution)/shard_map/all_to_all | solution.py:222
  187.6 13.1 %all-to-all-done.1 = f32[128,8,128]{2,1,0:T(8,128)S(1)} async-done(((f32[128,8,128]{2,1,0:T(8,128)}), f32[128,8,128]{2,1,0:T(8,128)S(1)}, u32[]{:S(2)}, u32[]{:S(2)}) %all-to-all-start.1) | async-done | bytes 524320 | tf_op jit(solution)/shard_map/all_to_all | solution.py:222
  206.6 3.6 %all-to-all-start.2 = ((bf16[8,32,4096]{2,1,0:T(8,128)(2,1)}), bf16[8,32,4096]{2,1,0:T(8,128)(2,1)S(1)}, u32[]{:S(2)}, u32[]{:S(2)}) async-start(bf16[8,32,4096]{2,1,0:T(8,128)(2,1)} %broadcast_in_dim.7), calls=%async_computation.2 | async-start | bytes 4194304 | tf_op jit(solution)/shard_map/all_to_all | solution.py:233
  211.2 26.5 %all-to-all-done.2 = bf16[8,32,4096]{2,1,0:T(8,128)(2,1)S(1)} async-done(((bf16[8,32,4096]{2,1,0:T(8,128)(2,1)}), bf16[8,32,4096]{2,1,0:T(8,128)(2,1)S(1)}, u32[]{:S(2)}, u32[]{:S(2)}) %all-to-all-start.2) | async-done | bytes 2097184 | tf_op jit(solution)/shard_map/all_to_all | solution.py:233
  (179 shorter events, 84.8 us)
Async XLA Ops:
  4.3 15.7 %collective-permute-start.7 = (bf16[1024,256]{1,0:T(8,128)(2,1)S(1)}, bf16[1024,256]{1,0:T(8,128)(2,1)S(1)}, u32[]{:S(2)}, u32[]{:S(2)}) collective-permute-start(bf16[1024,256]{1,0:T(8,128)(2,1)S(1)} %get-tuple-element.66.refs_2_), channel_id=1, source_target_pairs={{0,8},{1,9},{32,40},{33,41},{64,72},{65,73},{96,104},{97,105},{2,1... | collective-permute-start | bytes 1572872 | tf_op jit(solution)/shard_map/ppermute | solution.py:37
  11.3 37.5 %collective-permute-start.3 = (bf16[2,256,1024]{2,1,0:T(8,128)(2,1)S(1)}, bf16[2,256,1024]{2,1,0:T(8,128)(2,1)S(1)}, u32[]{:S(2)}, u32[]{:S(2)}) collective-permute-start(bf16[2,256,1024]{2,1,0:T(8,128)(2,1)S(1)} %get-tuple-element.69), channel_id=1, source_target_pairs={{0,2},{1,3},{32,34},{33,35},{64,66},{65,67},{96,98},{97,99},{2,4},... | collective-permute-start | bytes 3145736 | tf_op jit(solution)/shard_map/ppermute | solution.py:37
  12.9 35.8 %collective-permute-start.4 = (bf16[2,256,1024]{2,1,0:T(8,128)(2,1)S(1)}, bf16[2,256,1024]{2,1,0:T(8,128)(2,1)S(1)}, u32[]{:S(2)}, u32[]{:S(2)}) collective-permute-start(bf16[2,256,1024]{2,1,0:T(8,128)(2,1)S(1)} %get-tuple-element.70), channel_id=1, source_target_pairs={{0,6},{1,7},{32,38},{33,39},{64,70},{65,71},{96,102},{97,103},{2,0... | collective-permute-start | bytes 3145736 | tf_op jit(solution)/shard_map/ppermute | solution.py:37
  20.0 16.4 %collective-permute-start.9 = (bf16[256,1024]{1,0:T(8,128)(2,1)S(1)}, bf16[256,1024]{1,0:T(8,128)(2,1)S(1)}, u32[]{:S(2)}, u32[]{:S(2)}) collective-permute-start(bf16[256,1024]{1,0:T(8,128)(2,1)S(1)} %get-tuple-element.72), channel_id=1, source_target_pairs={{0,8},{1,9},{32,40},{33,41},{64,72},{65,73},{96,104},{97,105},{2,1... | collective-permute-start | bytes 1572872 | tf_op jit(solution)/shard_map/ppermute | solution.py:37
  23.1 22.1 %collective-permute-start.8 = (bf16[1024,256]{1,0:T(8,128)(2,1)S(1)}, bf16[1024,256]{1,0:T(8,128)(2,1)S(1)}, u32[]{:S(2)}, u32[]{:S(2)}) collective-permute-start(bf16[1024,256]{1,0:T(8,128)(2,1)S(1)} %get-tuple-element.67), channel_id=1, source_target_pairs={{0,9},{1,8},{32,41},{33,40},{64,73},{65,72},{96,105},{97,104},{2,1... | collective-permute-start | bytes 1572872 | tf_op jit(solution)/shard_map/ppermute | solution.py:37
  36.4 17.3 %collective-permute-start.10 = (bf16[256,1024]{1,0:T(8,128)(2,1)S(1)}, bf16[256,1024]{1,0:T(8,128)(2,1)S(1)}, u32[]{:S(2)}, u32[]{:S(2)}) collective-permute-start(bf16[256,1024]{1,0:T(8,128)(2,1)S(1)} %collective-permute-done.9.refs_6_), channel_id=1, source_target_pairs={{0,1},{1,0},{32,33},{33,32},{64,65},{65,64},{96,97},{97,96},{2,3},... | collective-permute-start | bytes 1572872 | tf_op jit(solution)/shard_map/ppermute | solution.py:37
  45.2 16.4 %collective-permute-start.16 = (bf16[256,1024]{1,0:T(8,128)(2,1)S(1)}, bf16[256,1024]{1,0:T(8,128)(2,1)}, u32[]{:S(2)}, u32[]{:S(2)}) collective-permute-start(bf16[256,1024]{1,0:T(8,128)(2,1)S(1)} %get-tuple-element.84), channel_id=1, source_target_pairs={{0,8},{1,9},{32,40},{33,41},{64,72},{65,73},{96,104},{97,105},{2,1... | collective-permute-start | bytes 1572872 | tf_op jit(solution)/shard_map/ppermute | solution.py:37
  47.7 24.9 %collective-permute-start.19 = (bf16[256,1024]{1,0:T(8,128)(2,1)S(1)}, bf16[256,1024]{1,0:T(8,128)(2,1)}, u32[]{:S(2)}, u32[]{:S(2)}) collective-permute-start(bf16[256,1024]{1,0:T(8,128)(2,1)S(1)} %get-tuple-element.93), channel_id=1, source_target_pairs={{0,8},{1,9},{32,40},{33,41},{64,72},{65,73},{96,104},{97,105},{2,1... | collective-permute-start | bytes 1572872 | tf_op jit(solution)/shard_map/ppermute | solution.py:37
  50.4 22.2 %collective-permute-start.5 = (bf16[2,128,1024]{2,1,0:T(8,128)(2,1)}, bf16[2,128,1024]{2,1,0:T(8,128)(2,1)}, u32[]{:S(2)}, u32[]{:S(2)}) collective-permute-start(bf16[2,128,1024]{2,1,0:T(8,128)(2,1)} %get-tuple-element.142), channel_id=1, source_target_pairs={{0,2},{1,3},{32,34},{33,35},{64,66},{65,67},{96,98},{97,99},{2,4},... | collective-permute-start | bytes 1572872 | tf_op jit(solution)/shard_map/ppermute | solution.py:37
  52.0 21.2 %collective-permute-start.6 = (bf16[2,128,1024]{2,1,0:T(8,128)(2,1)}, bf16[2,128,1024]{2,1,0:T(8,128)(2,1)}, u32[]{:S(2)}, u32[]{:S(2)}) collective-permute-start(bf16[2,128,1024]{2,1,0:T(8,128)(2,1)} %get-tuple-element.141), channel_id=1, source_target_pairs={{0,6},{1,7},{32,38},{33,39},{64,70},{65,71},{96,102},{97,103},{2,0... | collective-permute-start | bytes 1572872 | tf_op jit(solution)/shard_map/ppermute | solution.py:37
  59.7 17.6 %collective-permute-start.12 = (bf16[1,256,1024]{2,1,0:T(8,128)(2,1)}, bf16[1,256,1024]{2,1,0:T(8,128)(2,1)}, u32[]{:S(2)}, u32[]{:S(2)}) collective-permute-start(bf16[1,256,1024]{2,1,0:T(8,128)(2,1)} %get-tuple-element.75), channel_id=1, source_target_pairs={{0,2},{1,3},{32,34},{33,35},{64,66},{65,67},{96,98},{97,99},{2,4},... | collective-permute-start | bytes 1572872 | tf_op jit(solution)/shard_map/ppermute | solution.py:37
  61.6 15.7 %collective-permute-start.13 = (bf16[1,256,1024]{2,1,0:T(8,128)(2,1)}, bf16[1,256,1024]{2,1,0:T(8,128)(2,1)}, u32[]{:S(2)}, u32[]{:S(2)}) collective-permute-start(bf16[1,256,1024]{2,1,0:T(8,128)(2,1)} %get-tuple-element.82), channel_id=1, source_target_pairs={{0,6},{1,7},{32,38},{33,39},{64,70},{65,71},{96,102},{97,103},{2,0... | collective-permute-start | bytes 1572872 | tf_op jit(solution)/shard_map/ppermute | solution.py:37
  72.6 35.0 %collective-permute-start.20 = (bf16[256,1024]{1,0:T(8,128)(2,1)}, bf16[256,1024]{1,0:T(8,128)(2,1)S(1)}, u32[]{:S(2)}, u32[]{:S(2)}) collective-permute-start(bf16[256,1024]{1,0:T(8,128)(2,1)} %collective-permute-done.19.refs_6_), channel_id=1, source_target_pairs={{0,1},{1,0},{32,33},{33,32},{64,65},{65,64},{96,97},{97,96},{2,3},... | collective-permute-start | bytes 1572872 | tf_op jit(solution)/shard_map/ppermute | solution.py:37
  78.6 14.4 %collective-permute-start.14 = (bf16[1,128,1024]{2,1,0:T(8,128)(2,1)S(1)}, bf16[1,128,1024]{2,1,0:T(8,128)(2,1)S(1)}, u32[]{:S(2)}, u32[]{:S(2)}) collective-permute-start(bf16[1,128,1024]{2,1,0:T(8,128)(2,1)S(1)} %get-tuple-element.156), channel_id=1, source_target_pairs={{0,2},{1,3},{32,34},{33,35},{64,66},{65,67},{96,98},{97,99},{2,4},... | collective-permute-start | bytes 786440 | tf_op jit(solution)/shard_map/ppermute | solution.py:37
  80.2 16.0 %collective-permute-start.15 = (bf16[1,128,1024]{2,1,0:T(8,128)(2,1)S(1)}, bf16[1,128,1024]{2,1,0:T(8,128)(2,1)S(1)}, u32[]{:S(2)}, u32[]{:S(2)}) collective-permute-start(bf16[1,128,1024]{2,1,0:T(8,128)(2,1)S(1)} %get-tuple-element.155), channel_id=1, source_target_pairs={{0,6},{1,7},{32,38},{33,39},{64,70},{65,71},{96,102},{97,103},{2,0... | collective-permute-start | bytes 786440 | tf_op jit(solution)/shard_map/ppermute | solution.py:37
  93.0 14.2 %collective-permute-start.11 = (bf16[256,1024]{1,0:T(8,128)(2,1)S(1)}, bf16[256,1024]{1,0:T(8,128)(2,1)S(1)}, u32[]{:S(2)}, u32[]{:S(2)}) collective-permute-start(bf16[256,1024]{1,0:T(8,128)(2,1)S(1)} %fusion.13), channel_id=1, source_target_pairs={{0,8},{1,9},{32,40},{33,41},{64,72},{65,73},{96,104},{97,105},{2,1... | collective-permute-start | bytes 1572872 | tf_op jit(solution)/shard_map/ppermute | solution.py:37
  117.7 26.8 %collective-permute-start.18 = (bf16[4,32,2048]{2,1,0:T(8,128)(2,1)}, bf16[4,32,2048]{2,1,0:T(8,128)(2,1)}, u32[]{:S(2)}, u32[]{:S(2)}) collective-permute-start(bf16[4,32,2048]{2,1,0:T(8,128)(2,1)} %get-tuple-element.137), channel_id=1, source_target_pairs={{0,16},{1,17},{32,48},{33,49},{64,80},{65,81},{96,112},{97,113},{2... | collective-permute-start | bytes 1572872 | tf_op jit(solution)/shard_map/ppermute | solution.py:37
  120.0 17.4 %collective-permute-start.30 = (bf16[1,128,512]{2,1,0:T(8,128)(2,1)S(1)}, bf16[1,128,512]{2,1,0:T(8,128)(2,1)S(1)}, u32[]{:S(2)}, u32[]{:S(2)}) collective-permute-start(bf16[1,128,512]{2,1,0:T(8,128)(2,1)S(1)} %get-tuple-element.164), channel_id=1, source_target_pairs={{0,2},{1,3},{32,34},{33,35},{64,66},{65,67},{96,98},{97,99},{2,4},... | collective-permute-start | bytes 393224 | tf_op jit(solution)/shard_map/ppermute | solution.py:37
  120.1 17.3 %collective-permute-start.31 = (bf16[1,128,512]{2,1,0:T(8,128)(2,1)S(1)}, bf16[1,128,512]{2,1,0:T(8,128)(2,1)S(1)}, u32[]{:S(2)}, u32[]{:S(2)}) collective-permute-start(bf16[1,128,512]{2,1,0:T(8,128)(2,1)S(1)} %get-tuple-element.163), channel_id=1, source_target_pairs={{0,6},{1,7},{32,38},{33,39},{64,70},{65,71},{96,102},{97,103},{2,0... | collective-permute-start | bytes 393224 | tf_op jit(solution)/shard_map/ppermute | solution.py:37
  154.0 19.4 %collective-permute-start.23 = (bf16[2,32,2048]{2,0,1:T(2,128)(2,1)S(1)}, bf16[2,32,2048]{2,0,1:T(2,128)(2,1)S(1)}, u32[]{:S(2)}, u32[]{:S(2)}) collective-permute-start(bf16[2,32,2048]{2,0,1:T(2,128)(2,1)S(1)} %bitcast.116), channel_id=1, source_target_pairs={{0,32},{1,33},{32,64},{33,65},{64,96},{65,97},{96,0},{97,1},{2,34}... | collective-permute-start | bytes 786440 | tf_op jit(solution)/shard_map/ppermute | solution.py:37
  156.3 17.1 %collective-permute-start.24 = (bf16[2,32,2048]{2,0,1:T(2,128)(2,1)S(1)}, bf16[2,32,2048]{2,0,1:T(2,128)(2,1)S(1)}, u32[]{:S(2)}, u32[]{:S(2)}) collective-permute-start(bf16[2,32,2048]{2,0,1:T(2,128)(2,1)S(1)} %bitcast.117), channel_id=1, source_target_pairs={{0,64},{1,65},{32,96},{33,97},{64,0},{65,1},{96,32},{97,33},{2,66}... | collective-permute-start | bytes 786440 | tf_op jit(solution)/shard_map/ppermute | solution.py:37
  158.3 15.1 %collective-permute-start.25 = (bf16[2,32,2048]{2,0,1:T(2,128)(2,1)S(1)}, bf16[2,32,2048]{2,0,1:T(2,128)(2,1)S(1)}, u32[]{:S(2)}, u32[]{:S(2)}) collective-permute-start(bf16[2,32,2048]{2,0,1:T(2,128)(2,1)S(1)} %bitcast.118), channel_id=1, source_target_pairs={{0,96},{1,97},{32,0},{33,1},{64,32},{65,33},{96,64},{97,65},{2,98}... | collective-permute-start | bytes 786440 | tf_op jit(solution)/shard_map/ppermute | solution.py:37
  177.3 23.3 %all-to-all-start.1 = ((f32[128,8,128]{2,1,0:T(8,128)}), f32[128,8,128]{2,1,0:T(8,128)S(1)}, u32[]{:S(2)}, u32[]{:S(2)}) async-start(f32[128,8,128]{2,1,0:T(8,128)} %broadcast_in_dim.6), calls=%async_computation.1 | async-start | bytes 1048576 | tf_op jit(solution)/shard_map/all_to_all | solution.py:222
  206.6 31.1 %all-to-all-start.2 = ((bf16[8,32,4096]{2,1,0:T(8,128)(2,1)}), bf16[8,32,4096]{2,1,0:T(8,128)(2,1)S(1)}, u32[]{:S(2)}, u32[]{:S(2)}) async-start(bf16[8,32,4096]{2,1,0:T(8,128)(2,1)} %broadcast_in_dim.7), calls=%async_computation.2 | async-start | bytes 4194304 | tf_op jit(solution)/shard_map/all_to_all | solution.py:233
  (47 other events, 687.7 us)

commit v2 on v1

v2 whole, which is shorter than its diff:
```python
import functools

import jax
import jax.numpy as jnp
from jax import lax
from jax.experimental import pallas as pl
from jax.experimental.pallas import tpu as pltpu
from jax.sharding import PartitionSpec as P

D_IN = 4096
WIN = 4096
AXES = ("dom", "shard")
EARLY = 1024
CHUNKS = (1024, 1024, 1024)
PIECES = ((0,), (1, 2))
HALF = 128
ORDER = ((0, 0), (0, 1), (1, 0), (3, 1), (2, 0), (1, 1), (2, 1), (3, 0))
PEERS = ((False, False), (False, True), (True, False), (True, True))
F32 = jnp.float32
BF16 = jnp.bfloat16


def device_index(x, y, z, core):
    return (z * 2 + x % 2) * 16 + (x // 2) * 8 + y * 2 + core


def shift(value, dx=0, dy=0, dz=0, pair=0, core=0):
    moves = [
        (
            device_index(x, y, z, c),
            device_index(((x ^ pair) + dx) % 4, (y + dy) % 4, (z + dz) % 4, c ^ core),
        )
        for x in range(4)
        for y in range(4)
        for z in range(4)
        for c in range(2)
    ]
    return lax.ppermute(value, AXES, moves)


def turn_kernel(at_ref, source, *outs):
    x_hi, y, core = at_ref[0], at_ref[1], at_ref[2]
    depth = source.shape[0]
    for out, (flip_x, flip_core) in zip(outs, PEERS):
        a = 1 - x_hi if flip_x else x_hi
        c = 1 - core if flip_core else core
        for i, (step, half) in enumerate(ORDER):
            block = ((a * 4 + lax.rem(y + step, 4)) * 2 + c) * 2 + half
            columns = pl.ds(pl.multiple_of(block * HALF, HALF), HALF)
            out[pl.ds(i % 2 * HALF, HALF), pl.ds(i // 2 * depth, depth)] = source[:, columns].T


def turned_columns(inputs, at):
    rows = inputs.shape[0]
    return pl.pallas_call(
        turn_kernel,
        in_specs=[
            pl.BlockSpec(memory_space=pltpu.SMEM),
            pl.BlockSpec(memory_space=pltpu.VMEM),
        ],
        out_specs=[pl.BlockSpec(memory_space=pltpu.VMEM)] * 4,
        out_shape=[jax.ShapeDtypeStruct((2 * HALF, 4 * rows), BF16)] * 4,
        compiler_params=pltpu.CompilerParams(vmem_limit_bytes=16 * 1024 * 1024),
        cost_estimate=pl.CostEstimate(
            flops=0, bytes_accessed=4 * inputs.size, transcendentals=0
        ),
    )(at, inputs)


def matmul_kernel(sets, terms, *refs):
    lefts, rights, outs = refs[: sets * terms], refs[sets * terms : -4], refs[-4:]
    depth = rights[0].shape[0]
    for r in range(sets):
        for i, out in enumerate(outs):
            total = None
            for left, right in zip(lefts[r * terms : (r + 1) * terms], rights):
                term = jnp.dot(
                    left[:, pl.ds(i * depth, depth)], right[...], preferred_element_type=F32
                )
                total = term if total is None else total + term
            out[r] = total.astype(BF16)


def block_products(sets, rights, width):
    rows, depth = 2 * HALF, rights[0][0].shape[0]
    tile = 512
    n, terms = len(sets), len(rights)
    lefts = sum(sets, [])

    def left_spec(offset):
        return pl.BlockSpec((rows, 4 * depth), lambda i: (0, offset // (4 * depth)))

    def right_spec(offset):
        return pl.BlockSpec((depth, tile), lambda i: (0, i + offset // tile))

    return pl.pallas_call(
        functools.partial(matmul_kernel, n, terms),
        grid=(width // tile,),
        in_specs=[left_spec(o) for _, o in lefts] + [right_spec(o) for _, o in rights],
        out_specs=[pl.BlockSpec((n, rows, tile), lambda i: (0, 0, i))] * 4,
        out_shape=[jax.ShapeDtypeStruct((n, rows, width), BF16)] * 4,
        compiler_params=pltpu.CompilerParams(vmem_limit_bytes=32 * 1024 * 1024),
        cost_estimate=pl.CostEstimate(
            flops=0, bytes_accessed=0,
            transcendentals=0,
        ),
    )(*[v for v, _ in lefts], *[v for v, _ in rights])


def after(values, *done):
    out = lax.optimization_barrier((tuple(values), done))
    return out[0]


def add(a, b):
    return (a.astype(F32) + b.astype(F32)).astype(BF16)


def per_device(inputs, grads_out, domain_weight, domain_ids, mix_weights):
    dom = lax.axis_index("dom")
    shard = lax.axis_index("shard")
    x_hi, y, core = shard // 8, (shard // 2) % 4, shard % 2
    count = D_IN * WIN
    hi = lax.Precision.HIGHEST
    weight = domain_weight[0]

    n_chunks = len(CHUNKS)
    starts = [EARLY + sum(CHUNKS[:k]) for k in range(n_chunks)]
    ends = [start + width for start, width in zip(starts, CHUNKS)]
    spans = [(starts[piece[0]], ends[piece[-1]]) for piece in PIECES]
    own_left, core_left, x_left, both_left = turned_columns(inputs, jnp.stack([x_hi, y, core]))
    grads_core = shift(grads_out, core=1)
    core_left = shift(core_left, core=1)
    both_left = shift(both_left, core=1)
    own_set = [(own_left, 0), (core_left, 0)]
    other_set = [(x_left, 0), (both_left, 0)]
    sent = jnp.concatenate([x_left, both_left, grads_out[:, slice(*spans[0])]], axis=1)
    skip = 2 * x_left.shape[1]
    across = [shift(sent, dx=2)]
    lefts = own_set + [(across[0], 0), (across[0], skip // 2)]
    waits = [sent, across[0]]
    for p in range(1, len(PIECES)):
        (piece,) = after([grads_out[:, slice(*spans[p])]], waits[p - 1])
        across.append(shift(piece, dx=2))
        waits.append(across[-1])
    def reduce_first(products):
        own, keep, up, down = products
        return own, keep, shift(up, dy=1), shift(down, dy=-1)

    def reduce_second(first):
        own, keep, from_back, from_next = first
        sums = add(keep[:, :HALF], from_back[:, :HALF]), add(keep[:, HALF:], from_next[:, :HALF])
        return sums, (
            own, from_back[:, HALF:], from_next[:, HALF:], shift(sums[0], dy=1), shift(sums[1], dy=-1),
        )

    def reduce_last(second, *done):
        own, back_own, next_own, back2, next2 = after(second, *done)
        top = own[:, :HALF].astype(F32) + back2.astype(F32) + next_own.astype(F32)
        bottom = own[:, HALF:].astype(F32) + back_own.astype(F32) + next2.astype(F32)
        return jnp.concatenate([top, bottom], axis=1)

    def centered(weff_grad, start):
        block = weight[:, start : start + weff_grad.shape[1]].astype(F32)
        return (weff_grad * block).astype(BF16)

    def spread(*centers):
        pieces = jnp.concatenate(centers, axis=1)
        return lax.all_to_all(pieces.reshape(8, 32, -1), "dom", 0, 0, tiled=True)

    swapped = {}

    def products(k, *done):
        p = next(p for p, piece in enumerate(PIECES) if k in piece)
        inner = starts[k] - spans[p][0]
        if p not in swapped:
            (far,) = after([across[p]], *done)
            swapped[p] = shift(far if p else far[:, skip:], core=1)
        far, far_core = after([across[p], swapped[p]], *done)
        rights = [
            (grads_out, starts[k]), (grads_core, starts[k]), (far, inner + (0 if p else skip)), (far_core, inner),
        ]
        return block_products([lefts], rights, CHUNKS[k])

    first = reduce_first(block_products([own_set, other_set], [(grads_out, 0), (grads_core, 0)], EARLY))
    sums, early = reduce_second(first)

    def partial_gram(slots):
        flat = slots.reshape(8, -1)
        return lax.dot_general(flat, flat, (((1,), (1,)), ((), ())), preferred_element_type=F32)

    out0 = products(0, *sums)
    first = reduce_first(out0)
    early = reduce_last(early, out0[2])
    early_other = early[1].astype(BF16)
    sums, second0 = reduce_second(first)
    out1 = products(1, *sums, early_other)
    early_other = shift(early_other, dx=2)
    first1 = reduce_first(out1)
    out2 = products(2, out1[2])
    first2 = reduce_first(out2)
    sums, second1 = reduce_second(after(first1, out2[2]))
    center_early = centered(early[0] + after([early_other], *sums)[0].astype(F32), 0)
    center0 = centered(reduce_last(second0, *sums)[0], starts[0])
    slots = [spread(center_early, center0)]
    sums, second2 = reduce_second(after(first2, center_early, center0))
    center1 = centered(reduce_last(second1, *sums)[0], starts[1])
    slots.append(spread(after([center1], slots[0])[0]))
    gram_slots = partial_gram(slots[0])
    center2 = centered(reduce_last(second2, center1, gram_slots, slots[1])[0], starts[2])
    slots.append(spread(center2))
    gram_slots = gram_slots + partial_gram(slots[1]) + partial_gram(slots[2])

    labels = jnp.arange(8, dtype=jnp.int32)
    onehot = (domain_ids[:, None] == labels[None, :]).astype(F32)
    weights = jnp.dot(onehot, mix_weights, precision=hi)

    local = gram_slots.reshape(1, 1, 64)
    sent = jnp.broadcast_to(jnp.pad(local, ((0, 0), (0, 0), (0, 64))), (128, 1, 128))
    parts = lax.all_to_all(sent, AXES, 0, 0, tiled=True)
    group_gram = jnp.sum(parts, axis=(0, 1))[:64].reshape(8, 8) / count
    scale = weights / jnp.sqrt(jnp.diagonal(group_gram) + 1e-06)

    def mixed(slots):
        return jnp.sum(scale[:, None, None] * slots.astype(F32), axis=0).astype(BF16)

    owned = jnp.concatenate([mixed(received) for received in slots], axis=1)
    combined = lax.all_to_all(jnp.broadcast_to(owned[None], (8, *owned.shape)), "dom", 0, 0, tiled=True)
    gram = jnp.dot(jnp.dot(onehot.T, group_gram, precision=hi), onehot, precision=hi)
    return (combined.reshape(-1, WIN), gram)


def solution(mesh):
    in_specs = (
        P(AXES, None),
        P(AXES, None),
        P("dom", "shard", None),
        P(),
        P(),
    )
    out_specs = (P("shard", None), P())
    return jax.shard_map(
        per_device, mesh=mesh, in_specs=in_specs, out_specs=out_specs, check_vma=False
    )
```

time: 240 us -> 209 us (0.87)
  starting transfers between devices: 81.9 us -> 52.7 us
  blocking collectives: 0 us -> 14 us
  waiting for transfers between devices: 109 us -> 99.5 us
  local copies, waits for them, and re-layouts: 13 us -> 8.99 us
    ppermute x40 -> x24, starting transfers between devices: 63.3 us -> 34 us  [shift(): return lax.ppermute(value, AXES, moves)]
    all_to_all x0 -> x1, blocking collectives: none -> 14 us  [spread(): return lax.all_to_all(pieces.reshape(8, 32, -1), 'dom', 0, 0, tiled=True)]
    ppermute x40 -> x24, waiting for transfers between devices: 67.8 us -> 60.2 us  [shift(): return lax.ppermute(value, AXES, moves)]
    all_to_all x1 -> x2, starting transfers between devices: 4.74 us -> 9.87 us  [spread(): return lax.all_to_all(pieces.reshape(8, 32, -1), 'dom', 0, 0, tiled=True)]
    all_to_all x1, starting transfers between devices: 10.2 us -> 5.2 us  [per_device(): parts = lax.all_to_all(sent, AXES, 0, 0, tiled=True)]
    all_to_all x1, waiting for transfers between devices: 13.1 us -> 9.24 us  [per_device(): parts = lax.all_to_all(sent, AXES, 0, 0, tiled=True)]
    reduce_sum x5 -> x3, other arithmetic: 3.43 us -> 0.58 us  [the longest x2 0.54 us: mixed(): jnp.sum(scale[:, None, None] * slots.astype(F32), axis=0).astype(BF16)]
    pallas_call x5 -> x4, Pallas kernels: 16.7 us -> 15.6 us  [block_products(): pl.pallas_call(functools.partial(matmul_kernel, n, terms), grid=(width //...]
  transfers between devices with their start and end apart: 43 -> 28, of which waited for: 17 -> 19; matrix products, arithmetic and copies ran while one was open for 7% -> 6% of each run, Pallas kernels for 7% -> 6%
where the time goes in v2:
time: 209 us; the launch traced here: 208 us
  waiting for transfers between devices  99.5 us (48%)
  starting transfers between devices  52.7 us (25%)
  Pallas kernels  16.8 us (8%)
  blocking collectives  14 us (7%)
  other arithmetic  11.5 us (6%)
  local copies, waits for them, and re-layouts  8.99 us (4%)
  matrix products  3.51 us (2%)
    ppermute x24, waiting for transfers between devices, shift(): return lax.ppermute(value, AXES, moves)  60.2 us
    ppermute x24, starting transfers between devices, shift(): return lax.ppermute(value, AXES, moves)  34 us
    all_to_all x1, waiting for transfers between devices, per_device(): lax.all_to_all(jnp.broadcast_to(owned[None], (8, *owned.shape)), 'dom', 0...  26.2 us
    pallas_call x4, Pallas kernels, block_products(): pl.pallas_call(functools.partial(matmul_kernel, n, terms), grid=(width //...  15.6 us
    all_to_all x1, blocking collectives, spread(): return lax.all_to_all(pieces.reshape(8, 32, -1), 'dom', 0, 0, tiled=True)  14 us
    all_to_all x2, starting transfers between devices, spread(): return lax.all_to_all(pieces.reshape(8, 32, -1), 'dom', 0, 0, tiled=True)  9.87 us
    all_to_all x1, waiting for transfers between devices, per_device(): parts = lax.all_to_all(sent, AXES, 0, 0, tiled=True)  9.24 us
    all_to_all x1, starting transfers between devices, per_device(): parts = lax.all_to_all(sent, AXES, 0, 0, tiled=True)  5.2 us
  transfers between devices with their start and end apart: 28, of which 19 were waited for; matrix products, arithmetic and copies ran while one was open for 6% of the time, Pallas kernels for 6%

profile of v2, /device:TPU:0, one launch (start us, length us, event | category | flops | bytes accessed | tf_op | source)
XLA Modules:
  0.0 208.0 jit_solution(5727963760826891205)
XLA Ops:
  5.8 3.2 %collective-permute-start.7 = (bf16[256,3072]{1,0:T(8,128)(2,1)S(1)}, bf16[256,3072]{1,0:T(8,128)(2,1)S(1)}, u32[]{:S(2)}, u32[]{:S(2)}) collective-permute-start(bf16[256,3072]{1,0:T(8,128)(2,1)S(1)} %pad_maximum_fusion), channel_id=1, source_target_pairs={{0,8},{1,9},{32,40},{33,41},{64,72},{65,73},{96,104},{97,105},{2,1... | collective-permute-start | bytes 4718600 | tf_op jit(solution)/shard_map/ppermute | solution.py:38
  9.0 3.8 %shard_map.69 = (bf16[2,256,1024]{2,1,0:T(8,128)(2,1)S(1)}, bf16[2,256,1024]{2,1,0:T(8,128)(2,1)S(1)}, bf16[2,256,1024]{2,1,0:T(8,128)(2,1)S(1)}, bf16[2,256,1024]{2,1,0:T(8,128)(2,1)S(1)}) custom-call(bf16[256,1024]{1,0:T(8,128)(2,1)S(1)} %get-tuple-element.61.refs_0_, bf16[256,1024]{1,0:T(8,128)(2,1)S(1)} %collective-permute-done.refs_1_, ...), custom_call_target="tpu_custom_call" | custom-call | tf_op jit(solution)/shard_map/pallas_call | solution.py:96
  16.2 23.1 %collective-permute-done.3 = bf16[2,256,1024]{2,1,0:T(8,128)(2,1)S(1)} collective-permute-done((bf16[2,256,1024]{2,1,0:T(8,128)(2,1)S(1)}, bf16[2,256,1024]{2,1,0:T(8,128)(2,1)S(1)}, u32[]{:S(2)}, u32[]{:S(2)}) %collective-permute-start.3) | collective-permute-done | bytes 1048608 | tf_op jit(solution)/shard_map/ppermute | solution.py:38
  39.7 4.3 %collective-permute-done.7.refs_2_.refs_3_.refs_6_ = bf16[256,3072]{1,0:T(8,128)(2,1)S(1)} collective-permute-done((bf16[256,3072]{1,0:T(8,128)(2,1)S(1)}, bf16[256,3072]{1,0:T(8,128)(2,1)S(1)}, u32[]{:S(2)}, u32[]{:S(2)}) %collective-permute-start.7) | collective-permute-done | bytes 1572896 | tf_op jit(solution)/shard_map/ppermute | solution.py:38
  44.2 3.2 %collective-permute-start.6 = (bf16[2,128,1024]{2,1,0:T(8,128)(2,1)S(1)}, bf16[2,128,1024]{2,1,0:T(8,128)(2,1)S(1)}, u32[]{:S(2)}, u32[]{:S(2)}) collective-permute-start(bf16[2,128,1024]{2,1,0:T(8,128)(2,1)S(1)} %get-tuple-element.126), channel_id=1, source_target_pairs={{0,6},{1,7},{32,38},{33,39},{64,70},{65,71},{96,102},{97,103},{2,0... | collective-permute-start | bytes 1572872 | tf_op jit(solution)/shard_map/ppermute | solution.py:38
  47.4 3.1 %collective-permute-start.10 = (bf16[256,2048]{1,0:T(8,128)(2,1)S(1)}, bf16[256,2048]{1,0:T(8,128)(2,1)S(1)}, u32[]{:S(2)}, u32[]{:S(2)}) collective-permute-start(bf16[256,2048]{1,0:T(8,128)(2,1)S(1)} %slice.147), channel_id=1, source_target_pairs={{0,8},{1,9},{32,40},{33,41},{64,72},{65,73},{96,104},{97,105},{2,1... | collective-permute-start | bytes 3145736 | tf_op jit(solution)/shard_map/ppermute | solution.py:38
  50.5 3.7 %shard_map.70 = (bf16[1,256,1024]{2,1,0:T(8,128)(2,1)S(1)}, bf16[1,256,1024]{2,1,0:T(8,128)(2,1)S(1)}, bf16[1,256,1024]{2,1,0:T(8,128)(2,1)S(1)}, bf16[1,256,1024]{2,1,0:T(8,128)(2,1)S(1)}) custom-call(bf16[256,1024]{1,0:T(8,128)(2,1)S(1)} %get-tuple-element.61.refs_0_, bf16[256,1024]{1,0:T(8,128)(2,1)S(1)} %collective-permute-done.refs_1_, ...), custom_call_target="tpu_custom_call" | custom-call | tf_op jit(solution)/shard_map/pallas_call | solution.py:96
  54.2 3.3 %collective-permute-start.12 = (bf16[1,256,1024]{2,1,0:T(8,128)(2,1)S(1)}, bf16[1,256,1024]{2,1,0:T(8,128)(2,1)S(1)}, u32[]{:S(2)}, u32[]{:S(2)}) collective-permute-start(bf16[1,256,1024]{2,1,0:T(8,128)(2,1)S(1)} %get-tuple-element.80), channel_id=1, source_target_pairs={{0,6},{1,7},{32,38},{33,39},{64,70},{65,71},{96,102},{97,103},{2,0... | collective-permute-start | bytes 1572872 | tf_op jit(solution)/shard_map/ppermute | solution.py:38
  59.6 3.7 %collective-permute-done.5 = bf16[2,128,1024]{2,1,0:T(8,128)(2,1)S(1)} collective-permute-done((bf16[2,128,1024]{2,1,0:T(8,128)(2,1)S(1)}, bf16[2,128,1024]{2,1,0:T(8,128)(2,1)S(1)}, u32[]{:S(2)}, u32[]{:S(2)}) %collective-permute-start.5) | collective-permute-done | bytes 524320 | tf_op jit(solution)/shard_map/ppermute | solution.py:38
  64.0 6.4 %collective-permute-done.12 = bf16[1,256,1024]{2,1,0:T(8,128)(2,1)S(1)} collective-permute-done((bf16[1,256,1024]{2,1,0:T(8,128)(2,1)S(1)}, bf16[1,256,1024]{2,1,0:T(8,128)(2,1)S(1)}, u32[]{:S(2)}, u32[]{:S(2)}) %collective-permute-start.12) | collective-permute-done | bytes 524320 | tf_op jit(solution)/shard_map/ppermute | solution.py:38
  70.4 3.4 %collective-permute-done.11 = bf16[1,256,1024]{2,1,0:T(8,128)(2,1)S(1)} collective-permute-done((bf16[1,256,1024]{2,1,0:T(8,128)(2,1)S(1)}, bf16[1,256,1024]{2,1,0:T(8,128)(2,1)S(1)}, u32[]{:S(2)}, u32[]{:S(2)}) %collective-permute-start.11) | collective-permute-done | bytes 524320 | tf_op jit(solution)/shard_map/ppermute | solution.py:38
  76.9 3.7 %shard_map.71 = (bf16[1,256,1024]{2,1,0:T(8,128)(2,1)S(1)}, bf16[1,256,1024]{2,1,0:T(8,128)(2,1)S(1)}, bf16[1,256,1024]{2,1,0:T(8,128)(2,1)S(1)}, bf16[1,256,1024]{2,1,0:T(8,128)(2,1)S(1)}) custom-call(bf16[256,1024]{1,0:T(8,128)(2,1)S(1)} %get-tuple-element.61.refs_0_, bf16[256,1024]{1,0:T(8,128)(2,1)S(1)} %collective-permute-done.refs_1_, ...), custom_call_target="tpu_custom_call" | custom-call | tf_op jit(solution)/shard_map/pallas_call | solution.py:96
  86.6 3.2 %collective-permute-start.17 = (bf16[1,128,1024]{2,1,0:T(8,128)(2,1)S(1)}, bf16[1,128,1024]{2,1,0:T(8,128)(2,1)S(1)}, u32[]{:S(2)}, u32[]{:S(2)}) collective-permute-start(bf16[1,128,1024]{2,1,0:T(8,128)(2,1)S(1)} %get-tuple-element.138), channel_id=1, source_target_pairs={{0,6},{1,7},{32,38},{33,39},{64,70},{65,71},{96,102},{97,103},{2,0... | collective-permute-start | bytes 786440 | tf_op jit(solution)/shard_map/ppermute | solution.py:38
  89.9 4.5 %shard_map.72 = (bf16[1,256,1024]{2,1,0:T(8,128)(2,1)S(1)}, bf16[1,256,1024]{2,1,0:T(8,128)(2,1)S(1)}, bf16[1,256,1024]{2,1,0:T(8,128)(2,1)}, bf16[1,256,1024]{2,1,0:T(8,128)(2,1)}) custom-call(bf16[256,1024]{1,0:T(8,128)(2,1)S(1)} %get-tuple-element.61.refs_0_, bf16[256,1024]{1,0:T(8,128)(2,1)S(1)} %collective-permute-done.refs_1_, ...), custom_call_target="tpu_custom_call" | custom-call | tf_op jit(solution)/shard_map/pallas_call | solution.py:96
  95.9 3.7 %collective-permute-start.21 = (bf16[1,256,1024]{2,1,0:T(8,128)(2,1)}, bf16[1,256,1024]{2,1,0:T(8,128)(2,1)}, u32[]{:S(2)}, u32[]{:S(2)}) collective-permute-start(bf16[1,256,1024]{2,1,0:T(8,128)(2,1)} %get-tuple-element.104), channel_id=1, source_target_pairs={{0,6},{1,7},{32,38},{33,39},{64,70},{65,71},{96,102},{97,103},{2,0... | collective-permute-start | bytes 1572872 | tf_op jit(solution)/shard_map/ppermute | solution.py:38
  101.5 3.7 %collective-permute-done.16 = bf16[1,128,1024]{2,1,0:T(8,128)(2,1)S(1)} collective-permute-done((bf16[1,128,1024]{2,1,0:T(8,128)(2,1)S(1)}, bf16[1,128,1024]{2,1,0:T(8,128)(2,1)S(1)}, u32[]{:S(2)}, u32[]{:S(2)}) %collective-permute-start.16) | collective-permute-done | bytes 262176 | tf_op jit(solution)/shard_map/ppermute | solution.py:38
  107.1 6.4 %all-to-all-start = ((bf16[8,32,2048]{2,1,0:T(8,128)(2,1)}), bf16[8,32,2048]{2,1,0:T(8,128)(2,1)S(1)}, u32[]{:S(2)}, u32[]{:S(2)}) async-start(bf16[8,32,2048]{2,1,0:T(8,128)(2,1)} %bitcast.61), calls=%async_computation | async-start | bytes 2097152 | tf_op jit(solution)/shard_map/all_to_all | solution.py:169
  123.5 3.8 %all-to-all-done = bf16[8,32,2048]{2,1,0:T(8,128)(2,1)S(1)} async-done(((bf16[8,32,2048]{2,1,0:T(8,128)(2,1)}), bf16[8,32,2048]{2,1,0:T(8,128)(2,1)S(1)}, u32[]{:S(2)}, u32[]{:S(2)}) %all-to-all-start) | async-done | bytes 1048608 | tf_op jit(solution)/shard_map/all_to_all | solution.py:169
  127.3 3.5 %all-to-all-start.1 = ((bf16[8,32,1024]{2,1,0:T(8,128)(2,1)}), bf16[8,32,1024]{2,1,0:T(8,128)(2,1)S(1)}, u32[]{:S(2)}, u32[]{:S(2)}) async-start(bf16[8,32,1024]{2,1,0:T(8,128)(2,1)} %bitcast.12), calls=%async_computation.1 | async-start | bytes 1048576 | tf_op jit(solution)/shard_map/all_to_all | solution.py:169
  142.3 14.0 %all_to_all.25 = bf16[8,32,1024]{2,1,0:T(8,128)(2,1)S(1)} all-to-all(bf16[8,32,1024]{2,1,0:T(8,128)(2,1)S(1)} %bitcast.62), channel_id=1, replica_groups=mesh['dom'=8,'shard'=16] {'dom'}, dimensions={0} | all-to-all | bytes 1048576 | tf_op jit(solution)/shard_map/all_to_all | solution.py:169
  158.2 5.2 %all-to-all-start.3 = ((f32[128,1,128]{2,1,0:T(1,128)}), f32[128,1,128]{2,1,0:T(1,128)S(1)}, u32[]{:S(2)}, u32[]{:S(2)}) async-start(f32[128,1,128]{2,1,0:T(1,128)} %broadcast_in_dim.11), calls=%async_computation.3 | async-start | bytes 131072 | tf_op jit(solution)/shard_map/all_to_all | solution.py:220
  163.5 9.2 %all-to-all-done.3 = f32[128,1,128]{2,1,0:T(1,128)S(1)} async-done(((f32[128,1,128]{2,1,0:T(1,128)}), f32[128,1,128]{2,1,0:T(1,128)S(1)}, u32[]{:S(2)}, u32[]{:S(2)}) %all-to-all-start.3) | async-done | bytes 65568 | tf_op jit(solution)/shard_map/all_to_all | solution.py:220
  175.8 3.6 %all-to-all-start.4 = ((bf16[8,32,4096]{2,1,0:T(8,128)(2,1)}), bf16[8,32,4096]{2,1,0:T(8,128)(2,1)S(1)}, u32[]{:S(2)}, u32[]{:S(2)}) async-start(bf16[8,32,4096]{2,1,0:T(8,128)(2,1)} %broadcast_in_dim.12), calls=%async_computation.4 | async-start | bytes 4194304 | tf_op jit(solution)/shard_map/all_to_all | solution.py:228
  180.4 26.2 %all-to-all-done.4 = bf16[8,32,4096]{2,1,0:T(8,128)(2,1)S(1)} async-done(((bf16[8,32,4096]{2,1,0:T(8,128)(2,1)}), bf16[8,32,4096]{2,1,0:T(8,128)(2,1)S(1)}, u32[]{:S(2)}, u32[]{:S(2)}) %all-to-all-start.4) | async-done | bytes 2097184 | tf_op jit(solution)/shard_map/all_to_all | solution.py:228
  (115 shorter events, 55.0 us)
Async XLA Ops:
  0.7 8.4 %collective-permute-start.2 = (bf16[256,4096]{1,0:T(8,128)(2,1)}, bf16[256,4096]{1,0:T(8,128)(2,1)}, u32[]{:S(2)}, u32[]{:S(2)}) collective-permute-start(bf16[256,4096]{1,0:T(8,128)(2,1)} %refs_4_.7), channel_id=1, source_target_pairs={{0,1},{1,0},{32,33},{33,32},{64,65},{65,64},{96,97},{97,96},{2,3},... | collective-permute-start | bytes 6291464 | tf_op jit(solution)/shard_map/ppermute | solution.py:38
  5.8 38.2 %collective-permute-start.7 = (bf16[256,3072]{1,0:T(8,128)(2,1)S(1)}, bf16[256,3072]{1,0:T(8,128)(2,1)S(1)}, u32[]{:S(2)}, u32[]{:S(2)}) collective-permute-start(bf16[256,3072]{1,0:T(8,128)(2,1)S(1)} %pad_maximum_fusion), channel_id=1, source_target_pairs={{0,8},{1,9},{32,40},{33,41},{64,72},{65,73},{96,104},{97,105},{2,1... | collective-permute-start | bytes 4718600 | tf_op jit(solution)/shard_map/ppermute | solution.py:38
  12.9 26.5 %collective-permute-start.3 = (bf16[2,256,1024]{2,1,0:T(8,128)(2,1)S(1)}, bf16[2,256,1024]{2,1,0:T(8,128)(2,1)S(1)}, u32[]{:S(2)}, u32[]{:S(2)}) collective-permute-start(bf16[2,256,1024]{2,1,0:T(8,128)(2,1)S(1)} %get-tuple-element.66), channel_id=1, source_target_pairs={{0,2},{1,3},{32,34},{33,35},{64,66},{65,67},{96,98},{97,99},{2,4},... | collective-permute-start | bytes 3145736 | tf_op jit(solution)/shard_map/ppermute | solution.py:38
  14.5 24.8 %collective-permute-start.4 = (bf16[2,256,1024]{2,1,0:T(8,128)(2,1)S(1)}, bf16[2,256,1024]{2,1,0:T(8,128)(2,1)S(1)}, u32[]{:S(2)}, u32[]{:S(2)}) collective-permute-start(bf16[2,256,1024]{2,1,0:T(8,128)(2,1)S(1)} %get-tuple-element.67), channel_id=1, source_target_pairs={{0,6},{1,7},{32,38},{33,39},{64,70},{65,71},{96,102},{97,103},{2,0... | collective-permute-start | bytes 3145736 | tf_op jit(solution)/shard_map/ppermute | solution.py:38
  44.2 15.4 %collective-permute-start.6 = (bf16[2,128,1024]{2,1,0:T(8,128)(2,1)S(1)}, bf16[2,128,1024]{2,1,0:T(8,128)(2,1)S(1)}, u32[]{:S(2)}, u32[]{:S(2)}) collective-permute-start(bf16[2,128,1024]{2,1,0:T(8,128)(2,1)S(1)} %get-tuple-element.126), channel_id=1, source_target_pairs={{0,6},{1,7},{32,38},{33,39},{64,70},{65,71},{96,102},{97,103},{2,0... | collective-permute-start | bytes 1572872 | tf_op jit(solution)/shard_map/ppermute | solution.py:38
  47.3 16.0 %collective-permute-start.5 = (bf16[2,128,1024]{2,1,0:T(8,128)(2,1)S(1)}, bf16[2,128,1024]{2,1,0:T(8,128)(2,1)S(1)}, u32[]{:S(2)}, u32[]{:S(2)}) collective-permute-start(bf16[2,128,1024]{2,1,0:T(8,128)(2,1)S(1)} %get-tuple-element.127), channel_id=1, source_target_pairs={{0,2},{1,3},{32,34},{33,35},{64,66},{65,67},{96,98},{97,99},{2,4},... | collective-permute-start | bytes 1572872 | tf_op jit(solution)/shard_map/ppermute | solution.py:38
  47.4 26.8 %collective-permute-start.10 = (bf16[256,2048]{1,0:T(8,128)(2,1)S(1)}, bf16[256,2048]{1,0:T(8,128)(2,1)S(1)}, u32[]{:S(2)}, u32[]{:S(2)}) collective-permute-start(bf16[256,2048]{1,0:T(8,128)(2,1)S(1)} %slice.147), channel_id=1, source_target_pairs={{0,8},{1,9},{32,40},{33,41},{64,72},{65,73},{96,104},{97,105},{2,1... | collective-permute-start | bytes 3145736 | tf_op jit(solution)/shard_map/ppermute | solution.py:38
  54.2 16.2 %collective-permute-start.12 = (bf16[1,256,1024]{2,1,0:T(8,128)(2,1)S(1)}, bf16[1,256,1024]{2,1,0:T(8,128)(2,1)S(1)}, u32[]{:S(2)}, u32[]{:S(2)}) collective-permute-start(bf16[1,256,1024]{2,1,0:T(8,128)(2,1)S(1)} %get-tuple-element.80), channel_id=1, source_target_pairs={{0,6},{1,7},{32,38},{33,39},{64,70},{65,71},{96,102},{97,103},{2,0... | collective-permute-start | bytes 1572872 | tf_op jit(solution)/shard_map/ppermute | solution.py:38
  57.5 16.3 %collective-permute-start.11 = (bf16[1,256,1024]{2,1,0:T(8,128)(2,1)S(1)}, bf16[1,256,1024]{2,1,0:T(8,128)(2,1)S(1)}, u32[]{:S(2)}, u32[]{:S(2)}) collective-permute-start(bf16[1,256,1024]{2,1,0:T(8,128)(2,1)S(1)} %get-tuple-element.72), channel_id=1, source_target_pairs={{0,2},{1,3},{32,34},{33,35},{64,66},{65,67},{96,98},{97,99},{2,4},... | collective-permute-start | bytes 1572872 | tf_op jit(solution)/shard_map/ppermute | solution.py:38
  80.6 15.3 %collective-permute-start.15 = (bf16[1,256,1024]{2,1,0:T(8,128)(2,1)S(1)}, bf16[1,256,1024]{2,1,0:T(8,128)(2,1)S(1)}, u32[]{:S(2)}, u32[]{:S(2)}) collective-permute-start(bf16[1,256,1024]{2,1,0:T(8,128)(2,1)S(1)} %get-tuple-element.87), channel_id=1, source_target_pairs={{0,6},{1,7},{32,38},{33,39},{64,70},{65,71},{96,102},{97,103},{2,0... | collective-permute-start | bytes 1572872 | tf_op jit(solution)/shard_map/ppermute | solution.py:38
  83.6 16.0 %collective-permute-start.14 = (bf16[1,256,1024]{2,1,0:T(8,128)(2,1)S(1)}, bf16[1,256,1024]{2,1,0:T(8,128)(2,1)S(1)}, u32[]{:S(2)}, u32[]{:S(2)}) collective-permute-start(bf16[1,256,1024]{2,1,0:T(8,128)(2,1)S(1)} %get-tuple-element.86), channel_id=1, source_target_pairs={{0,2},{1,3},{32,34},{33,35},{64,66},{65,67},{96,98},{97,99},{2,4},... | collective-permute-start | bytes 1572872 | tf_op jit(solution)/shard_map/ppermute | solution.py:38
  83.6 21.6 %collective-permute-start.9 = (bf16[256,1024]{1,0:T(8,128)(2,1)S(1)}, bf16[256,1024]{1,0:T(8,128)(2,1)S(1)}, u32[]{:S(2)}, u32[]{:S(2)}) collective-permute-start(bf16[256,1024]{1,0:T(8,128)(2,1)S(1)} %fusion.16), channel_id=1, source_target_pairs={{0,8},{1,9},{32,40},{33,41},{64,72},{65,73},{96,104},{97,105},{2,1... | collective-permute-start | bytes 1572872 | tf_op jit(solution)/shard_map/ppermute | solution.py:38
  86.6 14.9 %collective-permute-start.17 = (bf16[1,128,1024]{2,1,0:T(8,128)(2,1)S(1)}, bf16[1,128,1024]{2,1,0:T(8,128)(2,1)S(1)}, u32[]{:S(2)}, u32[]{:S(2)}) collective-permute-start(bf16[1,128,1024]{2,1,0:T(8,128)(2,1)S(1)} %get-tuple-element.138), channel_id=1, source_target_pairs={{0,6},{1,7},{32,38},{33,39},{64,70},{65,71},{96,102},{97,103},{2,0... | collective-permute-start | bytes 786440 | tf_op jit(solution)/shard_map/ppermute | solution.py:38
  89.9 15.4 %collective-permute-start.16 = (bf16[1,128,1024]{2,1,0:T(8,128)(2,1)S(1)}, bf16[1,128,1024]{2,1,0:T(8,128)(2,1)S(1)}, u32[]{:S(2)}, u32[]{:S(2)}) collective-permute-start(bf16[1,128,1024]{2,1,0:T(8,128)(2,1)S(1)} %get-tuple-element.139), channel_id=1, source_target_pairs={{0,2},{1,3},{32,34},{33,35},{64,66},{65,67},{96,98},{97,99},{2,4},... | collective-permute-start | bytes 786440 | tf_op jit(solution)/shard_map/ppermute | solution.py:38
  95.9 19.7 %collective-permute-start.21 = (bf16[1,256,1024]{2,1,0:T(8,128)(2,1)}, bf16[1,256,1024]{2,1,0:T(8,128)(2,1)}, u32[]{:S(2)}, u32[]{:S(2)}) collective-permute-start(bf16[1,256,1024]{2,1,0:T(8,128)(2,1)} %get-tuple-element.104), channel_id=1, source_target_pairs={{0,6},{1,7},{32,38},{33,39},{64,70},{65,71},{96,102},{97,103},{2,0... | collective-permute-start | bytes 1572872 | tf_op jit(solution)/shard_map/ppermute | solution.py:38
  99.6 16.0 %collective-permute-start.20 = (bf16[1,256,1024]{2,1,0:T(8,128)(2,1)}, bf16[1,256,1024]{2,1,0:T(8,128)(2,1)}, u32[]{:S(2)}, u32[]{:S(2)}) collective-permute-start(bf16[1,256,1024]{2,1,0:T(8,128)(2,1)} %get-tuple-element.90), channel_id=1, source_target_pairs={{0,2},{1,3},{32,34},{33,35},{64,66},{65,67},{96,98},{97,99},{2,4},... | collective-permute-start | bytes 1572872 | tf_op jit(solution)/shard_map/ppermute | solution.py:38
  107.1 20.2 %all-to-all-start = ((bf16[8,32,2048]{2,1,0:T(8,128)(2,1)}), bf16[8,32,2048]{2,1,0:T(8,128)(2,1)S(1)}, u32[]{:S(2)}, u32[]{:S(2)}) async-start(bf16[8,32,2048]{2,1,0:T(8,128)(2,1)} %bitcast.61), calls=%async_computation | async-start | bytes 2097152 | tf_op jit(solution)/shard_map/all_to_all | solution.py:169
  113.5 6.4 %collective-permute-start.19 = (bf16[1,128,1024]{2,1,0:T(8,128)(2,1)S(1)}, bf16[1,128,1024]{2,1,0:T(8,128)(2,1)S(1)}, u32[]{:S(2)}, u32[]{:S(2)}) collective-permute-start(bf16[1,128,1024]{2,1,0:T(8,128)(2,1)S(1)} %copy-done.12), channel_id=1, source_target_pairs={{0,6},{1,7},{32,38},{33,39},{64,70},{65,71},{96,102},{97,103},{2,0... | collective-permute-start | bytes 786440 | tf_op jit(solution)/shard_map/ppermute | solution.py:38
  113.6 7.7 %collective-permute-start.18 = (bf16[1,128,1024]{2,1,0:T(8,128)(2,1)S(1)}, bf16[1,128,1024]{2,1,0:T(8,128)(2,1)S(1)}, u32[]{:S(2)}, u32[]{:S(2)}) collective-permute-start(bf16[1,128,1024]{2,1,0:T(8,128)(2,1)S(1)} %copy-done.11), channel_id=1, source_target_pairs={{0,2},{1,3},{32,34},{33,35},{64,66},{65,67},{96,98},{97,99},{2,4},... | collective-permute-start | bytes 786440 | tf_op jit(solution)/shard_map/ppermute | solution.py:38
  127.3 12.6 %all-to-all-start.1 = ((bf16[8,32,1024]{2,1,0:T(8,128)(2,1)}), bf16[8,32,1024]{2,1,0:T(8,128)(2,1)S(1)}, u32[]{:S(2)}, u32[]{:S(2)}) async-start(bf16[8,32,1024]{2,1,0:T(8,128)(2,1)} %bitcast.12), calls=%async_computation.1 | async-start | bytes 1048576 | tf_op jit(solution)/shard_map/all_to_all | solution.py:169
  130.8 6.7 %collective-permute-start.23 = (bf16[1,128,1024]{2,1,0:T(8,128)(2,1)}, bf16[1,128,1024]{2,1,0:T(8,128)(2,1)S(1)}, u32[]{:S(2)}, u32[]{:S(2)}) collective-permute-start(bf16[1,128,1024]{2,1,0:T(8,128)(2,1)} %get-tuple-element.132), channel_id=1, source_target_pairs={{0,6},{1,7},{32,38},{33,39},{64,70},{65,71},{96,102},{97,103},{2,0... | collective-permute-start | bytes 786440 | tf_op jit(solution)/shard_map/ppermute | solution.py:38
  131.4 7.8 %collective-permute-start.22 = (bf16[1,128,1024]{2,1,0:T(8,128)(2,1)}, bf16[1,128,1024]{2,1,0:T(8,128)(2,1)S(1)}, u32[]{:S(2)}, u32[]{:S(2)}) collective-permute-start(bf16[1,128,1024]{2,1,0:T(8,128)(2,1)} %get-tuple-element.133), channel_id=1, source_target_pairs={{0,2},{1,3},{32,34},{33,35},{64,66},{65,67},{96,98},{97,99},{2,4},... | collective-permute-start | bytes 786440 | tf_op jit(solution)/shard_map/ppermute | solution.py:38
  158.2 14.5 %all-to-all-start.3 = ((f32[128,1,128]{2,1,0:T(1,128)}), f32[128,1,128]{2,1,0:T(1,128)S(1)}, u32[]{:S(2)}, u32[]{:S(2)}) async-start(f32[128,1,128]{2,1,0:T(1,128)} %broadcast_in_dim.11), calls=%async_computation.3 | async-start | bytes 131072 | tf_op jit(solution)/shard_map/all_to_all | solution.py:220
  175.8 30.9 %all-to-all-start.4 = ((bf16[8,32,4096]{2,1,0:T(8,128)(2,1)}), bf16[8,32,4096]{2,1,0:T(8,128)(2,1)S(1)}, u32[]{:S(2)}, u32[]{:S(2)}) async-start(bf16[8,32,4096]{2,1,0:T(8,128)(2,1)} %broadcast_in_dim.12), calls=%async_computation.4 | async-start | bytes 4194304 | tf_op jit(solution)/shard_map/all_to_all | solution.py:228
  (22 other events, 370.1 us)

commit v3 on v2

--- a/solution.py
+++ b/solution.py
@@ -10,9 +10,9 @@
 D_IN = 4096
 WIN = 4096
 AXES = ("dom", "shard")
-EARLY = 1024
-CHUNKS = (1024, 1024, 1024)
-PIECES = ((0,), (1, 2))
+EARLY = 1536
+CHUNKS = (1024, 1536)
+PIECES = ((0,), (1,))
 HALF = 128
 ORDER = ((0, 0), (0, 1), (1, 0), (3, 1), (2, 0), (1, 1), (2, 1), (3, 0))
 PEERS = ((False, False), (False, True), (True, False), (True, True))
@@ -190,26 +190,19 @@
         return lax.dot_general(flat, flat, (((1,), (1,)), ((), ())), preferred_element_type=F32)
 
     out0 = products(0, *sums)
-    first = reduce_first(out0)
-    early = reduce_last(early, out0[2])
-    early_other = early[1].astype(BF16)
-    sums, second0 = reduce_second(first)
-    out1 = products(1, *sums, early_other)
-    early_other = shift(early_other, dx=2)
+    first0 = reduce_first(out0)
+    out1 = products(1, out0[2], *early)
     first1 = reduce_first(out1)
-    out2 = products(2, out1[2])
-    first2 = reduce_first(out2)
-    sums, second1 = reduce_second(after(first1, out2[2]))
+    early = reduce_last(early, out1[2])
+    early_other = shift(early[1].astype(BF16), dx=2)
+    sums, second0 = reduce_second(after(first0, out1[2]))
+    sums, second1 = reduce_second(after(first1, *sums))
     center_early = centered(early[0] + after([early_other], *sums)[0].astype(F32), 0)
-    center0 = centered(reduce_last(second0, *sums)[0], starts[0])
-    slots = [spread(center_early, center0)]
-    sums, second2 = reduce_second(after(first2, center_early, center0))
-    center1 = centered(reduce_last(second1, *sums)[0], starts[1])
-    slots.append(spread(after([center1], slots[0])[0]))
-    gram_slots = partial_gram(slots[0])
-    center2 = centered(reduce_last(second2, center1, gram_slots, slots[1])[0], starts[2])
-    slots.append(spread(center2))
-    gram_slots = gram_slots + partial_gram(slots[1]) + partial_gram(slots[2])
+    slots = [spread(center_early)]
+    center0 = centered(reduce_last(second0, center_early)[0], starts[0])
+    center1 = centered(reduce_last(second1, center0)[0], starts[1])
+    slots.append(spread(after([center0], slots[0])[0], center1))
+    gram_slots = partial_gram(after([slots[0]], center1)[0]) + partial_gram(slots[1])
 
     labels = jnp.arange(8, dtype=jnp.int32)
     onehot = (domain_ids[:, None] == labels[None, :]).astype(F32)

time: 209 us -> 204 us (0.976)
  waiting for transfers between devices: 99.5 us -> 117 us
  blocking collectives: 14 us -> 0 us
  starting transfers between devices: 52.7 us -> 47.5 us
  matrix products: 3.51 us -> 5.95 us
    all_to_all x2, waiting for transfers between devices: 3.78 us -> 21.2 us  [spread(): return lax.all_to_all(pieces.reshape(8, 32, -1), 'dom', 0, 0, tiled=True)]
    all_to_all x1 -> x0, blocking collectives: 14 us -> none  [spread(): return lax.all_to_all(pieces.reshape(8, 32, -1), 'dom', 0, 0, tiled=True)]
    ppermute x24 -> x20, starting transfers between devices: 34 us -> 27.3 us  [shift(): return lax.ppermute(value, AXES, moves)]
    dot_general x3 -> x2, matrix products: 2.28 us -> 4.72 us  [partial_gram(): lax.dot_general(flat, flat, (((1,), (1,)), ((), ())), preferred_element_t...]
    pallas_call x4 -> x3, Pallas kernels: 15.6 us -> 13.9 us  [block_products(): pl.pallas_call(functools.partial(matmul_kernel, n, terms), grid=(width //...]
    ppermute x24 -> x20, waiting for transfers between devices: 60.2 us -> 60.1 us  [shift(): return lax.ppermute(value, AXES, moves)]
  transfers between devices with their start and end apart: 28 -> 24, of which waited for: 19 -> 13; matrix products, arithmetic and copies ran while one was open for 6% -> 6% of each run, Pallas kernels for 6% -> 5%
where the time goes in v3:
time: 204 us
  waiting for transfers between devices  117 us (57%)
  starting transfers between devices  47.5 us (23%)
  Pallas kernels  15.1 us (7%)
  other arithmetic  9.97 us (5%)
  local copies, waits for them, and re-layouts  7.32 us (4%)
  matrix products  5.95 us (3%)
    ppermute x20, waiting for transfers between devices, shift(): return lax.ppermute(value, AXES, moves)  60.1 us
    ppermute x20, starting transfers between devices, shift(): return lax.ppermute(value, AXES, moves)  27.3 us
    all_to_all x1, waiting for transfers between devices, per_device(): lax.all_to_all(jnp.broadcast_to(owned[None], (8, *owned.shape)), 'dom', 0...  26.2 us
    all_to_all x2, waiting for transfers between devices, spread(): return lax.all_to_all(pieces.reshape(8, 32, -1), 'dom', 0, 0, tiled=True)  21.2 us
    pallas_call x3, Pallas kernels, block_products(): pl.pallas_call(functools.partial(matmul_kernel, n, terms), grid=(width //...  13.9 us
    all_to_all x2, starting transfers between devices, spread(): return lax.all_to_all(pieces.reshape(8, 32, -1), 'dom', 0, 0, tiled=True)  9.86 us
    all_to_all x1, waiting for transfers between devices, per_device(): parts = lax.all_to_all(sent, AXES, 0, 0, tiled=True)  9.24 us
    all_to_all x1, starting transfers between devices, per_device(): parts = lax.all_to_all(sent, AXES, 0, 0, tiled=True)  6.74 us
  transfers between devices with their start and end apart: 24, of which 13 were waited for; matrix products, arithmetic and copies ran while one was open for 6% of the time, Pallas kernels for 5%

profile of v3, /device:TPU:0, one launch (start us, length us, event | category | flops | bytes accessed | tf_op | source)
XLA Modules:
  0.0 203.6 jit_solution(17516895735970856361)
XLA Ops:
  6.5 5.2 %shard_map.69 = (bf16[2,256,1536]{2,1,0:T(8,128)(2,1)S(1)}, bf16[2,256,1536]{2,1,0:T(8,128)(2,1)S(1)}, bf16[2,256,1536]{2,1,0:T(8,128)(2,1)S(1)}, bf16[2,256,1536]{2,1,0:T(8,128)(2,1)S(1)}) custom-call(bf16[256,1024]{1,0:T(8,128)(2,1)S(1)} %get-tuple-element.51.refs_0_, bf16[256,1024]{1,0:T(8,128)(2,1)S(1)} %collective-permute-done.refs_1_, ...), custom_call_target="tpu_custom_call" | custom-call | tf_op jit(solution)/shard_map/pallas_call | solution.py:96
  11.7 1.7 collective-permute-start.3
  15.1 3.2 %collective-permute-start.7 = (bf16[256,3072]{1,0:T(8,128)(2,1)S(1)}, bf16[256,3072]{1,0:T(8,128)(2,1)S(1)}, u32[]{:S(2)}, u32[]{:S(2)}) collective-permute-start(bf16[256,3072]{1,0:T(8,128)(2,1)S(1)} %pad_maximum_fusion.1), channel_id=1, source_target_pairs={{0,8},{1,9},{32,40},{33,41},{64,72},{65,73},{96,104},{97,105},{2,1... | collective-permute-start | bytes 4718600 | tf_op jit(solution)/shard_map/ppermute | solution.py:38
  18.9 30.8 %collective-permute-done.3 = bf16[2,256,1536]{2,1,0:T(8,128)(2,1)S(1)} collective-permute-done((bf16[2,256,1536]{2,1,0:T(8,128)(2,1)S(1)}, bf16[2,256,1536]{2,1,0:T(8,128)(2,1)S(1)}, u32[]{:S(2)}, u32[]{:S(2)}) %collective-permute-start.3) | collective-permute-done | bytes 1572896 | tf_op jit(solution)/shard_map/ppermute | solution.py:38
  54.1 1.9 collective-permute-done.9.refs_7_
  56.0 3.7 %shard_map.70 = (bf16[1,256,1024]{2,1,0:T(8,128)(2,1)S(1)}, bf16[1,256,1024]{2,1,0:T(8,128)(2,1)S(1)}, bf16[1,256,1024]{2,1,0:T(8,128)(2,1)S(1)}, bf16[1,256,1024]{2,1,0:T(8,128)(2,1)S(1)}) custom-call(bf16[256,1024]{1,0:T(8,128)(2,1)S(1)} %get-tuple-element.51.refs_0_, bf16[256,1024]{1,0:T(8,128)(2,1)S(1)} %collective-permute-done.refs_1_, ...), custom_call_target="tpu_custom_call" | custom-call | tf_op jit(solution)/shard_map/pallas_call | solution.py:96
  59.7 10.2 %collective-permute-done.8.refs_6_ = bf16[256,1536]{1,0:T(8,128)(2,1)S(1)} collective-permute-done((bf16[256,1536]{1,0:T(8,128)(2,1)S(1)}, bf16[256,1536]{1,0:T(8,128)(2,1)S(1)}, u32[]{:S(2)}, u32[]{:S(2)}) %collective-permute-start.8) | collective-permute-done | bytes 786464 | tf_op jit(solution)/shard_map/ppermute | solution.py:38
  71.5 2.3 %collective-permute-start.15 = (bf16[1,256,1024]{2,1,0:T(8,128)(2,1)S(1)}, bf16[1,256,1024]{2,1,0:T(8,128)(2,1)S(1)}, u32[]{:S(2)}, u32[]{:S(2)}) collective-permute-start(bf16[1,256,1024]{2,1,0:T(8,128)(2,1)S(1)} %get-tuple-element.78), channel_id=1, source_target_pairs={{0,6},{1,7},{32,38},{33,39},{64,70},{65,71},{96,102},{97,103},{2,0... | collective-permute-start | bytes 1572872 | tf_op jit(solution)/shard_map/ppermute | solution.py:38
  73.8 5.1 %shard_map.71 = (bf16[1,256,1536]{2,1,0:T(8,128)(2,1)S(1)}, bf16[1,256,1536]{2,1,0:T(8,128)(2,1)S(1)}, bf16[1,256,1536]{2,1,0:T(8,128)(2,1)S(1)}, bf16[1,256,1536]{2,1,0:T(8,128)(2,1)S(1)}) custom-call(bf16[256,1024]{1,0:T(8,128)(2,1)S(1)} %get-tuple-element.51.refs_0_, bf16[256,1024]{1,0:T(8,128)(2,1)S(1)} %collective-permute-done.refs_1_, ...), custom_call_target="tpu_custom_call" | custom-call | tf_op jit(solution)/shard_map/pallas_call | solution.py:96
  79.0 3.2 %collective-permute-start.13 = (bf16[1,256,1536]{2,1,0:T(8,128)(2,1)S(1)}, bf16[1,256,1536]{2,1,0:T(8,128)(2,1)S(1)}, u32[]{:S(2)}, u32[]{:S(2)}) collective-permute-start(bf16[1,256,1536]{2,1,0:T(8,128)(2,1)S(1)} %get-tuple-element.75), channel_id=1, source_target_pairs={{0,6},{1,7},{32,38},{33,39},{64,70},{65,71},{96,102},{97,103},{2,0... | collective-permute-start | bytes 2359304 | tf_op jit(solution)/shard_map/ppermute | solution.py:38
  82.9 3.0 %collective-permute-start.11 = (bf16[256,1536]{1,0:T(8,128)(2,1)S(1)}, bf16[256,1536]{1,0:T(8,128)(2,1)S(1)}, u32[]{:S(2)}, u32[]{:S(2)}) collective-permute-start(bf16[256,1536]{1,0:T(8,128)(2,1)S(1)} %fusion.19), channel_id=1, source_target_pairs={{0,8},{1,9},{32,40},{33,41},{64,72},{65,73},{96,104},{97,105},{2,1... | collective-permute-start | bytes 2359304 | tf_op jit(solution)/shard_map/ppermute | solution.py:38
  88.3 1.8 collective-permute-start.19
  90.1 13.2 %collective-permute-done.12 = bf16[1,256,1536]{2,1,0:T(8,128)(2,1)S(1)} collective-permute-done((bf16[1,256,1536]{2,1,0:T(8,128)(2,1)S(1)}, bf16[1,256,1536]{2,1,0:T(8,128)(2,1)S(1)}, u32[]{:S(2)}, u32[]{:S(2)}) %collective-permute-start.12) | collective-permute-done | bytes 786464 | tf_op jit(solution)/shard_map/ppermute | solution.py:38
  106.1 1.8 collective-permute-start.17
  107.9 2.3 %fusion.4 = bf16[256,1536]{1,0:T(8,128)(2,1)} fusion(f32[2,128,1536]{2,1,0:T(8,128)S(1)} %get-tuple-element.101, f32[2,128,1536]{2,1,0:T(8,128)S(1)} %get-tuple-element.100, bf16[256,1536]{1,0:T(8,128)(2,1)S(1)} %collective-permute-done.11, bf16[256,4096]{1,0:T(8,128)(2,1)} %bitcast.50), kind=kLoop, calls=%fused_computation.8 | loop fusion | flops 2359296 | bytes 5505024 | tf_op jit(solution)/shard_map/convert_element_type | solution.py:165
  110.2 6.3 %all-to-all-start = ((bf16[8,32,1536]{2,1,0:T(8,128)(2,1)}), bf16[8,32,1536]{2,1,0:T(8,128)(2,1)S(1)}, u32[]{:S(2)}, u32[]{:S(2)}) async-start(bf16[8,32,1536]{2,1,0:T(8,128)(2,1)} %bitcast.8), calls=%async_computation | async-start | bytes 1572864 | tf_op jit(solution)/shard_map/all_to_all | solution.py:169
  120.6 7.8 %all-to-all-done = bf16[8,32,1536]{2,1,0:T(8,128)(2,1)S(1)} async-done(((bf16[8,32,1536]{2,1,0:T(8,128)(2,1)}), bf16[8,32,1536]{2,1,0:T(8,128)(2,1)S(1)}, u32[]{:S(2)}, u32[]{:S(2)}) %all-to-all-start) | async-done | bytes 786464 | tf_op jit(solution)/shard_map/all_to_all | solution.py:169
  129.9 3.6 %all-to-all-start.1 = ((bf16[8,32,2560]{2,1,0:T(8,128)(2,1)}), bf16[8,32,2560]{2,1,0:T(8,128)(2,1)S(1)}, u32[]{:S(2)}, u32[]{:S(2)}) async-start(bf16[8,32,2560]{2,1,0:T(8,128)(2,1)} %bitcast.12), calls=%async_computation.1 | async-start | bytes 2621440 | tf_op jit(solution)/shard_map/all_to_all | solution.py:169
  133.4 3.1 %convolution_bitcast_fusion = f32[8,8]{1,0:T(8,128)S(1)} fusion(bf16[8,32,1536]{2,1,0:T(8,128)(2,1)} %copy-done.3), kind=kOutput, calls=%fused_computation.23 | convolution fusion | flops 6291456 | bytes 786688 | tf_op jit(solution)/shard_map/dot_general | solution.py:190
  136.5 13.4 %all-to-all-done.1 = bf16[8,32,2560]{2,1,0:T(8,128)(2,1)S(1)} async-done(((bf16[8,32,2560]{2,1,0:T(8,128)(2,1)}), bf16[8,32,2560]{2,1,0:T(8,128)(2,1)S(1)}, u32[]{:S(2)}, u32[]{:S(2)}) %all-to-all-start.1) | async-done | bytes 1310752 | tf_op jit(solution)/shard_map/all_to_all | solution.py:169
  152.3 6.7 %all-to-all-start.2 = ((f32[128,1,128]{2,1,0:T(1,128)}), f32[128,1,128]{2,1,0:T(1,128)S(1)}, u32[]{:S(2)}, u32[]{:S(2)}) async-start(f32[128,1,128]{2,1,0:T(1,128)} %broadcast_in_dim.11), calls=%async_computation.2 | async-start | bytes 131072 | tf_op jit(solution)/shard_map/all_to_all | solution.py:213
  159.1 9.2 %all-to-all-done.2 = f32[128,1,128]{2,1,0:T(1,128)S(1)} async-done(((f32[128,1,128]{2,1,0:T(1,128)}), f32[128,1,128]{2,1,0:T(1,128)S(1)}, u32[]{:S(2)}, u32[]{:S(2)}) %all-to-all-start.2) | async-done | bytes 65568 | tf_op jit(solution)/shard_map/all_to_all | solution.py:213
  171.4 3.6 %all-to-all-start.3 = ((bf16[8,32,4096]{2,1,0:T(8,128)(2,1)}), bf16[8,32,4096]{2,1,0:T(8,128)(2,1)S(1)}, u32[]{:S(2)}, u32[]{:S(2)}) async-start(bf16[8,32,4096]{2,1,0:T(8,128)(2,1)} %broadcast_in_dim.12), calls=%async_computation.3 | async-start | bytes 4194304 | tf_op jit(solution)/shard_map/all_to_all | solution.py:221
  176.1 26.2 %all-to-all-done.3 = bf16[8,32,4096]{2,1,0:T(8,128)(2,1)S(1)} async-done(((bf16[8,32,4096]{2,1,0:T(8,128)(2,1)}), bf16[8,32,4096]{2,1,0:T(8,128)(2,1)S(1)}, u32[]{:S(2)}, u32[]{:S(2)}) %all-to-all-start.3) | async-done | bytes 2097184 | tf_op jit(solution)/shard_map/all_to_all | solution.py:221
  (100 shorter events, 33.2 us)
Async XLA Ops:
  0.7 5.8 %collective-permute-start.2 = (bf16[256,4096]{1,0:T(8,128)(2,1)}, bf16[256,4096]{1,0:T(8,128)(2,1)}, u32[]{:S(2)}, u32[]{:S(2)}) collective-permute-start(bf16[256,4096]{1,0:T(8,128)(2,1)} %refs_4_.5), channel_id=1, source_target_pairs={{0,1},{1,0},{32,33},{33,32},{64,65},{65,64},{96,97},{97,96},{2,3},... | collective-permute-start | bytes 6291464 | tf_op jit(solution)/shard_map/ppermute | solution.py:38
  3.7 2.0 collective-permute-start
  4.2 2.3 %collective-permute-start.1 = (bf16[256,1024]{1,0:T(8,128)(2,1)S(1)}, bf16[256,1024]{1,0:T(8,128)(2,1)S(1)}, u32[]{:S(2)}, u32[]{:S(2)}) collective-permute-start(bf16[256,1024]{1,0:T(8,128)(2,1)S(1)} %get-tuple-element.54), channel_id=1, source_target_pairs={{0,1},{1,0},{32,33},{33,32},{64,65},{65,64},{96,97},{97,96},{2,3},... | collective-permute-start | bytes 1572872 | tf_op jit(solution)/shard_map/ppermute | solution.py:38
  11.7 38.1 %collective-permute-start.3 = (bf16[2,256,1536]{2,1,0:T(8,128)(2,1)S(1)}, bf16[2,256,1536]{2,1,0:T(8,128)(2,1)S(1)}, u32[]{:S(2)}, u32[]{:S(2)}) collective-permute-start(bf16[2,256,1536]{2,1,0:T(8,128)(2,1)S(1)} %get-tuple-element.56), channel_id=1, source_target_pairs={{0,2},{1,3},{32,34},{33,35},{64,66},{65,67},{96,98},{97,99},{2,4},... | collective-permute-start | bytes 4718600 | tf_op jit(solution)/shard_map/ppermute | solution.py:38
  13.4 36.4 %collective-permute-start.4 = (bf16[2,256,1536]{2,1,0:T(8,128)(2,1)S(1)}, bf16[2,256,1536]{2,1,0:T(8,128)(2,1)S(1)}, u32[]{:S(2)}, u32[]{:S(2)}) collective-permute-start(bf16[2,256,1536]{2,1,0:T(8,128)(2,1)S(1)} %get-tuple-element.57), channel_id=1, source_target_pairs={{0,6},{1,7},{32,38},{33,39},{64,70},{65,71},{96,102},{97,103},{2,0... | collective-permute-start | bytes 4718600 | tf_op jit(solution)/shard_map/ppermute | solution.py:38
  15.1 38.8 %collective-permute-start.7 = (bf16[256,3072]{1,0:T(8,128)(2,1)S(1)}, bf16[256,3072]{1,0:T(8,128)(2,1)S(1)}, u32[]{:S(2)}, u32[]{:S(2)}) collective-permute-start(bf16[256,3072]{1,0:T(8,128)(2,1)S(1)} %pad_maximum_fusion.1), channel_id=1, source_target_pairs={{0,8},{1,9},{32,40},{33,41},{64,72},{65,73},{96,104},{97,105},{2,1... | collective-permute-start | bytes 4718600 | tf_op jit(solution)/shard_map/ppermute | solution.py:38
  18.4 51.5 %collective-permute-start.8 = (bf16[256,1536]{1,0:T(8,128)(2,1)S(1)}, bf16[256,1536]{1,0:T(8,128)(2,1)S(1)}, u32[]{:S(2)}, u32[]{:S(2)}) collective-permute-start(bf16[256,1536]{1,0:T(8,128)(2,1)S(1)} %slice.115), channel_id=1, source_target_pairs={{0,8},{1,9},{32,40},{33,41},{64,72},{65,73},{96,104},{97,105},{2,1... | collective-permute-start | bytes 2359304 | tf_op jit(solution)/shard_map/ppermute | solution.py:38
  50.1 20.4 %collective-permute-start.5 = (bf16[2,128,1536]{2,1,0:T(8,128)(2,1)S(1)}, bf16[2,128,1536]{2,1,0:T(8,128)(2,1)S(1)}, u32[]{:S(2)}, u32[]{:S(2)}) collective-permute-start(bf16[2,128,1536]{2,1,0:T(8,128)(2,1)S(1)} %get-tuple-element.103), channel_id=1, source_target_pairs={{0,2},{1,3},{32,34},{33,35},{64,66},{65,67},{96,98},{97,99},{2,4},... | collective-permute-start | bytes 2359304 | tf_op jit(solution)/shard_map/ppermute | solution.py:38
  51.8 18.7 %collective-permute-start.6 = (bf16[2,128,1536]{2,1,0:T(8,128)(2,1)S(1)}, bf16[2,128,1536]{2,1,0:T(8,128)(2,1)S(1)}, u32[]{:S(2)}, u32[]{:S(2)}) collective-permute-start(bf16[2,128,1536]{2,1,0:T(8,128)(2,1)S(1)} %get-tuple-element.102), channel_id=1, source_target_pairs={{0,6},{1,7},{32,38},{33,39},{64,70},{65,71},{96,102},{97,103},{2,0... | collective-permute-start | bytes 2359304 | tf_op jit(solution)/shard_map/ppermute | solution.py:38
  54.0 2.0 collective-permute-start.9
  70.5 3.2 %collective-permute-start.10 = (bf16[256,1536]{1,0:T(8,128)(2,1)S(1)}, bf16[256,1536]{1,0:T(8,128)(2,1)S(1)}, u32[]{:S(2)}, u32[]{:S(2)}) collective-permute-start(bf16[256,1536]{1,0:T(8,128)(2,1)S(1)} %collective-permute-done.8.refs_6_), channel_id=1, source_target_pairs={{0,1},{1,0},{32,33},{33,32},{64,65},{65,64},{96,97},{97,96},{2,3},... | collective-permute-start | bytes 2359304 | tf_op jit(solution)/shard_map/ppermute | solution.py:38
  70.5 15.9 %collective-permute-start.14 = (bf16[1,256,1024]{2,1,0:T(8,128)(2,1)S(1)}, bf16[1,256,1024]{2,1,0:T(8,128)(2,1)S(1)}, u32[]{:S(2)}, u32[]{:S(2)}) collective-permute-start(bf16[1,256,1024]{2,1,0:T(8,128)(2,1)S(1)} %get-tuple-element.63), channel_id=1, source_target_pairs={{0,2},{1,3},{32,34},{33,35},{64,66},{65,67},{96,98},{97,99},{2,4},... | collective-permute-start | bytes 1572872 | tf_op jit(solution)/shard_map/ppermute | solution.py:38
  71.5 14.9 %collective-permute-start.15 = (bf16[1,256,1024]{2,1,0:T(8,128)(2,1)S(1)}, bf16[1,256,1024]{2,1,0:T(8,128)(2,1)S(1)}, u32[]{:S(2)}, u32[]{:S(2)}) collective-permute-start(bf16[1,256,1024]{2,1,0:T(8,128)(2,1)S(1)} %get-tuple-element.78), channel_id=1, source_target_pairs={{0,6},{1,7},{32,38},{33,39},{64,70},{65,71},{96,102},{97,103},{2,0... | collective-permute-start | bytes 1572872 | tf_op jit(solution)/shard_map/ppermute | solution.py:38
  78.9 24.5 %collective-permute-start.12 = (bf16[1,256,1536]{2,1,0:T(8,128)(2,1)S(1)}, bf16[1,256,1536]{2,1,0:T(8,128)(2,1)S(1)}, u32[]{:S(2)}, u32[]{:S(2)}) collective-permute-start(bf16[1,256,1536]{2,1,0:T(8,128)(2,1)S(1)} %get-tuple-element.67), channel_id=1, source_target_pairs={{0,2},{1,3},{32,34},{33,35},{64,66},{65,67},{96,98},{97,99},{2,4},... | collective-permute-start | bytes 2359304 | tf_op jit(solution)/shard_map/ppermute | solution.py:38
  79.0 24.4 %collective-permute-start.13 = (bf16[1,256,1536]{2,1,0:T(8,128)(2,1)S(1)}, bf16[1,256,1536]{2,1,0:T(8,128)(2,1)S(1)}, u32[]{:S(2)}, u32[]{:S(2)}) collective-permute-start(bf16[1,256,1536]{2,1,0:T(8,128)(2,1)S(1)} %get-tuple-element.75), channel_id=1, source_target_pairs={{0,6},{1,7},{32,38},{33,39},{64,70},{65,71},{96,102},{97,103},{2,0... | collective-permute-start | bytes 2359304 | tf_op jit(solution)/shard_map/ppermute | solution.py:38
  82.9 25.0 %collective-permute-start.11 = (bf16[256,1536]{1,0:T(8,128)(2,1)S(1)}, bf16[256,1536]{1,0:T(8,128)(2,1)S(1)}, u32[]{:S(2)}, u32[]{:S(2)}) collective-permute-start(bf16[256,1536]{1,0:T(8,128)(2,1)S(1)} %fusion.19), channel_id=1, source_target_pairs={{0,8},{1,9},{32,40},{33,41},{64,72},{65,73},{96,104},{97,105},{2,1... | collective-permute-start | bytes 2359304 | tf_op jit(solution)/shard_map/ppermute | solution.py:38
  86.7 23.5 %collective-permute-start.18 = (bf16[1,128,1024]{2,1,0:T(8,128)(2,1)S(1)}, bf16[1,128,1024]{2,1,0:T(8,128)(2,1)S(1)}, u32[]{:S(2)}, u32[]{:S(2)}) collective-permute-start(bf16[1,128,1024]{2,1,0:T(8,128)(2,1)S(1)} %get-tuple-element.111), channel_id=1, source_target_pairs={{0,2},{1,3},{32,34},{33,35},{64,66},{65,67},{96,98},{97,99},{2,4},... | collective-permute-start | bytes 786440 | tf_op jit(solution)/shard_map/ppermute | solution.py:38
  88.3 21.9 %collective-permute-start.19 = (bf16[1,128,1024]{2,1,0:T(8,128)(2,1)S(1)}, bf16[1,128,1024]{2,1,0:T(8,128)(2,1)}, u32[]{:S(2)}, u32[]{:S(2)}) collective-permute-start(bf16[1,128,1024]{2,1,0:T(8,128)(2,1)S(1)} %get-tuple-element.110), channel_id=1, source_target_pairs={{0,6},{1,7},{32,38},{33,39},{64,70},{65,71},{96,102},{97,103},{2,0... | collective-permute-start | bytes 786440 | tf_op jit(solution)/shard_map/ppermute | solution.py:38
  104.6 13.8 %collective-permute-start.16 = (bf16[1,128,1536]{2,1,0:T(8,128)(2,1)}, bf16[1,128,1536]{2,1,0:T(8,128)(2,1)}, u32[]{:S(2)}, u32[]{:S(2)}) collective-permute-start(bf16[1,128,1536]{2,1,0:T(8,128)(2,1)} %get-tuple-element.107), channel_id=1, source_target_pairs={{0,2},{1,3},{32,34},{33,35},{64,66},{65,67},{96,98},{97,99},{2,4},... | collective-permute-start | bytes 1179656 | tf_op jit(solution)/shard_map/ppermute | solution.py:38
  106.1 12.4 %collective-permute-start.17 = (bf16[1,128,1536]{2,1,0:T(8,128)(2,1)}, bf16[1,128,1536]{2,1,0:T(8,128)(2,1)}, u32[]{:S(2)}, u32[]{:S(2)}) collective-permute-start(bf16[1,128,1536]{2,1,0:T(8,128)(2,1)} %get-tuple-element.106), channel_id=1, source_target_pairs={{0,6},{1,7},{32,38},{33,39},{64,70},{65,71},{96,102},{97,103},{2,0... | collective-permute-start | bytes 1179656 | tf_op jit(solution)/shard_map/ppermute | solution.py:38
  110.2 18.2 %all-to-all-start = ((bf16[8,32,1536]{2,1,0:T(8,128)(2,1)}), bf16[8,32,1536]{2,1,0:T(8,128)(2,1)S(1)}, u32[]{:S(2)}, u32[]{:S(2)}) async-start(bf16[8,32,1536]{2,1,0:T(8,128)(2,1)} %bitcast.8), calls=%async_computation | async-start | bytes 1572864 | tf_op jit(solution)/shard_map/all_to_all | solution.py:169
  129.9 20.1 %all-to-all-start.1 = ((bf16[8,32,2560]{2,1,0:T(8,128)(2,1)}), bf16[8,32,2560]{2,1,0:T(8,128)(2,1)S(1)}, u32[]{:S(2)}, u32[]{:S(2)}) async-start(bf16[8,32,2560]{2,1,0:T(8,128)(2,1)} %bitcast.12), calls=%async_computation.1 | async-start | bytes 2621440 | tf_op jit(solution)/shard_map/all_to_all | solution.py:169
  152.3 16.0 %all-to-all-start.2 = ((f32[128,1,128]{2,1,0:T(1,128)}), f32[128,1,128]{2,1,0:T(1,128)S(1)}, u32[]{:S(2)}, u32[]{:S(2)}) async-start(f32[128,1,128]{2,1,0:T(1,128)} %broadcast_in_dim.11), calls=%async_computation.2 | async-start | bytes 131072 | tf_op jit(solution)/shard_map/all_to_all | solution.py:213
  171.4 30.9 %all-to-all-start.3 = ((bf16[8,32,4096]{2,1,0:T(8,128)(2,1)}), bf16[8,32,4096]{2,1,0:T(8,128)(2,1)S(1)}, u32[]{:S(2)}, u32[]{:S(2)}) async-start(bf16[8,32,4096]{2,1,0:T(8,128)(2,1)} %broadcast_in_dim.12), calls=%async_computation.3 | async-start | bytes 4194304 | tf_op jit(solution)/shard_map/all_to_all | solution.py:221
  (19 other events, 339.3 us)

commit v4 on v3

--- a/solution.py
+++ b/solution.py
@@ -112,6 +112,30 @@
     return out[0]
 
 
+def finish_kernel(offset, ready, own, from_back, from_next, back2, next2, weight, out):
+    before, width = ready.shape[1], own.shape[2]
+    out[:, pl.ds(0, before)] = ready[...]
+    for half, first, second in ((0, from_next, back2), (1, from_back, next2)):
+        rows = pl.ds(half * HALF, HALF)
+        total = own[0, rows, :].astype(F32) + second[0].astype(F32)
+        total += first[0, pl.ds(HALF, HALF), :].astype(F32)
+        scaled = total * weight[rows, pl.ds(offset, width)].astype(F32)
+        out[rows, pl.ds(before, width)] = scaled.astype(BF16)
+
+
+def finished(ready, second, weight, offset):
+    whole = pl.BlockSpec(memory_space=pltpu.VMEM)
+    width = ready.shape[1] + second[0].shape[2]
+    return pl.pallas_call(
+        functools.partial(finish_kernel, offset),
+        in_specs=[whole] * 7,
+        out_specs=whole,
+        out_shape=jax.ShapeDtypeStruct((2 * HALF, width), BF16),
+        compiler_params=pltpu.CompilerParams(vmem_limit_bytes=40 * 1024 * 1024),
+        cost_estimate=pl.CostEstimate(flops=0, bytes_accessed=0, transcendentals=0),
+    )(ready, *second, weight)
+
+
 def add(a, b):
     return (a.astype(F32) + b.astype(F32)).astype(BF16)
 
@@ -119,6 +143,7 @@
 def per_device(inputs, grads_out, domain_weight, domain_ids, mix_weights):
     dom = lax.axis_index("dom")
     shard = lax.axis_index("shard")
+    z, x_lo = dom // 2, dom % 2
     x_hi, y, core = shard // 8, (shard // 2) % 4, shard % 2
     count = D_IN * WIN
     hi = lax.Precision.HIGHEST
@@ -151,13 +176,13 @@
         own, keep, from_back, from_next = first
         sums = add(keep[:, :HALF], from_back[:, :HALF]), add(keep[:, HALF:], from_next[:, :HALF])
         return sums, (
-            own, from_back[:, HALF:], from_next[:, HALF:], shift(sums[0], dy=1), shift(sums[1], dy=-1),
+            own, from_back, from_next, shift(sums[0], dy=1), shift(sums[1], dy=-1),
         )
 
     def reduce_last(second, *done):
-        own, back_own, next_own, back2, next2 = after(second, *done)
-        top = own[:, :HALF].astype(F32) + back2.astype(F32) + next_own.astype(F32)
-        bottom = own[:, HALF:].astype(F32) + back_own.astype(F32) + next2.astype(F32)
+        own, from_back, from_next, back2, next2 = after(second, *done)
+        top = own[:, :HALF].astype(F32) + back2.astype(F32) + from_next[:, HALF:].astype(F32)
+        bottom = own[:, HALF:].astype(F32) + from_back[:, HALF:].astype(F32) + next2.astype(F32)
         return jnp.concatenate([top, bottom], axis=1)
 
     def centered(weff_grad, start):
@@ -170,11 +195,11 @@
 
     swapped = {}
 
-    def products(k, *done):
+    def products(k, *done, swap_after=()):
         p = next(p for p, piece in enumerate(PIECES) if k in piece)
         inner = starts[k] - spans[p][0]
         if p not in swapped:
-            (far,) = after([across[p]], *done)
+            (far,) = after([across[p]], *(swap_after or done))
             swapped[p] = shift(far if p else far[:, skip:], core=1)
         far, far_core = after([across[p], swapped[p]], *done)
         rights = [
@@ -191,18 +216,18 @@
 
     out0 = products(0, *sums)
     first0 = reduce_first(out0)
-    out1 = products(1, out0[2], *early)
+    out1 = products(1, out0[2], *early, swap_after=out0[2:3])
+    early = reduce_last(early, out0[2])
+    early_other = shift(early[1].astype(BF16), dx=2)
     first1 = reduce_first(out1)
-    early = reduce_last(early, out1[2])
-    early_other = shift(early[1].astype(BF16), dx=2)
     sums, second0 = reduce_second(after(first0, out1[2]))
-    sums, second1 = reduce_second(after(first1, *sums))
     center_early = centered(early[0] + after([early_other], *sums)[0].astype(F32), 0)
     slots = [spread(center_early)]
-    center0 = centered(reduce_last(second0, center_early)[0], starts[0])
-    center1 = centered(reduce_last(second1, center0)[0], starts[1])
-    slots.append(spread(after([center0], slots[0])[0], center1))
-    gram_slots = partial_gram(after([slots[0]], center1)[0]) + partial_gram(slots[1])
+    sums, second1 = reduce_second(after(first1, center_early))
+    center0 = centered(reduce_last(second0, *sums)[0], starts[0])
+    center = finished(center0, second1, weight, starts[1])
+    slots.append(spread(after([center], slots[0])[0]))
+    gram_slots = partial_gram(after([slots[0]], center)[0]) + partial_gram(slots[1])
 
     labels = jnp.arange(8, dtype=jnp.int32)
     onehot = (domain_ids[:, None] == labels[None, :]).astype(F32)
@@ -218,9 +243,19 @@
         return jnp.sum(scale[:, None, None] * slots.astype(F32), axis=0).astype(BF16)
 
     owned = jnp.concatenate([mixed(received) for received in slots], axis=1)
-    combined = lax.all_to_all(jnp.broadcast_to(owned[None], (8, *owned.shape)), "dom", 0, 0, tiled=True)
+    left, right = jnp.split(owned, 2, axis=1)
+    left = jnp.stack([left, shift(left, pair=1)])
+    right = jnp.stack([right] + [shift(right, dz=n) for n in (1, 2, 3)])
+    right = jnp.stack([right, shift(right, pair=1)], axis=1)
+    left = jnp.stack([left] + [shift(left, dz=n) for n in (1, 2, 3)])
+    pieces = jnp.concatenate([left, right], axis=3)
+    combined = jnp.zeros((2 * HALF, WIN), BF16)
+    for n in range(4):
+        for b in range(2):
+            row = (((z - n) % 4) * 2 + (x_lo ^ b)) * 32
+            combined = lax.dynamic_update_slice(combined, pieces[n, b], (row, 0))
     gram = jnp.dot(jnp.dot(onehot.T, group_gram, precision=hi), onehot, precision=hi)
-    return (combined.reshape(-1, WIN), gram)
+    return (combined, gram)
 
 
 def solution(mesh):

time: 204 us -> 194 us (0.951)
  waiting for transfers between devices: 117 us -> 100 us
  starting transfers between devices: 47.5 us -> 53.9 us
  Pallas kernels: 15.1 us -> 17.5 us
  local copies, waits for them, and re-layouts: 7.32 us -> 5.09 us
    all_to_all x1 -> x0, waiting for transfers between devices: 26.2 us -> none  [per_device(): lax.all_to_all(jnp.broadcast_to(owned[None], (8, *owned.shape)), 'dom', 0...]
    ppermute x20 -> x28, waiting for transfers between devices: 60.1 us -> 77.2 us  [shift(): return lax.ppermute(value, AXES, moves)]
    ppermute x20 -> x28, starting transfers between devices: 27.3 us -> 36.3 us  [shift(): return lax.ppermute(value, AXES, moves)]
    all_to_all x2, waiting for transfers between devices: 21.2 us -> 13.5 us  [spread(): return lax.all_to_all(pieces.reshape(8, 32, -1), 'dom', 0, 0, tiled=True)]
    all_to_all x1 -> x0, starting transfers between devices: 3.6 us -> none  [per_device(): lax.all_to_all(jnp.broadcast_to(owned[None], (8, *owned.shape)), 'dom', 0...]
  transfers between devices with their start and end apart: 24 -> 31, of which waited for: 13 -> 17; matrix products, arithmetic and copies ran while one was open for 6% -> 6% of each run, Pallas kernels for 5% -> 6%
where the time goes in v4:
time: 194 us; the launch traced here: 193 us
  waiting for transfers between devices  100 us (52%)
  starting transfers between devices  53.9 us (28%)
  Pallas kernels  17.5 us (9%)
  other arithmetic  9.77 us (5%)
  matrix products  5.97 us (3%)
  local copies, waits for them, and re-layouts  5.09 us (3%)
    ppermute x28, waiting for transfers between devices, shift(): return lax.ppermute(value, AXES, moves)  77.2 us
    ppermute x28, starting transfers between devices, shift(): return lax.ppermute(value, AXES, moves)  36.3 us
    pallas_call x3, Pallas kernels, block_products(): pl.pallas_call(functools.partial(matmul_kernel, n, terms), grid=(width //...  14.9 us
    all_to_all x2, waiting for transfers between devices, spread(): return lax.all_to_all(pieces.reshape(8, 32, -1), 'dom', 0, 0, tiled=True)  13.5 us
    all_to_all x2, starting transfers between devices, spread(): return lax.all_to_all(pieces.reshape(8, 32, -1), 'dom', 0, 0, tiled=True)  10.7 us
    all_to_all x1, waiting for transfers between devices, per_device(): parts = lax.all_to_all(sent, AXES, 0, 0, tiled=True)  9.24 us
    all_to_all x1, starting transfers between devices, per_device(): parts = lax.all_to_all(sent, AXES, 0, 0, tiled=True)  6.91 us
    dot_general x2, matrix products, partial_gram(): lax.dot_general(flat, flat, (((1,), (1,)), ((), ())), preferred_element_t...  4.74 us
  transfers between devices with their start and end apart: 31, of which 17 were waited for; matrix products, arithmetic and copies ran while one was open for 6% of the time, Pallas kernels for 6%

profile of v4, /device:TPU:0, one launch (start us, length us, event | category | flops | bytes accessed | tf_op | source)
XLA Modules:
  0.0 193.2 jit_solution(14701473382141312856)
XLA Ops:
  6.5 5.3 %shard_map.69 = (bf16[2,256,1536]{2,1,0:T(8,128)(2,1)S(1)}, bf16[2,256,1536]{2,1,0:T(8,128)(2,1)S(1)}, bf16[2,256,1536]{2,1,0:T(8,128)(2,1)S(1)}, bf16[2,256,1536]{2,1,0:T(8,128)(2,1)S(1)}) custom-call(bf16[256,1024]{1,0:T(8,128)(2,1)S(1)} %get-tuple-element.46.refs_0_, bf16[256,1024]{1,0:T(8,128)(2,1)S(1)} %collective-permute-done.refs_1_, ...), custom_call_target="tpu_custom_call" | custom-call | tf_op jit(solution)/shard_map/pallas_call | solution.py:96
  15.3 3.2 %collective-permute-start.7 = (bf16[256,3072]{1,0:T(8,128)(2,1)S(1)}, bf16[256,3072]{1,0:T(8,128)(2,1)S(1)}, u32[]{:S(2)}, u32[]{:S(2)}) collective-permute-start(bf16[256,3072]{1,0:T(8,128)(2,1)S(1)} %pad_maximum_fusion.1), channel_id=1, source_target_pairs={{0,8},{1,9},{32,40},{33,41},{64,72},{65,73},{96,104},{97,105},{2,1... | collective-permute-start | bytes 4718600 | tf_op jit(solution)/shard_map/ppermute | solution.py:38
  19.0 30.8 %collective-permute-done.3 = bf16[2,256,1536]{2,1,0:T(8,128)(2,1)S(1)} collective-permute-done((bf16[2,256,1536]{2,1,0:T(8,128)(2,1)S(1)}, bf16[2,256,1536]{2,1,0:T(8,128)(2,1)S(1)}, u32[]{:S(2)}, u32[]{:S(2)}) %collective-permute-start.3) | collective-permute-done | bytes 1572896 | tf_op jit(solution)/shard_map/ppermute | solution.py:38
  54.3 1.9 collective-permute-done.8.refs_7_
  56.2 3.7 %shard_map.70 = (bf16[1,256,1024]{2,1,0:T(8,128)(2,1)S(1)}, bf16[1,256,1024]{2,1,0:T(8,128)(2,1)S(1)}, bf16[1,256,1024]{2,1,0:T(8,128)(2,1)S(1)}, bf16[1,256,1024]{2,1,0:T(8,128)(2,1)S(1)}) custom-call(bf16[256,1024]{1,0:T(8,128)(2,1)S(1)} %get-tuple-element.46.refs_0_, bf16[256,1024]{1,0:T(8,128)(2,1)S(1)} %collective-permute-done.refs_1_, ...), custom_call_target="tpu_custom_call" | custom-call | tf_op jit(solution)/shard_map/pallas_call | solution.py:96
  59.9 10.1 %collective-permute-done.12.refs_6_ = bf16[256,1536]{1,0:T(8,128)(2,1)S(1)} collective-permute-done((bf16[256,1536]{1,0:T(8,128)(2,1)S(1)}, bf16[256,1536]{1,0:T(8,128)(2,1)S(1)}, u32[]{:S(2)}, u32[]{:S(2)}) %collective-permute-start.12) | collective-permute-done | bytes 786464 | tf_op jit(solution)/shard_map/ppermute | solution.py:38
  71.4 3.0 %collective-permute-start.9 = (bf16[256,1536]{1,0:T(8,128)(2,1)S(1)}, bf16[256,1536]{1,0:T(8,128)(2,1)S(1)}, u32[]{:S(2)}, u32[]{:S(2)}) collective-permute-start(bf16[256,1536]{1,0:T(8,128)(2,1)S(1)} %fusion.17), channel_id=1, source_target_pairs={{0,8},{1,9},{32,40},{33,41},{64,72},{65,73},{96,104},{97,105},{2,1... | collective-permute-start | bytes 2359304 | tf_op jit(solution)/shard_map/ppermute | solution.py:38
  75.4 2.2 %collective-permute-start.11 = (bf16[1,256,1024]{2,1,0:T(8,128)(2,1)S(1)}, bf16[1,256,1024]{2,1,0:T(8,128)(2,1)S(1)}, u32[]{:S(2)}, u32[]{:S(2)}) collective-permute-start(bf16[1,256,1024]{2,1,0:T(8,128)(2,1)S(1)} %get-tuple-element.65), channel_id=1, source_target_pairs={{0,6},{1,7},{32,38},{33,39},{64,70},{65,71},{96,102},{97,103},{2,0... | collective-permute-start | bytes 1572872 | tf_op jit(solution)/shard_map/ppermute | solution.py:38
  77.7 5.8 %shard_map.71 = (bf16[1,256,1536]{2,1,0:T(8,128)(2,1)S(1)}, bf16[1,256,1536]{2,1,0:T(8,128)(2,1)S(1)}, bf16[1,256,1536]{2,1,0:T(8,128)(2,1)}, bf16[1,256,1536]{2,1,0:T(8,128)(2,1)}) custom-call(bf16[256,1024]{1,0:T(8,128)(2,1)S(1)} %get-tuple-element.46.refs_0_, bf16[256,1024]{1,0:T(8,128)(2,1)S(1)} %collective-permute-done.refs_1_, ...), custom_call_target="tpu_custom_call" | custom-call | tf_op jit(solution)/shard_map/pallas_call | solution.py:96
  83.5 3.2 %collective-permute-start.17 = (bf16[1,256,1536]{2,1,0:T(8,128)(2,1)}, bf16[1,256,1536]{2,1,0:T(8,128)(2,1)S(1)}, u32[]{:S(2)}, u32[]{:S(2)}) collective-permute-start(bf16[1,256,1536]{2,1,0:T(8,128)(2,1)} %get-tuple-element.78), channel_id=1, source_target_pairs={{0,6},{1,7},{32,38},{33,39},{64,70},{65,71},{96,102},{97,103},{2,0... | collective-permute-start | bytes 2359304 | tf_op jit(solution)/shard_map/ppermute | solution.py:38
  86.7 3.8 %collective-permute-done.10 = bf16[1,256,1024]{2,1,0:T(8,128)(2,1)S(1)} collective-permute-done((bf16[1,256,1024]{2,1,0:T(8,128)(2,1)S(1)}, bf16[1,256,1024]{2,1,0:T(8,128)(2,1)S(1)}, u32[]{:S(2)}, u32[]{:S(2)}) %collective-permute-start.10) | collective-permute-done | bytes 524320 | tf_op jit(solution)/shard_map/ppermute | solution.py:38
  94.9 2.3 %fusion.4 = bf16[256,1536]{1,0:T(8,128)(2,1)} fusion(f32[2,128,1536]{2,1,0:T(8,128)S(1)} %get-tuple-element.91, f32[2,128,1536]{2,1,0:T(8,128)S(1)} %get-tuple-element.90, bf16[256,1536]{1,0:T(8,128)(2,1)S(1)} %collective-permute-done.9, bf16[256,4096]{1,0:T(8,128)(2,1)} %bitcast.91), kind=kLoop, calls=%fused_computation.9 | loop fusion | flops 2359296 | bytes 5505024 | tf_op jit(solution)/shard_map/convert_element_type | solution.py:190
  97.3 5.4 %all-to-all-start = ((bf16[8,32,1536]{2,1,0:T(8,128)(2,1)}), bf16[8,32,1536]{2,1,0:T(8,128)(2,1)}, u32[]{:S(2)}, u32[]{:S(2)}) async-start(bf16[8,32,1536]{2,1,0:T(8,128)(2,1)} %bitcast.94), calls=%async_computation | async-start | bytes 1572864 | tf_op jit(solution)/shard_map/all_to_all | solution.py:194
  102.6 4.7 %collective-permute-done.16.from_back = bf16[1,256,1536]{2,1,0:T(8,128)(2,1)S(1)} collective-permute-done((bf16[1,256,1536]{2,1,0:T(8,128)(2,1)}, bf16[1,256,1536]{2,1,0:T(8,128)(2,1)S(1)}, u32[]{:S(2)}, u32[]{:S(2)}) %collective-permute-start.16) | collective-permute-done | bytes 786464 | tf_op jit(solution)/shard_map/ppermute | solution.py:38
  114.5 5.5 %collective-permute-done.18.back2 = bf16[1,128,1536]{2,1,0:T(8,128)(2,1)S(1)} collective-permute-done((bf16[1,128,1536]{2,1,0:T(8,128)(2,1)S(1)}, bf16[1,128,1536]{2,1,0:T(8,128)(2,1)S(1)}, u32[]{:S(2)}, u32[]{:S(2)}) %collective-permute-start.18) | collective-permute-done | bytes 393248 | tf_op jit(solution)/shard_map/ppermute | solution.py:38
  121.5 5.3 %all-to-all-start.1 = ((bf16[8,32,2560]{2,1,0:T(8,128)(2,1)}), bf16[8,32,2560]{2,1,0:T(8,128)(2,1)S(1)}, u32[]{:S(2)}, u32[]{:S(2)}) async-start(bf16[8,32,2560]{2,1,0:T(8,128)(2,1)} %bitcast.11), calls=%async_computation.1 | async-start | bytes 2621440 | tf_op jit(solution)/shard_map/all_to_all | solution.py:194
  126.8 3.1 %convolution_bitcast_fusion = f32[8,8]{1,0:T(8,128)S(1)} fusion(bf16[8,32,1536]{2,1,0:T(8,128)(2,1)} %all-to-all-done), kind=kOutput, calls=%fused_computation.20 | convolution fusion | flops 6291456 | bytes 786688 | tf_op jit(solution)/shard_map/dot_general | solution.py:215
  129.9 13.5 %all-to-all-done.1 = bf16[8,32,2560]{2,1,0:T(8,128)(2,1)S(1)} async-done(((bf16[8,32,2560]{2,1,0:T(8,128)(2,1)}), bf16[8,32,2560]{2,1,0:T(8,128)(2,1)S(1)}, u32[]{:S(2)}, u32[]{:S(2)}) %all-to-all-start.1) | async-done | bytes 1310752 | tf_op jit(solution)/shard_map/all_to_all | solution.py:194
  145.8 6.9 %all-to-all-start.2 = ((f32[128,1,128]{2,1,0:T(1,128)}), f32[128,1,128]{2,1,0:T(1,128)S(1)}, u32[]{:S(2)}, u32[]{:S(2)}) async-start(f32[128,1,128]{2,1,0:T(1,128)} %broadcast_in_dim.20), calls=%async_computation.2 | async-start | bytes 131072 | tf_op jit(solution)/shard_map/all_to_all | solution.py:238
  152.7 9.2 %all-to-all-done.2 = f32[128,1,128]{2,1,0:T(1,128)S(1)} async-done(((f32[128,1,128]{2,1,0:T(1,128)}), f32[128,1,128]{2,1,0:T(1,128)S(1)}, u32[]{:S(2)}, u32[]{:S(2)}) %all-to-all-start.2) | async-done | bytes 65568 | tf_op jit(solution)/shard_map/all_to_all | solution.py:238
  168.9 5.1 %collective-permute-done.24 = bf16[32,2048]{1,0:T(8,128)(2,1)S(1)} collective-permute-done((bf16[32,2048]{1,0:T(8,128)(2,1)S(1)}, bf16[32,2048]{1,0:T(8,128)(2,1)S(1)}, u32[]{:S(2)}, u32[]{:S(2)}) %collective-permute-start.24) | collective-permute-done | bytes 131104 | tf_op jit(solution)/shard_map/ppermute | solution.py:38
  176.1 3.5 %collective-permute-start.22 = (bf16[2,32,2048]{2,1,0:T(8,128)(2,1)S(1)}, bf16[2,32,2048]{2,1,0:T(8,128)(2,1)S(1)}, u32[]{:S(2)}, u32[]{:S(2)}) collective-permute-start(bf16[2,32,2048]{2,1,0:T(8,128)(2,1)S(1)} %get-tuple-element.103), channel_id=1, source_target_pairs={{0,64},{1,65},{32,96},{33,97},{64,0},{65,1},{96,32},{97,33},{2,66}... | collective-permute-start | bytes 786440 | tf_op jit(solution)/shard_map/ppermute | solution.py:38
  180.7 3.8 %collective-permute-done.21 = bf16[2,32,2048]{2,1,0:T(8,128)(2,1)S(1)} collective-permute-done((bf16[2,32,2048]{2,1,0:T(8,128)(2,1)S(1)}, bf16[2,32,2048]{2,1,0:T(8,128)(2,1)S(1)}, u32[]{:S(2)}, u32[]{:S(2)}) %collective-permute-start.21) | collective-permute-done | bytes 262176 | tf_op jit(solution)/shard_map/ppermute | solution.py:38
  184.5 6.7 %collective-permute-done.22 = bf16[2,32,2048]{2,1,0:T(8,128)(2,1)S(1)} collective-permute-done((bf16[2,32,2048]{2,1,0:T(8,128)(2,1)S(1)}, bf16[2,32,2048]{2,1,0:T(8,128)(2,1)S(1)}, u32[]{:S(2)}, u32[]{:S(2)}) %collective-permute-start.22) | collective-permute-done | bytes 262176 | tf_op jit(solution)/shard_map/ppermute | solution.py:38
  (106 shorter events, 43.9 us)
Async XLA Ops:
  11.8 38.1 %collective-permute-start.3 = (bf16[2,256,1536]{2,1,0:T(8,128)(2,1)S(1)}, bf16[2,256,1536]{2,1,0:T(8,128)(2,1)S(1)}, u32[]{:S(2)}, u32[]{:S(2)}) collective-permute-start(bf16[2,256,1536]{2,1,0:T(8,128)(2,1)S(1)} %get-tuple-element.51), channel_id=1, source_target_pairs={{0,2},{1,3},{32,34},{33,35},{64,66},{65,67},{96,98},{97,99},{2,4},... | collective-permute-start | bytes 4718600 | tf_op jit(solution)/shard_map/ppermute | solution.py:38
  13.6 36.4 %collective-permute-start.4 = (bf16[2,256,1536]{2,1,0:T(8,128)(2,1)S(1)}, bf16[2,256,1536]{2,1,0:T(8,128)(2,1)S(1)}, u32[]{:S(2)}, u32[]{:S(2)}) collective-permute-start(bf16[2,256,1536]{2,1,0:T(8,128)(2,1)S(1)} %get-tuple-element.52), channel_id=1, source_target_pairs={{0,6},{1,7},{32,38},{33,39},{64,70},{65,71},{96,102},{97,103},{2,0... | collective-permute-start | bytes 4718600 | tf_op jit(solution)/shard_map/ppermute | solution.py:38
  15.3 38.8 %collective-permute-start.7 = (bf16[256,3072]{1,0:T(8,128)(2,1)S(1)}, bf16[256,3072]{1,0:T(8,128)(2,1)S(1)}, u32[]{:S(2)}, u32[]{:S(2)}) collective-permute-start(bf16[256,3072]{1,0:T(8,128)(2,1)S(1)} %pad_maximum_fusion.1), channel_id=1, source_target_pairs={{0,8},{1,9},{32,40},{33,41},{64,72},{65,73},{96,104},{97,105},{2,1... | collective-permute-start | bytes 4718600 | tf_op jit(solution)/shard_map/ppermute | solution.py:38
  18.5 51.5 %collective-permute-start.12 = (bf16[256,1536]{1,0:T(8,128)(2,1)S(1)}, bf16[256,1536]{1,0:T(8,128)(2,1)S(1)}, u32[]{:S(2)}, u32[]{:S(2)}) collective-permute-start(bf16[256,1536]{1,0:T(8,128)(2,1)S(1)} %slice.129), channel_id=1, source_target_pairs={{0,8},{1,9},{32,40},{33,41},{64,72},{65,73},{96,104},{97,105},{2,1... | collective-permute-start | bytes 2359304 | tf_op jit(solution)/shard_map/ppermute | solution.py:38
  50.3 20.4 %collective-permute-start.5 = (bf16[2,128,1536]{2,1,0:T(8,128)(2,1)S(1)}, bf16[2,128,1536]{2,1,0:T(8,128)(2,1)S(1)}, u32[]{:S(2)}, u32[]{:S(2)}) collective-permute-start(bf16[2,128,1536]{2,1,0:T(8,128)(2,1)S(1)} %get-tuple-element.93), channel_id=1, source_target_pairs={{0,2},{1,3},{32,34},{33,35},{64,66},{65,67},{96,98},{97,99},{2,4},... | collective-permute-start | bytes 2359304 | tf_op jit(solution)/shard_map/ppermute | solution.py:38
  52.0 18.7 %collective-permute-start.6 = (bf16[2,128,1536]{2,1,0:T(8,128)(2,1)S(1)}, bf16[2,128,1536]{2,1,0:T(8,128)(2,1)S(1)}, u32[]{:S(2)}, u32[]{:S(2)}) collective-permute-start(bf16[2,128,1536]{2,1,0:T(8,128)(2,1)S(1)} %get-tuple-element.92), channel_id=1, source_target_pairs={{0,6},{1,7},{32,38},{33,39},{64,70},{65,71},{96,102},{97,103},{2,0... | collective-permute-start | bytes 2359304 | tf_op jit(solution)/shard_map/ppermute | solution.py:38
  71.4 23.5 %collective-permute-start.9 = (bf16[256,1536]{1,0:T(8,128)(2,1)S(1)}, bf16[256,1536]{1,0:T(8,128)(2,1)S(1)}, u32[]{:S(2)}, u32[]{:S(2)}) collective-permute-start(bf16[256,1536]{1,0:T(8,128)(2,1)S(1)} %fusion.17), channel_id=1, source_target_pairs={{0,8},{1,9},{32,40},{33,41},{64,72},{65,73},{96,104},{97,105},{2,1... | collective-permute-start | bytes 2359304 | tf_op jit(solution)/shard_map/ppermute | solution.py:38
  74.4 16.1 %collective-permute-start.10 = (bf16[1,256,1024]{2,1,0:T(8,128)(2,1)S(1)}, bf16[1,256,1024]{2,1,0:T(8,128)(2,1)S(1)}, u32[]{:S(2)}, u32[]{:S(2)}) collective-permute-start(bf16[1,256,1024]{2,1,0:T(8,128)(2,1)S(1)} %get-tuple-element.57), channel_id=1, source_target_pairs={{0,2},{1,3},{32,34},{33,35},{64,66},{65,67},{96,98},{97,99},{2,4},... | collective-permute-start | bytes 1572872 | tf_op jit(solution)/shard_map/ppermute | solution.py:38
  75.4 15.1 %collective-permute-start.11 = (bf16[1,256,1024]{2,1,0:T(8,128)(2,1)S(1)}, bf16[1,256,1024]{2,1,0:T(8,128)(2,1)S(1)}, u32[]{:S(2)}, u32[]{:S(2)}) collective-permute-start(bf16[1,256,1024]{2,1,0:T(8,128)(2,1)S(1)} %get-tuple-element.65), channel_id=1, source_target_pairs={{0,6},{1,7},{32,38},{33,39},{64,70},{65,71},{96,102},{97,103},{2,0... | collective-permute-start | bytes 1572872 | tf_op jit(solution)/shard_map/ppermute | solution.py:38
  83.5 23.9 %collective-permute-start.16 = (bf16[1,256,1536]{2,1,0:T(8,128)(2,1)}, bf16[1,256,1536]{2,1,0:T(8,128)(2,1)S(1)}, u32[]{:S(2)}, u32[]{:S(2)}) collective-permute-start(bf16[1,256,1536]{2,1,0:T(8,128)(2,1)} %get-tuple-element.70), channel_id=1, source_target_pairs={{0,2},{1,3},{32,34},{33,35},{64,66},{65,67},{96,98},{97,99},{2,4},... | collective-permute-start | bytes 2359304 | tf_op jit(solution)/shard_map/ppermute | solution.py:38
  83.5 23.9 %collective-permute-start.17 = (bf16[1,256,1536]{2,1,0:T(8,128)(2,1)}, bf16[1,256,1536]{2,1,0:T(8,128)(2,1)S(1)}, u32[]{:S(2)}, u32[]{:S(2)}) collective-permute-start(bf16[1,256,1536]{2,1,0:T(8,128)(2,1)} %get-tuple-element.78), channel_id=1, source_target_pairs={{0,6},{1,7},{32,38},{33,39},{64,70},{65,71},{96,102},{97,103},{2,0... | collective-permute-start | bytes 2359304 | tf_op jit(solution)/shard_map/ppermute | solution.py:38
  91.7 21.4 %collective-permute-start.14 = (bf16[1,128,1024]{2,1,0:T(8,128)(2,1)}, bf16[1,128,1024]{2,1,0:T(8,128)(2,1)}, u32[]{:S(2)}, u32[]{:S(2)}) collective-permute-start(bf16[1,128,1024]{2,1,0:T(8,128)(2,1)} %get-tuple-element.101), channel_id=1, source_target_pairs={{0,2},{1,3},{32,34},{33,35},{64,66},{65,67},{96,98},{97,99},{2,4},... | collective-permute-start | bytes 786440 | tf_op jit(solution)/shard_map/ppermute | solution.py:38
  93.0 20.0 %collective-permute-start.15 = (bf16[1,128,1024]{2,1,0:T(8,128)(2,1)}, bf16[1,128,1024]{2,1,0:T(8,128)(2,1)}, u32[]{:S(2)}, u32[]{:S(2)}) collective-permute-start(bf16[1,128,1024]{2,1,0:T(8,128)(2,1)} %get-tuple-element.100), channel_id=1, source_target_pairs={{0,6},{1,7},{32,38},{33,39},{64,70},{65,71},{96,102},{97,103},{2,0... | collective-permute-start | bytes 786440 | tf_op jit(solution)/shard_map/ppermute | solution.py:38
  97.3 24.2 %all-to-all-start = ((bf16[8,32,1536]{2,1,0:T(8,128)(2,1)}), bf16[8,32,1536]{2,1,0:T(8,128)(2,1)}, u32[]{:S(2)}, u32[]{:S(2)}) async-start(bf16[8,32,1536]{2,1,0:T(8,128)(2,1)} %bitcast.94), calls=%async_computation | async-start | bytes 1572864 | tf_op jit(solution)/shard_map/all_to_all | solution.py:194
  108.8 11.1 %collective-permute-start.18 = (bf16[1,128,1536]{2,1,0:T(8,128)(2,1)S(1)}, bf16[1,128,1536]{2,1,0:T(8,128)(2,1)S(1)}, u32[]{:S(2)}, u32[]{:S(2)}) collective-permute-start(bf16[1,128,1536]{2,1,0:T(8,128)(2,1)S(1)} %get-tuple-element.95), channel_id=1, source_target_pairs={{0,2},{1,3},{32,34},{33,35},{64,66},{65,67},{96,98},{97,99},{2,4},... | collective-permute-start | bytes 1179656 | tf_op jit(solution)/shard_map/ppermute | solution.py:38
  110.4 9.5 %collective-permute-start.19 = (bf16[1,128,1536]{2,1,0:T(8,128)(2,1)S(1)}, bf16[1,128,1536]{2,1,0:T(8,128)(2,1)S(1)}, u32[]{:S(2)}, u32[]{:S(2)}) collective-permute-start(bf16[1,128,1536]{2,1,0:T(8,128)(2,1)S(1)} %get-tuple-element.94), channel_id=1, source_target_pairs={{0,6},{1,7},{32,38},{33,39},{64,70},{65,71},{96,102},{97,103},{2,0... | collective-permute-start | bytes 1179656 | tf_op jit(solution)/shard_map/ppermute | solution.py:38
  121.5 22.0 %all-to-all-start.1 = ((bf16[8,32,2560]{2,1,0:T(8,128)(2,1)}), bf16[8,32,2560]{2,1,0:T(8,128)(2,1)S(1)}, u32[]{:S(2)}, u32[]{:S(2)}) async-start(bf16[8,32,2560]{2,1,0:T(8,128)(2,1)} %bitcast.11), calls=%async_computation.1 | async-start | bytes 2621440 | tf_op jit(solution)/shard_map/all_to_all | solution.py:194
  145.8 16.2 %all-to-all-start.2 = ((f32[128,1,128]{2,1,0:T(1,128)}), f32[128,1,128]{2,1,0:T(1,128)S(1)}, u32[]{:S(2)}, u32[]{:S(2)}) async-start(f32[128,1,128]{2,1,0:T(1,128)} %broadcast_in_dim.20), calls=%async_computation.2 | async-start | bytes 131072 | tf_op jit(solution)/shard_map/all_to_all | solution.py:238
  164.7 9.4 %collective-permute-start.24 = (bf16[32,2048]{1,0:T(8,128)(2,1)S(1)}, bf16[32,2048]{1,0:T(8,128)(2,1)S(1)}, u32[]{:S(2)}, u32[]{:S(2)}) collective-permute-start(bf16[32,2048]{1,0:T(8,128)(2,1)S(1)} %get-tuple-element.105), channel_id=1, source_target_pairs={{0,32},{1,33},{32,64},{33,65},{64,96},{65,97},{96,0},{97,1},{2,34}... | collective-permute-start | bytes 393224 | tf_op jit(solution)/shard_map/ppermute | solution.py:38
  165.6 8.5 %collective-permute-start.25 = (bf16[32,2048]{1,0:T(8,128)(2,1)S(1)}, bf16[32,2048]{1,0:T(8,128)(2,1)S(1)}, u32[]{:S(2)}, u32[]{:S(2)}) collective-permute-start(bf16[32,2048]{1,0:T(8,128)(2,1)S(1)} %get-tuple-element.105), channel_id=1, source_target_pairs={{0,64},{1,65},{32,96},{33,97},{64,0},{65,1},{96,32},{97,33},{2,66}... | collective-permute-start | bytes 393224 | tf_op jit(solution)/shard_map/ppermute | solution.py:38
  174.7 16.5 %collective-permute-start.27 = (bf16[4,32,2048]{2,1,0:T(8,128)(2,1)S(1)}, bf16[4,32,2048]{2,1,0:T(8,128)(2,1)S(1)}, u32[]{:S(2)}, u32[]{:S(2)}) collective-permute-start(bf16[4,32,2048]{2,1,0:T(8,128)(2,1)S(1)} %get-tuple-element.97), channel_id=1, source_target_pairs={{0,16},{1,17},{32,48},{33,49},{64,80},{65,81},{96,112},{97,113},{2... | collective-permute-start | bytes 1572872 | tf_op jit(solution)/shard_map/ppermute | solution.py:38
  175.4 9.0 %collective-permute-start.21 = (bf16[2,32,2048]{2,1,0:T(8,128)(2,1)S(1)}, bf16[2,32,2048]{2,1,0:T(8,128)(2,1)S(1)}, u32[]{:S(2)}, u32[]{:S(2)}) collective-permute-start(bf16[2,32,2048]{2,1,0:T(8,128)(2,1)S(1)} %get-tuple-element.103), channel_id=1, source_target_pairs={{0,32},{1,33},{32,64},{33,65},{64,96},{65,97},{96,0},{97,1},{2,34}... | collective-permute-start | bytes 786440 | tf_op jit(solution)/shard_map/ppermute | solution.py:38
  176.1 15.0 %collective-permute-start.22 = (bf16[2,32,2048]{2,1,0:T(8,128)(2,1)S(1)}, bf16[2,32,2048]{2,1,0:T(8,128)(2,1)S(1)}, u32[]{:S(2)}, u32[]{:S(2)}) collective-permute-start(bf16[2,32,2048]{2,1,0:T(8,128)(2,1)S(1)} %get-tuple-element.103), channel_id=1, source_target_pairs={{0,64},{1,65},{32,96},{33,97},{64,0},{65,1},{96,32},{97,33},{2,66}... | collective-permute-start | bytes 786440 | tf_op jit(solution)/shard_map/ppermute | solution.py:38
  179.6 11.5 %collective-permute-start.23 = (bf16[2,32,2048]{2,1,0:T(8,128)(2,1)S(1)}, bf16[2,32,2048]{2,1,0:T(8,128)(2,1)S(1)}, u32[]{:S(2)}, u32[]{:S(2)}) collective-permute-start(bf16[2,32,2048]{2,1,0:T(8,128)(2,1)S(1)} %get-tuple-element.103), channel_id=1, source_target_pairs={{0,96},{1,97},{32,0},{33,1},{64,32},{65,33},{96,64},{97,65},{2,98}... | collective-permute-start | bytes 786440 | tf_op jit(solution)/shard_map/ppermute | solution.py:38
  (18 other events, 296.4 us)

commit v5 on v4

--- a/solution.py
+++ b/solution.py
@@ -67,11 +67,12 @@
     )(at, inputs)
 
 
-def matmul_kernel(sets, terms, *refs):
-    lefts, rights, outs = refs[: sets * terms], refs[sets * terms : -4], refs[-4:]
+def matmul_kernel(sets, terms, parts, *refs):
+    operands, outs = refs[: (sets + 1) * terms], refs[(sets + 1) * terms :]
+    lefts, rights = operands[: sets * terms], operands[sets * terms :]
     depth = rights[0].shape[0]
     for r in range(sets):
-        for i, out in enumerate(outs):
+        for i, out in zip(parts, outs):
             total = None
             for left, right in zip(lefts[r * terms : (r + 1) * terms], rights):
                 term = jnp.dot(
@@ -81,7 +82,7 @@
             out[r] = total.astype(BF16)
 
 
-def block_products(sets, rights, width):
+def block_products(sets, rights, width, parts=(0, 1, 2, 3)):
     rows, depth = 2 * HALF, rights[0][0].shape[0]
     tile = 512
     n, terms = len(sets), len(rights)
@@ -94,16 +95,13 @@
         return pl.BlockSpec((depth, tile), lambda i: (0, i + offset // tile))
 
     return pl.pallas_call(
-        functools.partial(matmul_kernel, n, terms),
+        functools.partial(matmul_kernel, n, terms, parts),
         grid=(width // tile,),
         in_specs=[left_spec(o) for _, o in lefts] + [right_spec(o) for _, o in rights],
-        out_specs=[pl.BlockSpec((n, rows, tile), lambda i: (0, 0, i))] * 4,
-        out_shape=[jax.ShapeDtypeStruct((n, rows, width), BF16)] * 4,
+        out_specs=[pl.BlockSpec((n, rows, tile), lambda i: (0, 0, i))] * len(parts),
+        out_shape=[jax.ShapeDtypeStruct((n, rows, width), BF16)] * len(parts),
         compiler_params=pltpu.CompilerParams(vmem_limit_bytes=32 * 1024 * 1024),
-        cost_estimate=pl.CostEstimate(
-            flops=0, bytes_accessed=0,
-            transcendentals=0,
-        ),
+        cost_estimate=pl.CostEstimate(flops=0, bytes_accessed=0, transcendentals=0),
     )(*[v for v, _ in lefts], *[v for v, _ in rights])
 
 
@@ -207,7 +205,11 @@
         ]
         return block_products([lefts], rights, CHUNKS[k])
 
-    first = reduce_first(block_products([own_set, other_set], [(grads_out, 0), (grads_core, 0)], EARLY))
+    chip = [own_set, other_set], [(grads_out, 0), (grads_core, 0)]
+    up, down = block_products(*chip, EARLY, (2, 3))
+    grads, _ = after([grads_out, up])
+    own, keep = block_products(chip[0], [(grads, 0), (grads_core, 0)], EARLY, (0, 1))
+    first = reduce_first((own, keep, up, down))
     sums, early = reduce_second(first)
 
     def partial_gram(slots):
@@ -237,13 +239,12 @@
     sent = jnp.broadcast_to(jnp.pad(local, ((0, 0), (0, 0), (0, 64))), (128, 1, 128))
     parts = lax.all_to_all(sent, AXES, 0, 0, tiled=True)
     group_gram = jnp.sum(parts, axis=(0, 1))[:64].reshape(8, 8) / count
-    scale = weights / jnp.sqrt(jnp.diagonal(group_gram) + 1e-06)
+    scale = weights / jnp.sqrt(jnp.sum(jnp.where(labels[:, None] == labels[None, :], group_gram, 0.0), axis=1) + 1e-06)
 
     def mixed(slots):
         return jnp.sum(scale[:, None, None] * slots.astype(F32), axis=0).astype(BF16)
 
-    owned = jnp.concatenate([mixed(received) for received in slots], axis=1)
-    left, right = jnp.split(owned, 2, axis=1)
+    left, right = (mixed(received) for received in slots)
     left = jnp.stack([left, shift(left, pair=1)])
     right = jnp.stack([right] + [shift(right, dz=n) for n in (1, 2, 3)])
     right = jnp.stack([right, shift(right, pair=1)], axis=1)

time: 194 us -> 191 us (0.985)
  waiting for transfers between devices: 100 us -> 95.7 us
    ppermute x28, waiting for transfers between devices: 77.2 us -> 73 us  [shift(): return lax.ppermute(value, AXES, moves)]
    pallas_call x3 -> x4, Pallas kernels: 14.9 us -> 16.6 us  [block_products(): pl.pallas_call(functools.partial(matmul_kernel, n, terms, parts), grid=(w...]
  transfers between devices with their start and end apart: 31 -> 31, of which waited for: 17 -> 18; matrix products, arithmetic and copies ran while one was open for 6% -> 7% of each run, Pallas kernels for 6% -> 8%
where the time goes in v5:
time: 191 us; the launch traced here: 190 us
  waiting for transfers between devices  95.7 us (50%)
  starting transfers between devices  53.9 us (28%)
  Pallas kernels  19.2 us (10%)
  other arithmetic  9.91 us (5%)
  matrix products  5.96 us (3%)
  local copies, waits for them, and re-layouts  4.46 us (2%)
    ppermute x28, waiting for transfers between devices, shift(): return lax.ppermute(value, AXES, moves)  73 us
    ppermute x28, starting transfers between devices, shift(): return lax.ppermute(value, AXES, moves)  36.3 us
    pallas_call x4, Pallas kernels, block_products(): pl.pallas_call(functools.partial(matmul_kernel, n, terms, parts), grid=(w...  16.6 us
    all_to_all x2, waiting for transfers between devices, spread(): return lax.all_to_all(pieces.reshape(8, 32, -1), 'dom', 0, 0, tiled=True)  13.5 us
    all_to_all x2, starting transfers between devices, spread(): return lax.all_to_all(pieces.reshape(8, 32, -1), 'dom', 0, 0, tiled=True)  10.7 us
    all_to_all x1, waiting for transfers between devices, per_device(): parts = lax.all_to_all(sent, AXES, 0, 0, tiled=True)  9.2 us
    all_to_all x1, starting transfers between devices, per_device(): parts = lax.all_to_all(sent, AXES, 0, 0, tiled=True)  6.91 us
    dot_general x2, matrix products, partial_gram(): lax.dot_general(flat, flat, (((1,), (1,)), ((), ())), preferred_element_t...  4.74 us
  transfers between devices with their start and end apart: 31, of which 18 were waited for; matrix products, arithmetic and copies ran while one was open for 7% of the time, Pallas kernels for 8%

profile of v5, /device:TPU:0, one launch (start us, length us, event | category | flops | bytes accessed | tf_op | source)
XLA Modules:
  0.0 190.2 jit_solution(8578849135799094525)
XLA Ops:
  6.5 3.5 %shard_map.69 = (bf16[2,256,1536]{2,1,0:T(8,128)(2,1)S(1)}, bf16[2,256,1536]{2,1,0:T(8,128)(2,1)S(1)}) custom-call(bf16[256,1024]{1,0:T(8,128)(2,1)S(1)} %get-tuple-element.47.refs_0_, bf16[256,1024]{1,0:T(8,128)(2,1)S(1)} %collective-permute-done.refs_1_, bf16[256,1024]{1,0:T(8,128)(2,1)S(1)} %get-tuple-element.49.refs_2_, ...), custom_call_target="tpu_custom_call" | custom-call | tf_op jit(solution)/shard_map/pallas_call | solution.py:97
  13.5 3.2 %collective-permute-start.7 = (bf16[256,3072]{1,0:T(8,128)(2,1)S(1)}, bf16[256,3072]{1,0:T(8,128)(2,1)S(1)}, u32[]{:S(2)}, u32[]{:S(2)}) collective-permute-start(bf16[256,3072]{1,0:T(8,128)(2,1)S(1)} %pad_maximum_fusion.1), channel_id=1, source_target_pairs={{0,8},{1,9},{32,40},{33,41},{64,72},{65,73},{96,104},{97,105},{2,1... | collective-permute-start | bytes 4718600 | tf_op jit(solution)/shard_map/ppermute | solution.py:38
  17.2 3.5 %shard_map.70 = (bf16[2,256,1536]{2,1,0:T(8,128)(2,1)S(1)}, bf16[2,256,1536]{2,1,0:T(8,128)(2,1)S(1)}) custom-call(bf16[256,1024]{1,0:T(8,128)(2,1)S(1)} %get-tuple-element.47.refs_0_, bf16[256,1024]{1,0:T(8,128)(2,1)S(1)} %collective-permute-done.refs_1_, bf16[256,1024]{1,0:T(8,128)(2,1)S(1)} %get-tuple-element.49.refs_2_, ...), custom_call_target="tpu_custom_call" | custom-call | tf_op jit(solution)/shard_map/pallas_call | solution.py:97
  20.8 27.3 %collective-permute-done.3 = bf16[2,256,1536]{2,1,0:T(8,128)(2,1)S(1)} collective-permute-done((bf16[2,256,1536]{2,1,0:T(8,128)(2,1)S(1)}, bf16[2,256,1536]{2,1,0:T(8,128)(2,1)S(1)}, u32[]{:S(2)}, u32[]{:S(2)}) %collective-permute-start.3) | collective-permute-done | bytes 1572896 | tf_op jit(solution)/shard_map/ppermute | solution.py:38
  54.4 3.7 %shard_map.71 = (bf16[1,256,1024]{2,1,0:T(8,128)(2,1)S(1)}, bf16[1,256,1024]{2,1,0:T(8,128)(2,1)S(1)}, bf16[1,256,1024]{2,1,0:T(8,128)(2,1)S(1)}, bf16[1,256,1024]{2,1,0:T(8,128)(2,1)S(1)}) custom-call(bf16[256,1024]{1,0:T(8,128)(2,1)S(1)} %get-tuple-element.47.refs_0_, bf16[256,1024]{1,0:T(8,128)(2,1)S(1)} %collective-permute-done.refs_1_, ...), custom_call_target="tpu_custom_call" | custom-call | tf_op jit(solution)/shard_map/pallas_call | solution.py:97
  58.1 10.1 %collective-permute-done.12.refs_6_ = bf16[256,1536]{1,0:T(8,128)(2,1)S(1)} collective-permute-done((bf16[256,1536]{1,0:T(8,128)(2,1)S(1)}, bf16[256,1536]{1,0:T(8,128)(2,1)S(1)}, u32[]{:S(2)}, u32[]{:S(2)}) %collective-permute-start.12) | collective-permute-done | bytes 786464 | tf_op jit(solution)/shard_map/ppermute | solution.py:38
  69.6 3.0 %collective-permute-start.9 = (bf16[256,1536]{1,0:T(8,128)(2,1)S(1)}, bf16[256,1536]{1,0:T(8,128)(2,1)S(1)}, u32[]{:S(2)}, u32[]{:S(2)}) collective-permute-start(bf16[256,1536]{1,0:T(8,128)(2,1)S(1)} %fusion.17), channel_id=1, source_target_pairs={{0,8},{1,9},{32,40},{33,41},{64,72},{65,73},{96,104},{97,105},{2,1... | collective-permute-start | bytes 2359304 | tf_op jit(solution)/shard_map/ppermute | solution.py:38
  73.6 2.2 %collective-permute-start.11 = (bf16[1,256,1024]{2,1,0:T(8,128)(2,1)S(1)}, bf16[1,256,1024]{2,1,0:T(8,128)(2,1)S(1)}, u32[]{:S(2)}, u32[]{:S(2)}) collective-permute-start(bf16[1,256,1024]{2,1,0:T(8,128)(2,1)S(1)} %get-tuple-element.67), channel_id=1, source_target_pairs={{0,6},{1,7},{32,38},{33,39},{64,70},{65,71},{96,102},{97,103},{2,0... | collective-permute-start | bytes 1572872 | tf_op jit(solution)/shard_map/ppermute | solution.py:38
  75.9 5.8 %shard_map.72 = (bf16[1,256,1536]{2,1,0:T(8,128)(2,1)S(1)}, bf16[1,256,1536]{2,1,0:T(8,128)(2,1)S(1)}, bf16[1,256,1536]{2,1,0:T(8,128)(2,1)}, bf16[1,256,1536]{2,1,0:T(8,128)(2,1)}) custom-call(bf16[256,1024]{1,0:T(8,128)(2,1)S(1)} %get-tuple-element.47.refs_0_, bf16[256,1024]{1,0:T(8,128)(2,1)S(1)} %collective-permute-done.refs_1_, ...), custom_call_target="tpu_custom_call" | custom-call | tf_op jit(solution)/shard_map/pallas_call | solution.py:97
  81.7 3.2 %collective-permute-start.17 = (bf16[1,256,1536]{2,1,0:T(8,128)(2,1)}, bf16[1,256,1536]{2,1,0:T(8,128)(2,1)S(1)}, u32[]{:S(2)}, u32[]{:S(2)}) collective-permute-start(bf16[1,256,1536]{2,1,0:T(8,128)(2,1)} %get-tuple-element.80), channel_id=1, source_target_pairs={{0,6},{1,7},{32,38},{33,39},{64,70},{65,71},{96,102},{97,103},{2,0... | collective-permute-start | bytes 2359304 | tf_op jit(solution)/shard_map/ppermute | solution.py:38
  84.9 3.8 %collective-permute-done.10 = bf16[1,256,1024]{2,1,0:T(8,128)(2,1)S(1)} collective-permute-done((bf16[1,256,1024]{2,1,0:T(8,128)(2,1)S(1)}, bf16[1,256,1024]{2,1,0:T(8,128)(2,1)S(1)}, u32[]{:S(2)}, u32[]{:S(2)}) %collective-permute-start.10) | collective-permute-done | bytes 524320 | tf_op jit(solution)/shard_map/ppermute | solution.py:38
  93.1 2.3 %fusion.4 = bf16[256,1536]{1,0:T(8,128)(2,1)} fusion(f32[2,128,1536]{2,1,0:T(8,128)S(1)} %get-tuple-element.93, f32[2,128,1536]{2,1,0:T(8,128)S(1)} %get-tuple-element.92, bf16[256,1536]{1,0:T(8,128)(2,1)S(1)} %collective-permute-done.9, bf16[256,4096]{1,0:T(8,128)(2,1)} %bitcast.88), kind=kLoop, calls=%fused_computation.8 | loop fusion | flops 2359296 | bytes 5505024 | tf_op jit(solution)/shard_map/convert_element_type | solution.py:188
  95.4 5.4 %all-to-all-start = ((bf16[8,32,1536]{2,1,0:T(8,128)(2,1)}), bf16[8,32,1536]{2,1,0:T(8,128)(2,1)}, u32[]{:S(2)}, u32[]{:S(2)}) async-start(bf16[8,32,1536]{2,1,0:T(8,128)(2,1)} %bitcast.91), calls=%async_computation | async-start | bytes 1572864 | tf_op jit(solution)/shard_map/all_to_all | solution.py:192
  100.8 4.7 %collective-permute-done.16.from_back = bf16[1,256,1536]{2,1,0:T(8,128)(2,1)S(1)} collective-permute-done((bf16[1,256,1536]{2,1,0:T(8,128)(2,1)}, bf16[1,256,1536]{2,1,0:T(8,128)(2,1)S(1)}, u32[]{:S(2)}, u32[]{:S(2)}) %collective-permute-start.16) | collective-permute-done | bytes 786464 | tf_op jit(solution)/shard_map/ppermute | solution.py:38
  112.7 5.5 %collective-permute-done.18.back2 = bf16[1,128,1536]{2,1,0:T(8,128)(2,1)S(1)} collective-permute-done((bf16[1,128,1536]{2,1,0:T(8,128)(2,1)S(1)}, bf16[1,128,1536]{2,1,0:T(8,128)(2,1)S(1)}, u32[]{:S(2)}, u32[]{:S(2)}) %collective-permute-start.18) | collective-permute-done | bytes 393248 | tf_op jit(solution)/shard_map/ppermute | solution.py:38
  119.7 5.3 %all-to-all-start.1 = ((bf16[8,32,2560]{2,1,0:T(8,128)(2,1)}), bf16[8,32,2560]{2,1,0:T(8,128)(2,1)S(1)}, u32[]{:S(2)}, u32[]{:S(2)}) async-start(bf16[8,32,2560]{2,1,0:T(8,128)(2,1)} %bitcast.11), calls=%async_computation.1 | async-start | bytes 2621440 | tf_op jit(solution)/shard_map/all_to_all | solution.py:192
  125.0 3.1 %convolution_bitcast_fusion = f32[8,8]{1,0:T(8,128)S(1)} fusion(bf16[8,32,1536]{2,1,0:T(8,128)(2,1)} %all-to-all-done), kind=kOutput, calls=%fused_computation.19 | convolution fusion | flops 6291456 | bytes 786688 | tf_op jit(solution)/shard_map/dot_general | solution.py:217
  128.1 13.5 %all-to-all-done.1 = bf16[8,32,2560]{2,1,0:T(8,128)(2,1)S(1)} async-done(((bf16[8,32,2560]{2,1,0:T(8,128)(2,1)}), bf16[8,32,2560]{2,1,0:T(8,128)(2,1)S(1)}, u32[]{:S(2)}, u32[]{:S(2)}) %all-to-all-start.1) | async-done | bytes 1310752 | tf_op jit(solution)/shard_map/all_to_all | solution.py:192
  144.0 6.9 %all-to-all-start.2 = ((f32[128,1,128]{2,1,0:T(1,128)}), f32[128,1,128]{2,1,0:T(1,128)S(1)}, u32[]{:S(2)}, u32[]{:S(2)}) async-start(f32[128,1,128]{2,1,0:T(1,128)} %broadcast_in_dim.22), calls=%async_computation.2 | async-start | bytes 131072 | tf_op jit(solution)/shard_map/all_to_all | solution.py:240
  151.0 9.2 %all-to-all-done.2 = f32[128,1,128]{2,1,0:T(1,128)S(1)} async-done(((f32[128,1,128]{2,1,0:T(1,128)}), f32[128,1,128]{2,1,0:T(1,128)S(1)}, u32[]{:S(2)}, u32[]{:S(2)}) %all-to-all-start.2) | async-done | bytes 65568 | tf_op jit(solution)/shard_map/all_to_all | solution.py:240
  166.6 5.1 %collective-permute-done.24 = bf16[32,2560]{1,0:T(8,128)(2,1)S(1)} collective-permute-done((bf16[32,2560]{1,0:T(8,128)(2,1)S(1)}, bf16[32,2560]{1,0:T(8,128)(2,1)S(1)}, u32[]{:S(2)}, u32[]{:S(2)}) %collective-permute-start.24) | collective-permute-done | bytes 163872 | tf_op jit(solution)/shard_map/ppermute | solution.py:38
  174.1 3.5 %collective-permute-start.22 = (bf16[2,32,1536]{2,1,0:T(8,128)(2,1)S(1)}, bf16[2,32,1536]{2,1,0:T(8,128)(2,1)S(1)}, u32[]{:S(2)}, u32[]{:S(2)}) collective-permute-start(bf16[2,32,1536]{2,1,0:T(8,128)(2,1)S(1)} %get-tuple-element.105), channel_id=1, source_target_pairs={{0,64},{1,65},{32,96},{33,97},{64,0},{65,1},{96,32},{97,33},{2,66}... | collective-permute-start | bytes 589832 | tf_op jit(solution)/shard_map/ppermute | solution.py:38
  178.4 2.6 %collective-permute-done.21 = bf16[2,32,1536]{2,1,0:T(8,128)(2,1)S(1)} collective-permute-done((bf16[2,32,1536]{2,1,0:T(8,128)(2,1)S(1)}, bf16[2,32,1536]{2,1,0:T(8,128)(2,1)S(1)}, u32[]{:S(2)}, u32[]{:S(2)}) %collective-permute-start.21) | collective-permute-done | bytes 196640 | tf_op jit(solution)/shard_map/ppermute | solution.py:38
  181.0 5.3 %collective-permute-done.22 = bf16[2,32,1536]{2,1,0:T(8,128)(2,1)S(1)} collective-permute-done((bf16[2,32,1536]{2,1,0:T(8,128)(2,1)S(1)}, bf16[2,32,1536]{2,1,0:T(8,128)(2,1)S(1)}, u32[]{:S(2)}, u32[]{:S(2)}) %collective-permute-start.22) | collective-permute-done | bytes 196640 | tf_op jit(solution)/shard_map/ppermute | solution.py:38
  (105 shorter events, 47.2 us)
Async XLA Ops:
  10.0 38.1 %collective-permute-start.3 = (bf16[2,256,1536]{2,1,0:T(8,128)(2,1)S(1)}, bf16[2,256,1536]{2,1,0:T(8,128)(2,1)S(1)}, u32[]{:S(2)}, u32[]{:S(2)}) collective-permute-start(bf16[2,256,1536]{2,1,0:T(8,128)(2,1)S(1)} %get-tuple-element.51), channel_id=1, source_target_pairs={{0,2},{1,3},{32,34},{33,35},{64,66},{65,67},{96,98},{97,99},{2,4},... | collective-permute-start | bytes 4718600 | tf_op jit(solution)/shard_map/ppermute | solution.py:38
  11.7 36.4 %collective-permute-start.4 = (bf16[2,256,1536]{2,1,0:T(8,128)(2,1)S(1)}, bf16[2,256,1536]{2,1,0:T(8,128)(2,1)S(1)}, u32[]{:S(2)}, u32[]{:S(2)}) collective-permute-start(bf16[2,256,1536]{2,1,0:T(8,128)(2,1)S(1)} %get-tuple-element.54), channel_id=1, source_target_pairs={{0,6},{1,7},{32,38},{33,39},{64,70},{65,71},{96,102},{97,103},{2,0... | collective-permute-start | bytes 4718600 | tf_op jit(solution)/shard_map/ppermute | solution.py:38
  13.5 38.8 %collective-permute-start.7 = (bf16[256,3072]{1,0:T(8,128)(2,1)S(1)}, bf16[256,3072]{1,0:T(8,128)(2,1)S(1)}, u32[]{:S(2)}, u32[]{:S(2)}) collective-permute-start(bf16[256,3072]{1,0:T(8,128)(2,1)S(1)} %pad_maximum_fusion.1), channel_id=1, source_target_pairs={{0,8},{1,9},{32,40},{33,41},{64,72},{65,73},{96,104},{97,105},{2,1... | collective-permute-start | bytes 4718600 | tf_op jit(solution)/shard_map/ppermute | solution.py:38
  16.7 51.5 %collective-permute-start.12 = (bf16[256,1536]{1,0:T(8,128)(2,1)S(1)}, bf16[256,1536]{1,0:T(8,128)(2,1)S(1)}, u32[]{:S(2)}, u32[]{:S(2)}) collective-permute-start(bf16[256,1536]{1,0:T(8,128)(2,1)S(1)} %slice.129), channel_id=1, source_target_pairs={{0,8},{1,9},{32,40},{33,41},{64,72},{65,73},{96,104},{97,105},{2,1... | collective-permute-start | bytes 2359304 | tf_op jit(solution)/shard_map/ppermute | solution.py:38
  48.5 20.4 %collective-permute-start.5 = (bf16[2,128,1536]{2,1,0:T(8,128)(2,1)S(1)}, bf16[2,128,1536]{2,1,0:T(8,128)(2,1)S(1)}, u32[]{:S(2)}, u32[]{:S(2)}) collective-permute-start(bf16[2,128,1536]{2,1,0:T(8,128)(2,1)S(1)} %get-tuple-element.95), channel_id=1, source_target_pairs={{0,2},{1,3},{32,34},{33,35},{64,66},{65,67},{96,98},{97,99},{2,4},... | collective-permute-start | bytes 2359304 | tf_op jit(solution)/shard_map/ppermute | solution.py:38
  50.2 18.7 %collective-permute-start.6 = (bf16[2,128,1536]{2,1,0:T(8,128)(2,1)S(1)}, bf16[2,128,1536]{2,1,0:T(8,128)(2,1)S(1)}, u32[]{:S(2)}, u32[]{:S(2)}) collective-permute-start(bf16[2,128,1536]{2,1,0:T(8,128)(2,1)S(1)} %get-tuple-element.94), channel_id=1, source_target_pairs={{0,6},{1,7},{32,38},{33,39},{64,70},{65,71},{96,102},{97,103},{2,0... | collective-permute-start | bytes 2359304 | tf_op jit(solution)/shard_map/ppermute | solution.py:38
  69.6 23.5 %collective-permute-start.9 = (bf16[256,1536]{1,0:T(8,128)(2,1)S(1)}, bf16[256,1536]{1,0:T(8,128)(2,1)S(1)}, u32[]{:S(2)}, u32[]{:S(2)}) collective-permute-start(bf16[256,1536]{1,0:T(8,128)(2,1)S(1)} %fusion.17), channel_id=1, source_target_pairs={{0,8},{1,9},{32,40},{33,41},{64,72},{65,73},{96,104},{97,105},{2,1... | collective-permute-start | bytes 2359304 | tf_op jit(solution)/shard_map/ppermute | solution.py:38
  72.6 16.1 %collective-permute-start.10 = (bf16[1,256,1024]{2,1,0:T(8,128)(2,1)S(1)}, bf16[1,256,1024]{2,1,0:T(8,128)(2,1)S(1)}, u32[]{:S(2)}, u32[]{:S(2)}) collective-permute-start(bf16[1,256,1024]{2,1,0:T(8,128)(2,1)S(1)} %get-tuple-element.59), channel_id=1, source_target_pairs={{0,2},{1,3},{32,34},{33,35},{64,66},{65,67},{96,98},{97,99},{2,4},... | collective-permute-start | bytes 1572872 | tf_op jit(solution)/shard_map/ppermute | solution.py:38
  73.6 15.1 %collective-permute-start.11 = (bf16[1,256,1024]{2,1,0:T(8,128)(2,1)S(1)}, bf16[1,256,1024]{2,1,0:T(8,128)(2,1)S(1)}, u32[]{:S(2)}, u32[]{:S(2)}) collective-permute-start(bf16[1,256,1024]{2,1,0:T(8,128)(2,1)S(1)} %get-tuple-element.67), channel_id=1, source_target_pairs={{0,6},{1,7},{32,38},{33,39},{64,70},{65,71},{96,102},{97,103},{2,0... | collective-permute-start | bytes 1572872 | tf_op jit(solution)/shard_map/ppermute | solution.py:38
  81.7 23.9 %collective-permute-start.16 = (bf16[1,256,1536]{2,1,0:T(8,128)(2,1)}, bf16[1,256,1536]{2,1,0:T(8,128)(2,1)S(1)}, u32[]{:S(2)}, u32[]{:S(2)}) collective-permute-start(bf16[1,256,1536]{2,1,0:T(8,128)(2,1)} %get-tuple-element.72), channel_id=1, source_target_pairs={{0,2},{1,3},{32,34},{33,35},{64,66},{65,67},{96,98},{97,99},{2,4},... | collective-permute-start | bytes 2359304 | tf_op jit(solution)/shard_map/ppermute | solution.py:38
  81.7 23.9 %collective-permute-start.17 = (bf16[1,256,1536]{2,1,0:T(8,128)(2,1)}, bf16[1,256,1536]{2,1,0:T(8,128)(2,1)S(1)}, u32[]{:S(2)}, u32[]{:S(2)}) collective-permute-start(bf16[1,256,1536]{2,1,0:T(8,128)(2,1)} %get-tuple-element.80), channel_id=1, source_target_pairs={{0,6},{1,7},{32,38},{33,39},{64,70},{65,71},{96,102},{97,103},{2,0... | collective-permute-start | bytes 2359304 | tf_op jit(solution)/shard_map/ppermute | solution.py:38
  89.9 21.4 %collective-permute-start.14 = (bf16[1,128,1024]{2,1,0:T(8,128)(2,1)}, bf16[1,128,1024]{2,1,0:T(8,128)(2,1)}, u32[]{:S(2)}, u32[]{:S(2)}) collective-permute-start(bf16[1,128,1024]{2,1,0:T(8,128)(2,1)} %get-tuple-element.103), channel_id=1, source_target_pairs={{0,2},{1,3},{32,34},{33,35},{64,66},{65,67},{96,98},{97,99},{2,4},... | collective-permute-start | bytes 786440 | tf_op jit(solution)/shard_map/ppermute | solution.py:38
  91.2 20.0 %collective-permute-start.15 = (bf16[1,128,1024]{2,1,0:T(8,128)(2,1)}, bf16[1,128,1024]{2,1,0:T(8,128)(2,1)}, u32[]{:S(2)}, u32[]{:S(2)}) collective-permute-start(bf16[1,128,1024]{2,1,0:T(8,128)(2,1)} %get-tuple-element.102), channel_id=1, source_target_pairs={{0,6},{1,7},{32,38},{33,39},{64,70},{65,71},{96,102},{97,103},{2,0... | collective-permute-start | bytes 786440 | tf_op jit(solution)/shard_map/ppermute | solution.py:38
  95.4 24.2 %all-to-all-start = ((bf16[8,32,1536]{2,1,0:T(8,128)(2,1)}), bf16[8,32,1536]{2,1,0:T(8,128)(2,1)}, u32[]{:S(2)}, u32[]{:S(2)}) async-start(bf16[8,32,1536]{2,1,0:T(8,128)(2,1)} %bitcast.91), calls=%async_computation | async-start | bytes 1572864 | tf_op jit(solution)/shard_map/all_to_all | solution.py:192
  107.0 11.1 %collective-permute-start.18 = (bf16[1,128,1536]{2,1,0:T(8,128)(2,1)S(1)}, bf16[1,128,1536]{2,1,0:T(8,128)(2,1)S(1)}, u32[]{:S(2)}, u32[]{:S(2)}) collective-permute-start(bf16[1,128,1536]{2,1,0:T(8,128)(2,1)S(1)} %get-tuple-element.97), channel_id=1, source_target_pairs={{0,2},{1,3},{32,34},{33,35},{64,66},{65,67},{96,98},{97,99},{2,4},... | collective-permute-start | bytes 1179656 | tf_op jit(solution)/shard_map/ppermute | solution.py:38
  108.6 9.5 %collective-permute-start.19 = (bf16[1,128,1536]{2,1,0:T(8,128)(2,1)S(1)}, bf16[1,128,1536]{2,1,0:T(8,128)(2,1)S(1)}, u32[]{:S(2)}, u32[]{:S(2)}) collective-permute-start(bf16[1,128,1536]{2,1,0:T(8,128)(2,1)S(1)} %get-tuple-element.96), channel_id=1, source_target_pairs={{0,6},{1,7},{32,38},{33,39},{64,70},{65,71},{96,102},{97,103},{2,0... | collective-permute-start | bytes 1179656 | tf_op jit(solution)/shard_map/ppermute | solution.py:38
  119.7 22.0 %all-to-all-start.1 = ((bf16[8,32,2560]{2,1,0:T(8,128)(2,1)}), bf16[8,32,2560]{2,1,0:T(8,128)(2,1)S(1)}, u32[]{:S(2)}, u32[]{:S(2)}) async-start(bf16[8,32,2560]{2,1,0:T(8,128)(2,1)} %bitcast.11), calls=%async_computation.1 | async-start | bytes 2621440 | tf_op jit(solution)/shard_map/all_to_all | solution.py:192
  144.0 16.2 %all-to-all-start.2 = ((f32[128,1,128]{2,1,0:T(1,128)}), f32[128,1,128]{2,1,0:T(1,128)S(1)}, u32[]{:S(2)}, u32[]{:S(2)}) async-start(f32[128,1,128]{2,1,0:T(1,128)} %broadcast_in_dim.22), calls=%async_computation.2 | async-start | bytes 131072 | tf_op jit(solution)/shard_map/all_to_all | solution.py:240
  161.0 10.8 %collective-permute-start.24 = (bf16[32,2560]{1,0:T(8,128)(2,1)S(1)}, bf16[32,2560]{1,0:T(8,128)(2,1)S(1)}, u32[]{:S(2)}, u32[]{:S(2)}) collective-permute-start(bf16[32,2560]{1,0:T(8,128)(2,1)S(1)} %multiply_reduce_fusion), channel_id=1, source_target_pairs={{0,32},{1,33},{32,64},{33,65},{64,96},{65,97},{96,0},{97,1},{2,34}... | collective-permute-start | bytes 491528 | tf_op jit(solution)/shard_map/ppermute | solution.py:38
  161.9 9.9 %collective-permute-start.25 = (bf16[32,2560]{1,0:T(8,128)(2,1)S(1)}, bf16[32,2560]{1,0:T(8,128)(2,1)S(1)}, u32[]{:S(2)}, u32[]{:S(2)}) collective-permute-start(bf16[32,2560]{1,0:T(8,128)(2,1)S(1)} %multiply_reduce_fusion), channel_id=1, source_target_pairs={{0,64},{1,65},{32,96},{33,97},{64,0},{65,1},{96,32},{97,33},{2,66}... | collective-permute-start | bytes 491528 | tf_op jit(solution)/shard_map/ppermute | solution.py:38
  163.4 9.0 %collective-permute-start.26 = (bf16[32,2560]{1,0:T(8,128)(2,1)S(1)}, bf16[32,2560]{1,0:T(8,128)(2,1)S(1)}, u32[]{:S(2)}, u32[]{:S(2)}) collective-permute-start(bf16[32,2560]{1,0:T(8,128)(2,1)S(1)} %multiply_reduce_fusion), channel_id=1, source_target_pairs={{0,96},{1,97},{32,0},{33,1},{64,32},{65,33},{96,64},{97,65},{2,98}... | collective-permute-start | bytes 491528 | tf_op jit(solution)/shard_map/ppermute | solution.py:38
  172.5 15.7 %collective-permute-start.27 = (bf16[4,32,2560]{2,1,0:T(8,128)(2,1)S(1)}, bf16[4,32,2560]{2,1,0:T(8,128)(2,1)S(1)}, u32[]{:S(2)}, u32[]{:S(2)}) collective-permute-start(bf16[4,32,2560]{2,1,0:T(8,128)(2,1)S(1)} %get-tuple-element.99), channel_id=1, source_target_pairs={{0,16},{1,17},{32,48},{33,49},{64,80},{65,81},{96,112},{97,113},{2... | collective-permute-start | bytes 1966088 | tf_op jit(solution)/shard_map/ppermute | solution.py:38
  174.1 12.2 %collective-permute-start.22 = (bf16[2,32,1536]{2,1,0:T(8,128)(2,1)S(1)}, bf16[2,32,1536]{2,1,0:T(8,128)(2,1)S(1)}, u32[]{:S(2)}, u32[]{:S(2)}) collective-permute-start(bf16[2,32,1536]{2,1,0:T(8,128)(2,1)S(1)} %get-tuple-element.105), channel_id=1, source_target_pairs={{0,64},{1,65},{32,96},{33,97},{64,0},{65,1},{96,32},{97,33},{2,66}... | collective-permute-start | bytes 589832 | tf_op jit(solution)/shard_map/ppermute | solution.py:38
  177.6 8.7 %collective-permute-start.23 = (bf16[2,32,1536]{2,1,0:T(8,128)(2,1)S(1)}, bf16[2,32,1536]{2,1,0:T(8,128)(2,1)S(1)}, u32[]{:S(2)}, u32[]{:S(2)}) collective-permute-start(bf16[2,32,1536]{2,1,0:T(8,128)(2,1)S(1)} %get-tuple-element.105), channel_id=1, source_target_pairs={{0,96},{1,97},{32,0},{33,1},{64,32},{65,33},{96,64},{97,65},{2,98}... | collective-permute-start | bytes 589832 | tf_op jit(solution)/shard_map/ppermute | solution.py:38
  (18 other events, 294.0 us)

commit v6 on v5

--- a/solution.py
+++ b/solution.py
@@ -245,10 +245,15 @@
         return jnp.sum(scale[:, None, None] * slots.astype(F32), axis=0).astype(BF16)
 
     left, right = (mixed(received) for received in slots)
-    left = jnp.stack([left, shift(left, pair=1)])
-    right = jnp.stack([right] + [shift(right, dz=n) for n in (1, 2, 3)])
-    right = jnp.stack([right, shift(right, pair=1)], axis=1)
+    split = left.shape[1]
+    other = shift(jnp.concatenate([left, right], axis=1), pair=1)
+    around = jnp.stack([shift(right, dz=n) for n in (1, 2, 3)])
+    crossed = shift(around, pair=1)
+    left = jnp.stack([left, other[:, :split]])
     left = jnp.stack([left] + [shift(left, dz=n) for n in (1, 2, 3)])
+    right = jnp.concatenate(
+        [jnp.stack([right, other[:, split:]])[None], jnp.stack([around, crossed], axis=1)]
+    )
     pieces = jnp.concatenate([left, right], axis=3)
     combined = jnp.zeros((2 * HALF, WIN), BF16)
     for n in range(4):

time: 191 us -> 189 us (0.990)
  waiting for transfers between devices: 95.7 us -> 91.8 us
    ppermute x28, waiting for transfers between devices: 73 us -> 69.2 us  [shift(): return lax.ppermute(value, AXES, moves)]
where the time goes in v6:
time: 189 us; the launch traced here: 188 us
  waiting for transfers between devices  91.8 us (49%)
  starting transfers between devices  55.6 us (29%)
  Pallas kernels  19.2 us (10%)
  other arithmetic  9.93 us (5%)
  matrix products  5.96 us (3%)
  local copies, waits for them, and re-layouts  4.47 us (2%)
    ppermute x28, waiting for transfers between devices, shift(): return lax.ppermute(value, AXES, moves)  69.2 us
    ppermute x28, starting transfers between devices, shift(): return lax.ppermute(value, AXES, moves)  38 us
    pallas_call x4, Pallas kernels, block_products(): pl.pallas_call(functools.partial(matmul_kernel, n, terms, parts), grid=(w...  16.6 us
    all_to_all x2, waiting for transfers between devices, spread(): return lax.all_to_all(pieces.reshape(8, 32, -1), 'dom', 0, 0, tiled=True)  13.5 us
    all_to_all x2, starting transfers between devices, spread(): return lax.all_to_all(pieces.reshape(8, 32, -1), 'dom', 0, 0, tiled=True)  10.7 us
    all_to_all x1, waiting for transfers between devices, per_device(): parts = lax.all_to_all(sent, AXES, 0, 0, tiled=True)  9.12 us
    all_to_all x1, starting transfers between devices, per_device(): parts = lax.all_to_all(sent, AXES, 0, 0, tiled=True)  6.91 us
    dot_general x2, matrix products, partial_gram(): lax.dot_general(flat, flat, (((1,), (1,)), ((), ())), preferred_element_t...  4.74 us
  transfers between devices with their start and end apart: 31, of which 18 were waited for; matrix products, arithmetic and copies ran while one was open for 7% of the time, Pallas kernels for 8%

profile of v6, /device:TPU:0, one launch (start us, length us, event | category | flops | bytes accessed | tf_op | source)
XLA Modules:
  0.0 188.1 jit_solution(13383655200268184956)
XLA Ops:
  6.5 3.5 %shard_map.69 = (bf16[2,256,1536]{2,1,0:T(8,128)(2,1)S(1)}, bf16[2,256,1536]{2,1,0:T(8,128)(2,1)S(1)}) custom-call(bf16[256,1024]{1,0:T(8,128)(2,1)S(1)} %get-tuple-element.47.refs_0_, bf16[256,1024]{1,0:T(8,128)(2,1)S(1)} %collective-permute-done.refs_1_, bf16[256,1024]{1,0:T(8,128)(2,1)S(1)} %get-tuple-element.49.refs_2_, ...), custom_call_target="tpu_custom_call" | custom-call | tf_op jit(solution)/shard_map/pallas_call | solution.py:97
  13.5 3.2 %collective-permute-start.7 = (bf16[256,3072]{1,0:T(8,128)(2,1)S(1)}, bf16[256,3072]{1,0:T(8,128)(2,1)S(1)}, u32[]{:S(2)}, u32[]{:S(2)}) collective-permute-start(bf16[256,3072]{1,0:T(8,128)(2,1)S(1)} %pad_maximum_fusion.1), channel_id=1, source_target_pairs={{0,8},{1,9},{32,40},{33,41},{64,72},{65,73},{96,104},{97,105},{2,1... | collective-permute-start | bytes 4718600 | tf_op jit(solution)/shard_map/ppermute | solution.py:38
  17.2 3.5 %shard_map.70 = (bf16[2,256,1536]{2,1,0:T(8,128)(2,1)S(1)}, bf16[2,256,1536]{2,1,0:T(8,128)(2,1)S(1)}) custom-call(bf16[256,1024]{1,0:T(8,128)(2,1)S(1)} %get-tuple-element.47.refs_0_, bf16[256,1024]{1,0:T(8,128)(2,1)S(1)} %collective-permute-done.refs_1_, bf16[256,1024]{1,0:T(8,128)(2,1)S(1)} %get-tuple-element.49.refs_2_, ...), custom_call_target="tpu_custom_call" | custom-call | tf_op jit(solution)/shard_map/pallas_call | solution.py:97
  20.8 27.3 %collective-permute-done.3 = bf16[2,256,1536]{2,1,0:T(8,128)(2,1)S(1)} collective-permute-done((bf16[2,256,1536]{2,1,0:T(8,128)(2,1)S(1)}, bf16[2,256,1536]{2,1,0:T(8,128)(2,1)S(1)}, u32[]{:S(2)}, u32[]{:S(2)}) %collective-permute-start.3) | collective-permute-done | bytes 1572896 | tf_op jit(solution)/shard_map/ppermute | solution.py:38
  54.4 3.7 %shard_map.71 = (bf16[1,256,1024]{2,1,0:T(8,128)(2,1)S(1)}, bf16[1,256,1024]{2,1,0:T(8,128)(2,1)S(1)}, bf16[1,256,1024]{2,1,0:T(8,128)(2,1)S(1)}, bf16[1,256,1024]{2,1,0:T(8,128)(2,1)S(1)}) custom-call(bf16[256,1024]{1,0:T(8,128)(2,1)S(1)} %get-tuple-element.47.refs_0_, bf16[256,1024]{1,0:T(8,128)(2,1)S(1)} %collective-permute-done.refs_1_, ...), custom_call_target="tpu_custom_call" | custom-call | tf_op jit(solution)/shard_map/pallas_call | solution.py:97
  58.1 10.1 %collective-permute-done.12.refs_6_ = bf16[256,1536]{1,0:T(8,128)(2,1)S(1)} collective-permute-done((bf16[256,1536]{1,0:T(8,128)(2,1)S(1)}, bf16[256,1536]{1,0:T(8,128)(2,1)S(1)}, u32[]{:S(2)}, u32[]{:S(2)}) %collective-permute-start.12) | collective-permute-done | bytes 786464 | tf_op jit(solution)/shard_map/ppermute | solution.py:38
  69.6 3.0 %collective-permute-start.9 = (bf16[256,1536]{1,0:T(8,128)(2,1)S(1)}, bf16[256,1536]{1,0:T(8,128)(2,1)S(1)}, u32[]{:S(2)}, u32[]{:S(2)}) collective-permute-start(bf16[256,1536]{1,0:T(8,128)(2,1)S(1)} %fusion.17), channel_id=1, source_target_pairs={{0,8},{1,9},{32,40},{33,41},{64,72},{65,73},{96,104},{97,105},{2,1... | collective-permute-start | bytes 2359304 | tf_op jit(solution)/shard_map/ppermute | solution.py:38
  73.6 2.2 %collective-permute-start.11 = (bf16[1,256,1024]{2,1,0:T(8,128)(2,1)S(1)}, bf16[1,256,1024]{2,1,0:T(8,128)(2,1)S(1)}, u32[]{:S(2)}, u32[]{:S(2)}) collective-permute-start(bf16[1,256,1024]{2,1,0:T(8,128)(2,1)S(1)} %get-tuple-element.67), channel_id=1, source_target_pairs={{0,6},{1,7},{32,38},{33,39},{64,70},{65,71},{96,102},{97,103},{2,0... | collective-permute-start | bytes 1572872 | tf_op jit(solution)/shard_map/ppermute | solution.py:38
  75.9 5.8 %shard_map.72 = (bf16[1,256,1536]{2,1,0:T(8,128)(2,1)S(1)}, bf16[1,256,1536]{2,1,0:T(8,128)(2,1)S(1)}, bf16[1,256,1536]{2,1,0:T(8,128)(2,1)}, bf16[1,256,1536]{2,1,0:T(8,128)(2,1)}) custom-call(bf16[256,1024]{1,0:T(8,128)(2,1)S(1)} %get-tuple-element.47.refs_0_, bf16[256,1024]{1,0:T(8,128)(2,1)S(1)} %collective-permute-done.refs_1_, ...), custom_call_target="tpu_custom_call" | custom-call | tf_op jit(solution)/shard_map/pallas_call | solution.py:97
  81.7 3.2 %collective-permute-start.17 = (bf16[1,256,1536]{2,1,0:T(8,128)(2,1)}, bf16[1,256,1536]{2,1,0:T(8,128)(2,1)S(1)}, u32[]{:S(2)}, u32[]{:S(2)}) collective-permute-start(bf16[1,256,1536]{2,1,0:T(8,128)(2,1)} %get-tuple-element.80), channel_id=1, source_target_pairs={{0,6},{1,7},{32,38},{33,39},{64,70},{65,71},{96,102},{97,103},{2,0... | collective-permute-start | bytes 2359304 | tf_op jit(solution)/shard_map/ppermute | solution.py:38
  84.9 3.8 %collective-permute-done.10 = bf16[1,256,1024]{2,1,0:T(8,128)(2,1)S(1)} collective-permute-done((bf16[1,256,1024]{2,1,0:T(8,128)(2,1)S(1)}, bf16[1,256,1024]{2,1,0:T(8,128)(2,1)S(1)}, u32[]{:S(2)}, u32[]{:S(2)}) %collective-permute-start.10) | collective-permute-done | bytes 524320 | tf_op jit(solution)/shard_map/ppermute | solution.py:38
  93.1 2.3 %fusion.4 = bf16[256,1536]{1,0:T(8,128)(2,1)} fusion(f32[2,128,1536]{2,1,0:T(8,128)S(1)} %get-tuple-element.93, f32[2,128,1536]{2,1,0:T(8,128)S(1)} %get-tuple-element.92, bf16[256,1536]{1,0:T(8,128)(2,1)S(1)} %collective-permute-done.9, bf16[256,4096]{1,0:T(8,128)(2,1)} %bitcast.93), kind=kLoop, calls=%fused_computation.8 | loop fusion | flops 2359296 | bytes 5505024 | tf_op jit(solution)/shard_map/convert_element_type | solution.py:188
  95.4 5.4 %all-to-all-start = ((bf16[8,32,1536]{2,1,0:T(8,128)(2,1)}), bf16[8,32,1536]{2,1,0:T(8,128)(2,1)}, u32[]{:S(2)}, u32[]{:S(2)}) async-start(bf16[8,32,1536]{2,1,0:T(8,128)(2,1)} %bitcast.96), calls=%async_computation | async-start | bytes 1572864 | tf_op jit(solution)/shard_map/all_to_all | solution.py:192
  100.8 4.7 %collective-permute-done.16.from_back = bf16[1,256,1536]{2,1,0:T(8,128)(2,1)S(1)} collective-permute-done((bf16[1,256,1536]{2,1,0:T(8,128)(2,1)}, bf16[1,256,1536]{2,1,0:T(8,128)(2,1)S(1)}, u32[]{:S(2)}, u32[]{:S(2)}) %collective-permute-start.16) | collective-permute-done | bytes 786464 | tf_op jit(solution)/shard_map/ppermute | solution.py:38
  112.7 5.5 %collective-permute-done.18.back2 = bf16[1,128,1536]{2,1,0:T(8,128)(2,1)S(1)} collective-permute-done((bf16[1,128,1536]{2,1,0:T(8,128)(2,1)S(1)}, bf16[1,128,1536]{2,1,0:T(8,128)(2,1)S(1)}, u32[]{:S(2)}, u32[]{:S(2)}) %collective-permute-start.18) | collective-permute-done | bytes 393248 | tf_op jit(solution)/shard_map/ppermute | solution.py:38
  119.7 5.3 %all-to-all-start.1 = ((bf16[8,32,2560]{2,1,0:T(8,128)(2,1)}), bf16[8,32,2560]{2,1,0:T(8,128)(2,1)S(1)}, u32[]{:S(2)}, u32[]{:S(2)}) async-start(bf16[8,32,2560]{2,1,0:T(8,128)(2,1)} %bitcast.11), calls=%async_computation.1 | async-start | bytes 2621440 | tf_op jit(solution)/shard_map/all_to_all | solution.py:192
  125.0 3.1 %convolution_bitcast_fusion = f32[8,8]{1,0:T(8,128)S(1)} fusion(bf16[8,32,1536]{2,1,0:T(8,128)(2,1)} %all-to-all-done), kind=kOutput, calls=%fused_computation.19 | convolution fusion | flops 6291456 | bytes 786688 | tf_op jit(solution)/shard_map/dot_general | solution.py:217
  128.1 13.5 %all-to-all-done.1 = bf16[8,32,2560]{2,1,0:T(8,128)(2,1)S(1)} async-done(((bf16[8,32,2560]{2,1,0:T(8,128)(2,1)}), bf16[8,32,2560]{2,1,0:T(8,128)(2,1)S(1)}, u32[]{:S(2)}, u32[]{:S(2)}) %all-to-all-start.1) | async-done | bytes 1310752 | tf_op jit(solution)/shard_map/all_to_all | solution.py:192
  144.0 6.9 %all-to-all-start.2 = ((f32[128,1,128]{2,1,0:T(1,128)}), f32[128,1,128]{2,1,0:T(1,128)S(1)}, u32[]{:S(2)}, u32[]{:S(2)}) async-start(f32[128,1,128]{2,1,0:T(1,128)} %broadcast_in_dim.25), calls=%async_computation.2 | async-start | bytes 131072 | tf_op jit(solution)/shard_map/all_to_all | solution.py:240
  151.1 9.1 %all-to-all-done.2 = f32[128,1,128]{2,1,0:T(1,128)S(1)} async-done(((f32[128,1,128]{2,1,0:T(1,128)}), f32[128,1,128]{2,1,0:T(1,128)S(1)}, u32[]{:S(2)}, u32[]{:S(2)}) %all-to-all-start.2) | async-done | bytes 65568 | tf_op jit(solution)/shard_map/all_to_all | solution.py:240
  167.7 4.0 %collective-permute-done.24 = bf16[32,2560]{1,0:T(8,128)(2,1)S(1)} collective-permute-done((bf16[32,2560]{1,0:T(8,128)(2,1)S(1)}, bf16[32,2560]{1,0:T(8,128)(2,1)S(1)}, u32[]{:S(2)}, u32[]{:S(2)}) %collective-permute-start.24) | collective-permute-done | bytes 163872 | tf_op jit(solution)/shard_map/ppermute | solution.py:38
  174.5 2.8 %collective-permute-start.22 = (bf16[2,32,1536]{2,1,0:T(8,128)(2,1)S(1)}, bf16[2,32,1536]{2,1,0:T(8,128)(2,1)S(1)}, u32[]{:S(2)}, u32[]{:S(2)}) collective-permute-start(bf16[2,32,1536]{2,1,0:T(8,128)(2,1)S(1)} %get-tuple-element.105), channel_id=1, source_target_pairs={{0,64},{1,65},{32,96},{33,97},{64,0},{65,1},{96,32},{97,33},{2,66}... | collective-permute-start | bytes 589832 | tf_op jit(solution)/shard_map/ppermute | solution.py:38
  177.3 2.4 %collective-permute-start.23 = (bf16[2,32,1536]{2,1,0:T(8,128)(2,1)S(1)}, bf16[2,32,1536]{2,1,0:T(8,128)(2,1)S(1)}, u32[]{:S(2)}, u32[]{:S(2)}) collective-permute-start(bf16[2,32,1536]{2,1,0:T(8,128)(2,1)S(1)} %get-tuple-element.105), channel_id=1, source_target_pairs={{0,96},{1,97},{32,0},{33,1},{64,32},{65,33},{96,64},{97,65},{2,98}... | collective-permute-start | bytes 589832 | tf_op jit(solution)/shard_map/ppermute | solution.py:38
  181.2 4.8 %collective-permute-done.22 = bf16[2,32,1536]{2,1,0:T(8,128)(2,1)S(1)} collective-permute-done((bf16[2,32,1536]{2,1,0:T(8,128)(2,1)S(1)}, bf16[2,32,1536]{2,1,0:T(8,128)(2,1)S(1)}, u32[]{:S(2)}, u32[]{:S(2)}) %collective-permute-start.22) | collective-permute-done | bytes 196640 | tf_op jit(solution)/shard_map/ppermute | solution.py:38
  (109 shorter events, 47.5 us)
Async XLA Ops:
  10.0 38.1 %collective-permute-start.3 = (bf16[2,256,1536]{2,1,0:T(8,128)(2,1)S(1)}, bf16[2,256,1536]{2,1,0:T(8,128)(2,1)S(1)}, u32[]{:S(2)}, u32[]{:S(2)}) collective-permute-start(bf16[2,256,1536]{2,1,0:T(8,128)(2,1)S(1)} %get-tuple-element.51), channel_id=1, source_target_pairs={{0,2},{1,3},{32,34},{33,35},{64,66},{65,67},{96,98},{97,99},{2,4},... | collective-permute-start | bytes 4718600 | tf_op jit(solution)/shard_map/ppermute | solution.py:38
  11.7 36.4 %collective-permute-start.4 = (bf16[2,256,1536]{2,1,0:T(8,128)(2,1)S(1)}, bf16[2,256,1536]{2,1,0:T(8,128)(2,1)S(1)}, u32[]{:S(2)}, u32[]{:S(2)}) collective-permute-start(bf16[2,256,1536]{2,1,0:T(8,128)(2,1)S(1)} %get-tuple-element.54), channel_id=1, source_target_pairs={{0,6},{1,7},{32,38},{33,39},{64,70},{65,71},{96,102},{97,103},{2,0... | collective-permute-start | bytes 4718600 | tf_op jit(solution)/shard_map/ppermute | solution.py:38
  13.5 38.8 %collective-permute-start.7 = (bf16[256,3072]{1,0:T(8,128)(2,1)S(1)}, bf16[256,3072]{1,0:T(8,128)(2,1)S(1)}, u32[]{:S(2)}, u32[]{:S(2)}) collective-permute-start(bf16[256,3072]{1,0:T(8,128)(2,1)S(1)} %pad_maximum_fusion.1), channel_id=1, source_target_pairs={{0,8},{1,9},{32,40},{33,41},{64,72},{65,73},{96,104},{97,105},{2,1... | collective-permute-start | bytes 4718600 | tf_op jit(solution)/shard_map/ppermute | solution.py:38
  16.7 51.5 %collective-permute-start.12 = (bf16[256,1536]{1,0:T(8,128)(2,1)S(1)}, bf16[256,1536]{1,0:T(8,128)(2,1)S(1)}, u32[]{:S(2)}, u32[]{:S(2)}) collective-permute-start(bf16[256,1536]{1,0:T(8,128)(2,1)S(1)} %slice.135), channel_id=1, source_target_pairs={{0,8},{1,9},{32,40},{33,41},{64,72},{65,73},{96,104},{97,105},{2,1... | collective-permute-start | bytes 2359304 | tf_op jit(solution)/shard_map/ppermute | solution.py:38
  48.5 20.4 %collective-permute-start.5 = (bf16[2,128,1536]{2,1,0:T(8,128)(2,1)S(1)}, bf16[2,128,1536]{2,1,0:T(8,128)(2,1)S(1)}, u32[]{:S(2)}, u32[]{:S(2)}) collective-permute-start(bf16[2,128,1536]{2,1,0:T(8,128)(2,1)S(1)} %get-tuple-element.95), channel_id=1, source_target_pairs={{0,2},{1,3},{32,34},{33,35},{64,66},{65,67},{96,98},{97,99},{2,4},... | collective-permute-start | bytes 2359304 | tf_op jit(solution)/shard_map/ppermute | solution.py:38
  50.2 18.7 %collective-permute-start.6 = (bf16[2,128,1536]{2,1,0:T(8,128)(2,1)S(1)}, bf16[2,128,1536]{2,1,0:T(8,128)(2,1)S(1)}, u32[]{:S(2)}, u32[]{:S(2)}) collective-permute-start(bf16[2,128,1536]{2,1,0:T(8,128)(2,1)S(1)} %get-tuple-element.94), channel_id=1, source_target_pairs={{0,6},{1,7},{32,38},{33,39},{64,70},{65,71},{96,102},{97,103},{2,0... | collective-permute-start | bytes 2359304 | tf_op jit(solution)/shard_map/ppermute | solution.py:38
  69.6 23.5 %collective-permute-start.9 = (bf16[256,1536]{1,0:T(8,128)(2,1)S(1)}, bf16[256,1536]{1,0:T(8,128)(2,1)S(1)}, u32[]{:S(2)}, u32[]{:S(2)}) collective-permute-start(bf16[256,1536]{1,0:T(8,128)(2,1)S(1)} %fusion.17), channel_id=1, source_target_pairs={{0,8},{1,9},{32,40},{33,41},{64,72},{65,73},{96,104},{97,105},{2,1... | collective-permute-start | bytes 2359304 | tf_op jit(solution)/shard_map/ppermute | solution.py:38
  72.6 16.1 %collective-permute-start.10 = (bf16[1,256,1024]{2,1,0:T(8,128)(2,1)S(1)}, bf16[1,256,1024]{2,1,0:T(8,128)(2,1)S(1)}, u32[]{:S(2)}, u32[]{:S(2)}) collective-permute-start(bf16[1,256,1024]{2,1,0:T(8,128)(2,1)S(1)} %get-tuple-element.59), channel_id=1, source_target_pairs={{0,2},{1,3},{32,34},{33,35},{64,66},{65,67},{96,98},{97,99},{2,4},... | collective-permute-start | bytes 1572872 | tf_op jit(solution)/shard_map/ppermute | solution.py:38
  73.6 15.1 %collective-permute-start.11 = (bf16[1,256,1024]{2,1,0:T(8,128)(2,1)S(1)}, bf16[1,256,1024]{2,1,0:T(8,128)(2,1)S(1)}, u32[]{:S(2)}, u32[]{:S(2)}) collective-permute-start(bf16[1,256,1024]{2,1,0:T(8,128)(2,1)S(1)} %get-tuple-element.67), channel_id=1, source_target_pairs={{0,6},{1,7},{32,38},{33,39},{64,70},{65,71},{96,102},{97,103},{2,0... | collective-permute-start | bytes 1572872 | tf_op jit(solution)/shard_map/ppermute | solution.py:38
  81.7 23.9 %collective-permute-start.16 = (bf16[1,256,1536]{2,1,0:T(8,128)(2,1)}, bf16[1,256,1536]{2,1,0:T(8,128)(2,1)S(1)}, u32[]{:S(2)}, u32[]{:S(2)}) collective-permute-start(bf16[1,256,1536]{2,1,0:T(8,128)(2,1)} %get-tuple-element.72), channel_id=1, source_target_pairs={{0,2},{1,3},{32,34},{33,35},{64,66},{65,67},{96,98},{97,99},{2,4},... | collective-permute-start | bytes 2359304 | tf_op jit(solution)/shard_map/ppermute | solution.py:38
  81.7 23.9 %collective-permute-start.17 = (bf16[1,256,1536]{2,1,0:T(8,128)(2,1)}, bf16[1,256,1536]{2,1,0:T(8,128)(2,1)S(1)}, u32[]{:S(2)}, u32[]{:S(2)}) collective-permute-start(bf16[1,256,1536]{2,1,0:T(8,128)(2,1)} %get-tuple-element.80), channel_id=1, source_target_pairs={{0,6},{1,7},{32,38},{33,39},{64,70},{65,71},{96,102},{97,103},{2,0... | collective-permute-start | bytes 2359304 | tf_op jit(solution)/shard_map/ppermute | solution.py:38
  89.9 21.4 %collective-permute-start.14 = (bf16[1,128,1024]{2,1,0:T(8,128)(2,1)}, bf16[1,128,1024]{2,1,0:T(8,128)(2,1)}, u32[]{:S(2)}, u32[]{:S(2)}) collective-permute-start(bf16[1,128,1024]{2,1,0:T(8,128)(2,1)} %get-tuple-element.101), channel_id=1, source_target_pairs={{0,2},{1,3},{32,34},{33,35},{64,66},{65,67},{96,98},{97,99},{2,4},... | collective-permute-start | bytes 786440 | tf_op jit(solution)/shard_map/ppermute | solution.py:38
  91.2 20.0 %collective-permute-start.15 = (bf16[1,128,1024]{2,1,0:T(8,128)(2,1)}, bf16[1,128,1024]{2,1,0:T(8,128)(2,1)}, u32[]{:S(2)}, u32[]{:S(2)}) collective-permute-start(bf16[1,128,1024]{2,1,0:T(8,128)(2,1)} %get-tuple-element.100), channel_id=1, source_target_pairs={{0,6},{1,7},{32,38},{33,39},{64,70},{65,71},{96,102},{97,103},{2,0... | collective-permute-start | bytes 786440 | tf_op jit(solution)/shard_map/ppermute | solution.py:38
  95.4 24.2 %all-to-all-start = ((bf16[8,32,1536]{2,1,0:T(8,128)(2,1)}), bf16[8,32,1536]{2,1,0:T(8,128)(2,1)}, u32[]{:S(2)}, u32[]{:S(2)}) async-start(bf16[8,32,1536]{2,1,0:T(8,128)(2,1)} %bitcast.96), calls=%async_computation | async-start | bytes 1572864 | tf_op jit(solution)/shard_map/all_to_all | solution.py:192
  107.0 11.1 %collective-permute-start.18 = (bf16[1,128,1536]{2,1,0:T(8,128)(2,1)S(1)}, bf16[1,128,1536]{2,1,0:T(8,128)(2,1)S(1)}, u32[]{:S(2)}, u32[]{:S(2)}) collective-permute-start(bf16[1,128,1536]{2,1,0:T(8,128)(2,1)S(1)} %get-tuple-element.97), channel_id=1, source_target_pairs={{0,2},{1,3},{32,34},{33,35},{64,66},{65,67},{96,98},{97,99},{2,4},... | collective-permute-start | bytes 1179656 | tf_op jit(solution)/shard_map/ppermute | solution.py:38
  108.6 9.5 %collective-permute-start.19 = (bf16[1,128,1536]{2,1,0:T(8,128)(2,1)S(1)}, bf16[1,128,1536]{2,1,0:T(8,128)(2,1)S(1)}, u32[]{:S(2)}, u32[]{:S(2)}) collective-permute-start(bf16[1,128,1536]{2,1,0:T(8,128)(2,1)S(1)} %get-tuple-element.96), channel_id=1, source_target_pairs={{0,6},{1,7},{32,38},{33,39},{64,70},{65,71},{96,102},{97,103},{2,0... | collective-permute-start | bytes 1179656 | tf_op jit(solution)/shard_map/ppermute | solution.py:38
  119.7 22.0 %all-to-all-start.1 = ((bf16[8,32,2560]{2,1,0:T(8,128)(2,1)}), bf16[8,32,2560]{2,1,0:T(8,128)(2,1)S(1)}, u32[]{:S(2)}, u32[]{:S(2)}) async-start(bf16[8,32,2560]{2,1,0:T(8,128)(2,1)} %bitcast.11), calls=%async_computation.1 | async-start | bytes 2621440 | tf_op jit(solution)/shard_map/all_to_all | solution.py:192
  144.0 16.2 %all-to-all-start.2 = ((f32[128,1,128]{2,1,0:T(1,128)}), f32[128,1,128]{2,1,0:T(1,128)S(1)}, u32[]{:S(2)}, u32[]{:S(2)}) async-start(f32[128,1,128]{2,1,0:T(1,128)} %broadcast_in_dim.25), calls=%async_computation.2 | async-start | bytes 131072 | tf_op jit(solution)/shard_map/all_to_all | solution.py:240
  161.0 10.8 %collective-permute-start.24 = (bf16[32,2560]{1,0:T(8,128)(2,1)S(1)}, bf16[32,2560]{1,0:T(8,128)(2,1)S(1)}, u32[]{:S(2)}, u32[]{:S(2)}) collective-permute-start(bf16[32,2560]{1,0:T(8,128)(2,1)S(1)} %multiply_reduce_fusion), channel_id=1, source_target_pairs={{0,32},{1,33},{32,64},{33,65},{64,96},{65,97},{96,0},{97,1},{2,34}... | collective-permute-start | bytes 491528 | tf_op jit(solution)/shard_map/ppermute | solution.py:38
  161.9 9.9 %collective-permute-start.25 = (bf16[32,2560]{1,0:T(8,128)(2,1)S(1)}, bf16[32,2560]{1,0:T(8,128)(2,1)S(1)}, u32[]{:S(2)}, u32[]{:S(2)}) collective-permute-start(bf16[32,2560]{1,0:T(8,128)(2,1)S(1)} %multiply_reduce_fusion), channel_id=1, source_target_pairs={{0,64},{1,65},{32,96},{33,97},{64,0},{65,1},{96,32},{97,33},{2,66}... | collective-permute-start | bytes 491528 | tf_op jit(solution)/shard_map/ppermute | solution.py:38
  163.4 9.0 %collective-permute-start.26 = (bf16[32,2560]{1,0:T(8,128)(2,1)S(1)}, bf16[32,2560]{1,0:T(8,128)(2,1)S(1)}, u32[]{:S(2)}, u32[]{:S(2)}) collective-permute-start(bf16[32,2560]{1,0:T(8,128)(2,1)S(1)} %multiply_reduce_fusion), channel_id=1, source_target_pairs={{0,96},{1,97},{32,0},{33,1},{64,32},{65,33},{96,64},{97,65},{2,98}... | collective-permute-start | bytes 491528 | tf_op jit(solution)/shard_map/ppermute | solution.py:38
  172.4 13.6 %collective-permute-start.27 = (bf16[3,32,2560]{2,1,0:T(8,128)(2,1)S(1)}, bf16[3,32,2560]{2,1,0:T(8,128)(2,1)S(1)}, u32[]{:S(2)}, u32[]{:S(2)}) collective-permute-start(bf16[3,32,2560]{2,1,0:T(8,128)(2,1)S(1)} %get-tuple-element.103), channel_id=1, source_target_pairs={{0,16},{1,17},{32,48},{33,49},{64,80},{65,81},{96,112},{97,113},{2... | collective-permute-start | bytes 1474568 | tf_op jit(solution)/shard_map/ppermute | solution.py:38
  174.5 11.5 %collective-permute-start.22 = (bf16[2,32,1536]{2,1,0:T(8,128)(2,1)S(1)}, bf16[2,32,1536]{2,1,0:T(8,128)(2,1)S(1)}, u32[]{:S(2)}, u32[]{:S(2)}) collective-permute-start(bf16[2,32,1536]{2,1,0:T(8,128)(2,1)S(1)} %get-tuple-element.105), channel_id=1, source_target_pairs={{0,64},{1,65},{32,96},{33,97},{64,0},{65,1},{96,32},{97,33},{2,66}... | collective-permute-start | bytes 589832 | tf_op jit(solution)/shard_map/ppermute | solution.py:38
  177.3 8.7 %collective-permute-start.23 = (bf16[2,32,1536]{2,1,0:T(8,128)(2,1)S(1)}, bf16[2,32,1536]{2,1,0:T(8,128)(2,1)S(1)}, u32[]{:S(2)}, u32[]{:S(2)}) collective-permute-start(bf16[2,32,1536]{2,1,0:T(8,128)(2,1)S(1)} %get-tuple-element.105), channel_id=1, source_target_pairs={{0,96},{1,97},{32,0},{33,1},{64,32},{65,33},{96,64},{97,65},{2,98}... | collective-permute-start | bytes 589832 | tf_op jit(solution)/shard_map/ppermute | solution.py:38
  (18 other events, 293.9 us)

commit v7 on v6

--- a/solution.py
+++ b/solution.py
@@ -14,6 +14,7 @@
 CHUNKS = (1024, 1536)
 PIECES = ((0,), (1,))
 HALF = 128
+FAR_FIRST = (2, 1, 3)
 ORDER = ((0, 0), (0, 1), (1, 0), (3, 1), (2, 0), (1, 1), (2, 1), (3, 0))
 PEERS = ((False, False), (False, True), (True, False), (True, True))
 F32 = jnp.float32
@@ -80,6 +81,35 @@
                 )
                 total = term if total is None else total + term
             out[r] = total.astype(BF16)
+
+
+def message_kernel(n_left, parts, width, *refs):
+    terms = n_left // 2
+    rights, outs = refs[n_left : -len(parts)], refs[-len(parts) :]
+    depth, tile = rights[0].shape[0], 512
+    for start in range(0, width, tile):
+        columns = pl.ds(start, tile)
+        for r in range(2):
+            for i, out in zip(parts, outs):
+                total = None
+                for left, right in zip(refs[r * terms : (r + 1) * terms], rights):
+                    term = jnp.dot(
+                        left[:, pl.ds(i * depth, depth)], right[:, columns], preferred_element_type=F32
+                    )
+                    total = term if total is None else total + term
+                out[r, :, columns] = total.astype(BF16)
+
+
+def message_products(lefts, rights, width, parts):
+    whole = pl.BlockSpec(memory_space=pltpu.VMEM)
+    return pl.pallas_call(
+        functools.partial(message_kernel, len(lefts), parts, width),
+        in_specs=[whole] * (len(lefts) + len(rights)),
+        out_specs=[whole] * len(parts),
+        out_shape=[jax.ShapeDtypeStruct((2, 2 * HALF, width), BF16)] * len(parts),
+        compiler_params=pltpu.CompilerParams(vmem_limit_bytes=32 * 1024 * 1024),
+        cost_estimate=pl.CostEstimate(flops=0, bytes_accessed=0, transcendentals=0),
+    )(*lefts, *rights)
 
 
 def block_products(sets, rights, width, parts=(0, 1, 2, 3)):
@@ -206,7 +236,9 @@
         return block_products([lefts], rights, CHUNKS[k])
 
     chip = [own_set, other_set], [(grads_out, 0), (grads_core, 0)]
-    up, down = block_products(*chip, EARLY, (2, 3))
+    up, down = message_products(
+        [own_left, core_left, x_left, both_left], [grads_out, grads_core], EARLY, (2, 3)
+    )
     grads, _ = after([grads_out, up])
     own, keep = block_products(chip[0], [(grads, 0), (grads_core, 0)], EARLY, (0, 1))
     first = reduce_first((own, keep, up, down))
@@ -247,19 +279,19 @@
     left, right = (mixed(received) for received in slots)
     split = left.shape[1]
     other = shift(jnp.concatenate([left, right], axis=1), pair=1)
-    around = jnp.stack([shift(right, dz=n) for n in (1, 2, 3)])
+    around = jnp.stack([shift(right, dz=n) for n in FAR_FIRST])
     crossed = shift(around, pair=1)
     left = jnp.stack([left, other[:, :split]])
-    left = jnp.stack([left] + [shift(left, dz=n) for n in (1, 2, 3)])
+    left = jnp.stack([left] + [shift(left, dz=n) for n in FAR_FIRST])
     right = jnp.concatenate(
         [jnp.stack([right, other[:, split:]])[None], jnp.stack([around, crossed], axis=1)]
     )
     pieces = jnp.concatenate([left, right], axis=3)
     combined = jnp.zeros((2 * HALF, WIN), BF16)
-    for n in range(4):
+    for slot, n in enumerate((0, *FAR_FIRST)):
         for b in range(2):
             row = (((z - n) % 4) * 2 + (x_lo ^ b)) * 32
-            combined = lax.dynamic_update_slice(combined, pieces[n, b], (row, 0))
+            combined = lax.dynamic_update_slice(combined, pieces[slot, b], (row, 0))
     gram = jnp.dot(jnp.dot(onehot.T, group_gram, precision=hi), onehot, precision=hi)
     return (combined, gram)
 

time: 189 us -> 188 us (level)
    pallas_call x4 -> x3, Pallas kernels: 16.6 us -> 13.1 us  [block_products(): pl.pallas_call(functools.partial(matmul_kernel, n, terms, parts), grid=(w...]
    pallas_call x0 -> x1, Pallas kernels: none -> 3.42 us  [message_products(): pl.pallas_call(functools.partial(message_kernel, len(lefts), parts, width...]
  transfers between devices with their start and end apart: 31 -> 31, of which waited for: 18 -> 19; matrix products, arithmetic and copies ran while one was open for 7% -> 7% of each run, Pallas kernels for 8% -> 8%
where the time goes in v7:
time: 188 us; the launch traced here: 187 us
  waiting for transfers between devices  91.7 us (49%)
  starting transfers between devices  55 us (29%)
  Pallas kernels  19.1 us (10%)
  other arithmetic  9.93 us (5%)
  matrix products  5.96 us (3%)
  local copies, waits for them, and re-layouts  4.47 us (2%)
    ppermute x28, waiting for transfers between devices, shift(): return lax.ppermute(value, AXES, moves)  69.1 us
    ppermute x28, starting transfers between devices, shift(): return lax.ppermute(value, AXES, moves)  37.4 us
    all_to_all x2, waiting for transfers between devices, spread(): return lax.all_to_all(pieces.reshape(8, 32, -1), 'dom', 0, 0, tiled=True)  13.5 us
    pallas_call x3, Pallas kernels, block_products(): pl.pallas_call(functools.partial(matmul_kernel, n, terms, parts), grid=(w...  13.1 us
    all_to_all x2, starting transfers between devices, spread(): return lax.all_to_all(pieces.reshape(8, 32, -1), 'dom', 0, 0, tiled=True)  10.7 us
    all_to_all x1, waiting for transfers between devices, per_device(): parts = lax.all_to_all(sent, AXES, 0, 0, tiled=True)  9.12 us
    all_to_all x1, starting transfers between devices, per_device(): parts = lax.all_to_all(sent, AXES, 0, 0, tiled=True)  6.91 us
    dot_general x2, matrix products, partial_gram(): lax.dot_general(flat, flat, (((1,), (1,)), ((), ())), preferred_element_t...  4.74 us
  transfers between devices with their start and end apart: 31, of which 19 were waited for; matrix products, arithmetic and copies ran while one was open for 7% of the time, Pallas kernels for 8%

profile of v7, /device:TPU:0, one launch (start us, length us, event | category | flops | bytes accessed | tf_op | source)
XLA Modules:
  0.0 187.3 jit_solution(1352081116140173873)
XLA Ops:
  6.5 3.4 %shard_map.69 = (bf16[2,256,1536]{2,1,0:T(8,128)(2,1)S(1)}, bf16[2,256,1536]{2,1,0:T(8,128)(2,1)S(1)}) custom-call(bf16[256,1024]{1,0:T(8,128)(2,1)S(1)} %get-tuple-element.47.refs_0_, bf16[256,1024]{1,0:T(8,128)(2,1)S(1)} %collective-permute-done.refs_1_, bf16[256,1024]{1,0:T(8,128)(2,1)S(1)} %get-tuple-element.49.refs_2_, ...), custom_call_target="tpu_custom_call" | custom-call | tf_op jit(solution)/shard_map/pallas_call | solution.py:105
  13.4 3.2 %collective-permute-start.7 = (bf16[256,3072]{1,0:T(8,128)(2,1)S(1)}, bf16[256,3072]{1,0:T(8,128)(2,1)S(1)}, u32[]{:S(2)}, u32[]{:S(2)}) collective-permute-start(bf16[256,3072]{1,0:T(8,128)(2,1)S(1)} %pad_maximum_fusion.1), channel_id=1, source_target_pairs={{0,8},{1,9},{32,40},{33,41},{64,72},{65,73},{96,104},{97,105},{2,1... | collective-permute-start | bytes 4718600 | tf_op jit(solution)/shard_map/ppermute | solution.py:39
  17.1 3.5 %shard_map.70 = (bf16[2,256,1536]{2,1,0:T(8,128)(2,1)S(1)}, bf16[2,256,1536]{2,1,0:T(8,128)(2,1)S(1)}) custom-call(bf16[256,1024]{1,0:T(8,128)(2,1)S(1)} %get-tuple-element.47.refs_0_, bf16[256,1024]{1,0:T(8,128)(2,1)S(1)} %collective-permute-done.refs_1_, bf16[256,1024]{1,0:T(8,128)(2,1)S(1)} %get-tuple-element.49.refs_2_, ...), custom_call_target="tpu_custom_call" | custom-call | tf_op jit(solution)/shard_map/pallas_call | solution.py:127
  20.7 27.3 %collective-permute-done.3 = bf16[2,256,1536]{2,1,0:T(8,128)(2,1)S(1)} collective-permute-done((bf16[2,256,1536]{2,1,0:T(8,128)(2,1)S(1)}, bf16[2,256,1536]{2,1,0:T(8,128)(2,1)S(1)}, u32[]{:S(2)}, u32[]{:S(2)}) %collective-permute-start.3) | collective-permute-done | bytes 1572896 | tf_op jit(solution)/shard_map/ppermute | solution.py:39
  54.2 3.7 %shard_map.71 = (bf16[1,256,1024]{2,1,0:T(8,128)(2,1)S(1)}, bf16[1,256,1024]{2,1,0:T(8,128)(2,1)S(1)}, bf16[1,256,1024]{2,1,0:T(8,128)(2,1)S(1)}, bf16[1,256,1024]{2,1,0:T(8,128)(2,1)S(1)}) custom-call(bf16[256,1024]{1,0:T(8,128)(2,1)S(1)} %get-tuple-element.47.refs_0_, bf16[256,1024]{1,0:T(8,128)(2,1)S(1)} %collective-permute-done.refs_1_, ...), custom_call_target="tpu_custom_call" | custom-call | tf_op jit(solution)/shard_map/pallas_call | solution.py:127
  58.0 10.1 %collective-permute-done.12.refs_6_ = bf16[256,1536]{1,0:T(8,128)(2,1)S(1)} collective-permute-done((bf16[256,1536]{1,0:T(8,128)(2,1)S(1)}, bf16[256,1536]{1,0:T(8,128)(2,1)S(1)}, u32[]{:S(2)}, u32[]{:S(2)}) %collective-permute-start.12) | collective-permute-done | bytes 786464 | tf_op jit(solution)/shard_map/ppermute | solution.py:39
  69.5 3.0 %collective-permute-start.9 = (bf16[256,1536]{1,0:T(8,128)(2,1)S(1)}, bf16[256,1536]{1,0:T(8,128)(2,1)S(1)}, u32[]{:S(2)}, u32[]{:S(2)}) collective-permute-start(bf16[256,1536]{1,0:T(8,128)(2,1)S(1)} %fusion.17), channel_id=1, source_target_pairs={{0,8},{1,9},{32,40},{33,41},{64,72},{65,73},{96,104},{97,105},{2,1... | collective-permute-start | bytes 2359304 | tf_op jit(solution)/shard_map/ppermute | solution.py:39
  73.5 2.2 %collective-permute-start.11 = (bf16[1,256,1024]{2,1,0:T(8,128)(2,1)S(1)}, bf16[1,256,1024]{2,1,0:T(8,128)(2,1)S(1)}, u32[]{:S(2)}, u32[]{:S(2)}) collective-permute-start(bf16[1,256,1024]{2,1,0:T(8,128)(2,1)S(1)} %get-tuple-element.67), channel_id=1, source_target_pairs={{0,6},{1,7},{32,38},{33,39},{64,70},{65,71},{96,102},{97,103},{2,0... | collective-permute-start | bytes 1572872 | tf_op jit(solution)/shard_map/ppermute | solution.py:39
  75.7 5.8 %shard_map.72 = (bf16[1,256,1536]{2,1,0:T(8,128)(2,1)S(1)}, bf16[1,256,1536]{2,1,0:T(8,128)(2,1)S(1)}, bf16[1,256,1536]{2,1,0:T(8,128)(2,1)}, bf16[1,256,1536]{2,1,0:T(8,128)(2,1)}) custom-call(bf16[256,1024]{1,0:T(8,128)(2,1)S(1)} %get-tuple-element.47.refs_0_, bf16[256,1024]{1,0:T(8,128)(2,1)S(1)} %collective-permute-done.refs_1_, ...), custom_call_target="tpu_custom_call" | custom-call | tf_op jit(solution)/shard_map/pallas_call | solution.py:127
  81.6 3.2 %collective-permute-start.17 = (bf16[1,256,1536]{2,1,0:T(8,128)(2,1)}, bf16[1,256,1536]{2,1,0:T(8,128)(2,1)S(1)}, u32[]{:S(2)}, u32[]{:S(2)}) collective-permute-start(bf16[1,256,1536]{2,1,0:T(8,128)(2,1)} %get-tuple-element.80), channel_id=1, source_target_pairs={{0,6},{1,7},{32,38},{33,39},{64,70},{65,71},{96,102},{97,103},{2,0... | collective-permute-start | bytes 2359304 | tf_op jit(solution)/shard_map/ppermute | solution.py:39
  84.8 3.8 %collective-permute-done.10 = bf16[1,256,1024]{2,1,0:T(8,128)(2,1)S(1)} collective-permute-done((bf16[1,256,1024]{2,1,0:T(8,128)(2,1)S(1)}, bf16[1,256,1024]{2,1,0:T(8,128)(2,1)S(1)}, u32[]{:S(2)}, u32[]{:S(2)}) %collective-permute-start.10) | collective-permute-done | bytes 524320 | tf_op jit(solution)/shard_map/ppermute | solution.py:39
  93.0 2.3 %fusion.4 = bf16[256,1536]{1,0:T(8,128)(2,1)} fusion(f32[2,128,1536]{2,1,0:T(8,128)S(1)} %get-tuple-element.93, f32[2,128,1536]{2,1,0:T(8,128)S(1)} %get-tuple-element.92, bf16[256,1536]{1,0:T(8,128)(2,1)S(1)} %collective-permute-done.9, bf16[256,4096]{1,0:T(8,128)(2,1)} %bitcast.93), kind=kLoop, calls=%fused_computation.8 | loop fusion | flops 2359296 | bytes 5505024 | tf_op jit(solution)/shard_map/convert_element_type | solution.py:218
  95.3 5.4 %all-to-all-start = ((bf16[8,32,1536]{2,1,0:T(8,128)(2,1)}), bf16[8,32,1536]{2,1,0:T(8,128)(2,1)}, u32[]{:S(2)}, u32[]{:S(2)}) async-start(bf16[8,32,1536]{2,1,0:T(8,128)(2,1)} %bitcast.96), calls=%async_computation | async-start | bytes 1572864 | tf_op jit(solution)/shard_map/all_to_all | solution.py:222
  100.7 4.7 %collective-permute-done.16.from_back = bf16[1,256,1536]{2,1,0:T(8,128)(2,1)S(1)} collective-permute-done((bf16[1,256,1536]{2,1,0:T(8,128)(2,1)}, bf16[1,256,1536]{2,1,0:T(8,128)(2,1)S(1)}, u32[]{:S(2)}, u32[]{:S(2)}) %collective-permute-start.16) | collective-permute-done | bytes 786464 | tf_op jit(solution)/shard_map/ppermute | solution.py:39
  112.6 5.5 %collective-permute-done.18.back2 = bf16[1,128,1536]{2,1,0:T(8,128)(2,1)S(1)} collective-permute-done((bf16[1,128,1536]{2,1,0:T(8,128)(2,1)S(1)}, bf16[1,128,1536]{2,1,0:T(8,128)(2,1)S(1)}, u32[]{:S(2)}, u32[]{:S(2)}) %collective-permute-start.18) | collective-permute-done | bytes 393248 | tf_op jit(solution)/shard_map/ppermute | solution.py:39
  119.5 5.3 %all-to-all-start.1 = ((bf16[8,32,2560]{2,1,0:T(8,128)(2,1)}), bf16[8,32,2560]{2,1,0:T(8,128)(2,1)S(1)}, u32[]{:S(2)}, u32[]{:S(2)}) async-start(bf16[8,32,2560]{2,1,0:T(8,128)(2,1)} %bitcast.11), calls=%async_computation.1 | async-start | bytes 2621440 | tf_op jit(solution)/shard_map/all_to_all | solution.py:222
  124.9 3.1 %convolution_bitcast_fusion = f32[8,8]{1,0:T(8,128)S(1)} fusion(bf16[8,32,1536]{2,1,0:T(8,128)(2,1)} %all-to-all-done), kind=kOutput, calls=%fused_computation.19 | convolution fusion | flops 6291456 | bytes 786688 | tf_op jit(solution)/shard_map/dot_general | solution.py:249
  128.0 13.5 %all-to-all-done.1 = bf16[8,32,2560]{2,1,0:T(8,128)(2,1)S(1)} async-done(((bf16[8,32,2560]{2,1,0:T(8,128)(2,1)}), bf16[8,32,2560]{2,1,0:T(8,128)(2,1)S(1)}, u32[]{:S(2)}, u32[]{:S(2)}) %all-to-all-start.1) | async-done | bytes 1310752 | tf_op jit(solution)/shard_map/all_to_all | solution.py:222
  143.9 6.9 %all-to-all-start.2 = ((f32[128,1,128]{2,1,0:T(1,128)}), f32[128,1,128]{2,1,0:T(1,128)S(1)}, u32[]{:S(2)}, u32[]{:S(2)}) async-start(f32[128,1,128]{2,1,0:T(1,128)} %broadcast_in_dim.25), calls=%async_computation.2 | async-start | bytes 131072 | tf_op jit(solution)/shard_map/all_to_all | solution.py:272
  150.9 9.1 %all-to-all-done.2 = f32[128,1,128]{2,1,0:T(1,128)S(1)} async-done(((f32[128,1,128]{2,1,0:T(1,128)}), f32[128,1,128]{2,1,0:T(1,128)S(1)}, u32[]{:S(2)}, u32[]{:S(2)}) %all-to-all-start.2) | async-done | bytes 65568 | tf_op jit(solution)/shard_map/all_to_all | solution.py:272
  162.7 2.5 %collective-permute-start.26 = (bf16[32,2560]{1,0:T(8,128)(2,1)S(1)}, bf16[32,2560]{1,0:T(8,128)(2,1)S(1)}, u32[]{:S(2)}, u32[]{:S(2)}) collective-permute-start(bf16[32,2560]{1,0:T(8,128)(2,1)S(1)} %multiply_reduce_fusion), channel_id=1, source_target_pairs={{0,96},{1,97},{32,0},{33,1},{64,32},{65,33},{96,64},{97,65},{2,98}... | collective-permute-start | bytes 491528 | tf_op jit(solution)/shard_map/ppermute | solution.py:39
  169.5 2.4 %collective-permute-done.25 = bf16[32,2560]{1,0:T(8,128)(2,1)S(1)} collective-permute-done((bf16[32,2560]{1,0:T(8,128)(2,1)S(1)}, bf16[32,2560]{1,0:T(8,128)(2,1)S(1)}, u32[]{:S(2)}, u32[]{:S(2)}) %collective-permute-start.25) | collective-permute-done | bytes 163872 | tf_op jit(solution)/shard_map/ppermute | solution.py:39
  178.9 4.1 %collective-permute-done.21 = bf16[2,32,1536]{2,1,0:T(8,128)(2,1)S(1)} collective-permute-done((bf16[2,32,1536]{2,1,0:T(8,128)(2,1)S(1)}, bf16[2,32,1536]{2,1,0:T(8,128)(2,1)S(1)}, u32[]{:S(2)}, u32[]{:S(2)}) %collective-permute-start.21) | collective-permute-done | bytes 196640 | tf_op jit(solution)/shard_map/ppermute | solution.py:39
  183.0 2.0 %collective-permute-done.22 = bf16[2,32,1536]{2,1,0:T(8,128)(2,1)S(1)} collective-permute-done((bf16[2,32,1536]{2,1,0:T(8,128)(2,1)S(1)}, bf16[2,32,1536]{2,1,0:T(8,128)(2,1)S(1)}, u32[]{:S(2)}, u32[]{:S(2)}) %collective-permute-start.22) | collective-permute-done | bytes 196640 | tf_op jit(solution)/shard_map/ppermute | solution.py:39
  (109 shorter events, 49.9 us)
Async XLA Ops:
  9.9 38.1 %collective-permute-start.3 = (bf16[2,256,1536]{2,1,0:T(8,128)(2,1)S(1)}, bf16[2,256,1536]{2,1,0:T(8,128)(2,1)S(1)}, u32[]{:S(2)}, u32[]{:S(2)}) collective-permute-start(bf16[2,256,1536]{2,1,0:T(8,128)(2,1)S(1)} %get-tuple-element.51), channel_id=1, source_target_pairs={{0,2},{1,3},{32,34},{33,35},{64,66},{65,67},{96,98},{97,99},{2,4},... | collective-permute-start | bytes 4718600 | tf_op jit(solution)/shard_map/ppermute | solution.py:39
  11.6 36.4 %collective-permute-start.4 = (bf16[2,256,1536]{2,1,0:T(8,128)(2,1)S(1)}, bf16[2,256,1536]{2,1,0:T(8,128)(2,1)S(1)}, u32[]{:S(2)}, u32[]{:S(2)}) collective-permute-start(bf16[2,256,1536]{2,1,0:T(8,128)(2,1)S(1)} %get-tuple-element.54), channel_id=1, source_target_pairs={{0,6},{1,7},{32,38},{33,39},{64,70},{65,71},{96,102},{97,103},{2,0... | collective-permute-start | bytes 4718600 | tf_op jit(solution)/shard_map/ppermute | solution.py:39
  13.4 38.8 %collective-permute-start.7 = (bf16[256,3072]{1,0:T(8,128)(2,1)S(1)}, bf16[256,3072]{1,0:T(8,128)(2,1)S(1)}, u32[]{:S(2)}, u32[]{:S(2)}) collective-permute-start(bf16[256,3072]{1,0:T(8,128)(2,1)S(1)} %pad_maximum_fusion.1), channel_id=1, source_target_pairs={{0,8},{1,9},{32,40},{33,41},{64,72},{65,73},{96,104},{97,105},{2,1... | collective-permute-start | bytes 4718600 | tf_op jit(solution)/shard_map/ppermute | solution.py:39
  16.6 51.5 %collective-permute-start.12 = (bf16[256,1536]{1,0:T(8,128)(2,1)S(1)}, bf16[256,1536]{1,0:T(8,128)(2,1)S(1)}, u32[]{:S(2)}, u32[]{:S(2)}) collective-permute-start(bf16[256,1536]{1,0:T(8,128)(2,1)S(1)} %slice.135), channel_id=1, source_target_pairs={{0,8},{1,9},{32,40},{33,41},{64,72},{65,73},{96,104},{97,105},{2,1... | collective-permute-start | bytes 2359304 | tf_op jit(solution)/shard_map/ppermute | solution.py:39
  48.4 20.4 %collective-permute-start.5 = (bf16[2,128,1536]{2,1,0:T(8,128)(2,1)S(1)}, bf16[2,128,1536]{2,1,0:T(8,128)(2,1)S(1)}, u32[]{:S(2)}, u32[]{:S(2)}) collective-permute-start(bf16[2,128,1536]{2,1,0:T(8,128)(2,1)S(1)} %get-tuple-element.95), channel_id=1, source_target_pairs={{0,2},{1,3},{32,34},{33,35},{64,66},{65,67},{96,98},{97,99},{2,4},... | collective-permute-start | bytes 2359304 | tf_op jit(solution)/shard_map/ppermute | solution.py:39
  50.1 18.8 %collective-permute-start.6 = (bf16[2,128,1536]{2,1,0:T(8,128)(2,1)S(1)}, bf16[2,128,1536]{2,1,0:T(8,128)(2,1)S(1)}, u32[]{:S(2)}, u32[]{:S(2)}) collective-permute-start(bf16[2,128,1536]{2,1,0:T(8,128)(2,1)S(1)} %get-tuple-element.94), channel_id=1, source_target_pairs={{0,6},{1,7},{32,38},{33,39},{64,70},{65,71},{96,102},{97,103},{2,0... | collective-permute-start | bytes 2359304 | tf_op jit(solution)/shard_map/ppermute | solution.py:39
  69.5 23.5 %collective-permute-start.9 = (bf16[256,1536]{1,0:T(8,128)(2,1)S(1)}, bf16[256,1536]{1,0:T(8,128)(2,1)S(1)}, u32[]{:S(2)}, u32[]{:S(2)}) collective-permute-start(bf16[256,1536]{1,0:T(8,128)(2,1)S(1)} %fusion.17), channel_id=1, source_target_pairs={{0,8},{1,9},{32,40},{33,41},{64,72},{65,73},{96,104},{97,105},{2,1... | collective-permute-start | bytes 2359304 | tf_op jit(solution)/shard_map/ppermute | solution.py:39
  72.5 16.1 %collective-permute-start.10 = (bf16[1,256,1024]{2,1,0:T(8,128)(2,1)S(1)}, bf16[1,256,1024]{2,1,0:T(8,128)(2,1)S(1)}, u32[]{:S(2)}, u32[]{:S(2)}) collective-permute-start(bf16[1,256,1024]{2,1,0:T(8,128)(2,1)S(1)} %get-tuple-element.59), channel_id=1, source_target_pairs={{0,2},{1,3},{32,34},{33,35},{64,66},{65,67},{96,98},{97,99},{2,4},... | collective-permute-start | bytes 1572872 | tf_op jit(solution)/shard_map/ppermute | solution.py:39
  73.5 15.1 %collective-permute-start.11 = (bf16[1,256,1024]{2,1,0:T(8,128)(2,1)S(1)}, bf16[1,256,1024]{2,1,0:T(8,128)(2,1)S(1)}, u32[]{:S(2)}, u32[]{:S(2)}) collective-permute-start(bf16[1,256,1024]{2,1,0:T(8,128)(2,1)S(1)} %get-tuple-element.67), channel_id=1, source_target_pairs={{0,6},{1,7},{32,38},{33,39},{64,70},{65,71},{96,102},{97,103},{2,0... | collective-permute-start | bytes 1572872 | tf_op jit(solution)/shard_map/ppermute | solution.py:39
  81.6 23.9 %collective-permute-start.16 = (bf16[1,256,1536]{2,1,0:T(8,128)(2,1)}, bf16[1,256,1536]{2,1,0:T(8,128)(2,1)S(1)}, u32[]{:S(2)}, u32[]{:S(2)}) collective-permute-start(bf16[1,256,1536]{2,1,0:T(8,128)(2,1)} %get-tuple-element.72), channel_id=1, source_target_pairs={{0,2},{1,3},{32,34},{33,35},{64,66},{65,67},{96,98},{97,99},{2,4},... | collective-permute-start | bytes 2359304 | tf_op jit(solution)/shard_map/ppermute | solution.py:39
  81.6 23.9 %collective-permute-start.17 = (bf16[1,256,1536]{2,1,0:T(8,128)(2,1)}, bf16[1,256,1536]{2,1,0:T(8,128)(2,1)S(1)}, u32[]{:S(2)}, u32[]{:S(2)}) collective-permute-start(bf16[1,256,1536]{2,1,0:T(8,128)(2,1)} %get-tuple-element.80), channel_id=1, source_target_pairs={{0,6},{1,7},{32,38},{33,39},{64,70},{65,71},{96,102},{97,103},{2,0... | collective-permute-start | bytes 2359304 | tf_op jit(solution)/shard_map/ppermute | solution.py:39
  89.7 21.4 %collective-permute-start.14 = (bf16[1,128,1024]{2,1,0:T(8,128)(2,1)}, bf16[1,128,1024]{2,1,0:T(8,128)(2,1)}, u32[]{:S(2)}, u32[]{:S(2)}) collective-permute-start(bf16[1,128,1024]{2,1,0:T(8,128)(2,1)} %get-tuple-element.101), channel_id=1, source_target_pairs={{0,2},{1,3},{32,34},{33,35},{64,66},{65,67},{96,98},{97,99},{2,4},... | collective-permute-start | bytes 786440 | tf_op jit(solution)/shard_map/ppermute | solution.py:39
  91.1 20.0 %collective-permute-start.15 = (bf16[1,128,1024]{2,1,0:T(8,128)(2,1)}, bf16[1,128,1024]{2,1,0:T(8,128)(2,1)}, u32[]{:S(2)}, u32[]{:S(2)}) collective-permute-start(bf16[1,128,1024]{2,1,0:T(8,128)(2,1)} %get-tuple-element.100), channel_id=1, source_target_pairs={{0,6},{1,7},{32,38},{33,39},{64,70},{65,71},{96,102},{97,103},{2,0... | collective-permute-start | bytes 786440 | tf_op jit(solution)/shard_map/ppermute | solution.py:39
  95.3 24.2 %all-to-all-start = ((bf16[8,32,1536]{2,1,0:T(8,128)(2,1)}), bf16[8,32,1536]{2,1,0:T(8,128)(2,1)}, u32[]{:S(2)}, u32[]{:S(2)}) async-start(bf16[8,32,1536]{2,1,0:T(8,128)(2,1)} %bitcast.96), calls=%async_computation | async-start | bytes 1572864 | tf_op jit(solution)/shard_map/all_to_all | solution.py:222
  106.9 11.1 %collective-permute-start.18 = (bf16[1,128,1536]{2,1,0:T(8,128)(2,1)S(1)}, bf16[1,128,1536]{2,1,0:T(8,128)(2,1)S(1)}, u32[]{:S(2)}, u32[]{:S(2)}) collective-permute-start(bf16[1,128,1536]{2,1,0:T(8,128)(2,1)S(1)} %get-tuple-element.97), channel_id=1, source_target_pairs={{0,2},{1,3},{32,34},{33,35},{64,66},{65,67},{96,98},{97,99},{2,4},... | collective-permute-start | bytes 1179656 | tf_op jit(solution)/shard_map/ppermute | solution.py:39
  108.5 9.5 %collective-permute-start.19 = (bf16[1,128,1536]{2,1,0:T(8,128)(2,1)S(1)}, bf16[1,128,1536]{2,1,0:T(8,128)(2,1)S(1)}, u32[]{:S(2)}, u32[]{:S(2)}) collective-permute-start(bf16[1,128,1536]{2,1,0:T(8,128)(2,1)S(1)} %get-tuple-element.96), channel_id=1, source_target_pairs={{0,6},{1,7},{32,38},{33,39},{64,70},{65,71},{96,102},{97,103},{2,0... | collective-permute-start | bytes 1179656 | tf_op jit(solution)/shard_map/ppermute | solution.py:39
  119.5 22.0 %all-to-all-start.1 = ((bf16[8,32,2560]{2,1,0:T(8,128)(2,1)}), bf16[8,32,2560]{2,1,0:T(8,128)(2,1)S(1)}, u32[]{:S(2)}, u32[]{:S(2)}) async-start(bf16[8,32,2560]{2,1,0:T(8,128)(2,1)} %bitcast.11), calls=%async_computation.1 | async-start | bytes 2621440 | tf_op jit(solution)/shard_map/all_to_all | solution.py:222
  143.9 16.2 %all-to-all-start.2 = ((f32[128,1,128]{2,1,0:T(1,128)}), f32[128,1,128]{2,1,0:T(1,128)S(1)}, u32[]{:S(2)}, u32[]{:S(2)}) async-start(f32[128,1,128]{2,1,0:T(1,128)} %broadcast_in_dim.25), calls=%async_computation.2 | async-start | bytes 131072 | tf_op jit(solution)/shard_map/all_to_all | solution.py:272
  160.8 8.7 %collective-permute-start.24 = (bf16[32,2560]{1,0:T(8,128)(2,1)S(1)}, bf16[32,2560]{1,0:T(8,128)(2,1)S(1)}, u32[]{:S(2)}, u32[]{:S(2)}) collective-permute-start(bf16[32,2560]{1,0:T(8,128)(2,1)S(1)} %multiply_reduce_fusion), channel_id=1, source_target_pairs={{0,64},{1,65},{32,96},{33,97},{64,0},{65,1},{96,32},{97,33},{2,66}... | collective-permute-start | bytes 491528 | tf_op jit(solution)/shard_map/ppermute | solution.py:39
  162.0 10.0 %collective-permute-start.25 = (bf16[32,2560]{1,0:T(8,128)(2,1)S(1)}, bf16[32,2560]{1,0:T(8,128)(2,1)S(1)}, u32[]{:S(2)}, u32[]{:S(2)}) collective-permute-start(bf16[32,2560]{1,0:T(8,128)(2,1)S(1)} %multiply_reduce_fusion), channel_id=1, source_target_pairs={{0,32},{1,33},{32,64},{33,65},{64,96},{65,97},{96,0},{97,1},{2,34}... | collective-permute-start | bytes 491528 | tf_op jit(solution)/shard_map/ppermute | solution.py:39
  162.7 9.3 %collective-permute-start.26 = (bf16[32,2560]{1,0:T(8,128)(2,1)S(1)}, bf16[32,2560]{1,0:T(8,128)(2,1)S(1)}, u32[]{:S(2)}, u32[]{:S(2)}) collective-permute-start(bf16[32,2560]{1,0:T(8,128)(2,1)S(1)} %multiply_reduce_fusion), channel_id=1, source_target_pairs={{0,96},{1,97},{32,0},{33,1},{64,32},{65,33},{96,64},{97,65},{2,98}... | collective-permute-start | bytes 491528 | tf_op jit(solution)/shard_map/ppermute | solution.py:39
  172.0 13.2 %collective-permute-start.27 = (bf16[3,32,2560]{2,1,0:T(8,128)(2,1)S(1)}, bf16[3,32,2560]{2,1,0:T(8,128)(2,1)S(1)}, u32[]{:S(2)}, u32[]{:S(2)}) collective-permute-start(bf16[3,32,2560]{2,1,0:T(8,128)(2,1)S(1)} %get-tuple-element.103), channel_id=1, source_target_pairs={{0,16},{1,17},{32,48},{33,49},{64,80},{65,81},{96,112},{97,113},{2... | collective-permute-start | bytes 1474568 | tf_op jit(solution)/shard_map/ppermute | solution.py:39
  174.2 8.8 %collective-permute-start.21 = (bf16[2,32,1536]{2,1,0:T(8,128)(2,1)S(1)}, bf16[2,32,1536]{2,1,0:T(8,128)(2,1)S(1)}, u32[]{:S(2)}, u32[]{:S(2)}) collective-permute-start(bf16[2,32,1536]{2,1,0:T(8,128)(2,1)S(1)} %get-tuple-element.105), channel_id=1, source_target_pairs={{0,64},{1,65},{32,96},{33,97},{64,0},{65,1},{96,32},{97,33},{2,66}... | collective-permute-start | bytes 589832 | tf_op jit(solution)/shard_map/ppermute | solution.py:39
  175.6 9.5 %collective-permute-start.22 = (bf16[2,32,1536]{2,1,0:T(8,128)(2,1)S(1)}, bf16[2,32,1536]{2,1,0:T(8,128)(2,1)S(1)}, u32[]{:S(2)}, u32[]{:S(2)}) collective-permute-start(bf16[2,32,1536]{2,1,0:T(8,128)(2,1)S(1)} %get-tuple-element.105), channel_id=1, source_target_pairs={{0,32},{1,33},{32,64},{33,65},{64,96},{65,97},{96,0},{97,1},{2,34}... | collective-permute-start | bytes 589832 | tf_op jit(solution)/shard_map/ppermute | solution.py:39
  (18 other events, 294.4 us)
